TPU v7x, 128 devices: a whole 4x4x4 slice. The times are simulated.
128 devices in a mesh: az: 16 (over x_lo, z, core), rad: 8 (over y, x_hi).
Axes of the slice: x: 4 (x_hi: 2, x_lo: 2; x = x_hi * 2 + x_lo), y: 4, z: 4, core: 2. Of those that a mesh axis runs over, the one named last changes fastest.
Arguments:
- hidden_site_vector: bfloat16 [1, 256, 128, 512], P(None, 'az', 'rad')
- mesh_portion_descriptors: bfloat16 [262144, 128], P(('az', 'rad')), may hold values from -6 to 6
- mesh_entry_site: int32 [262144], P(('az', 'rad')), may hold values from 0 to 255
- mesh_portion_tally: int32 [128, 128], P(('az', 'rad')), may hold values from 0 to 16, as said below
- incline_grid_position: int32 [1], replicated, may hold values from 0 to 63
- incline_vector_lookup: bfloat16 [64, 512], replicated, may hold values from -6 to 6
- mesh_mapping_matrix: bfloat16 [128, 512], replicated, may hold values from -0.5 to 0.5
- prefocus_rescale_factor: float32 [2, 512], replicated, may hold values from 0.1 to 1.9
- probe_lock_payload_matrix: bfloat16 [2, 512, 1536], replicated, may hold values from -0.25 to 0.25
- sharpness_scale: float32 [2, 8], replicated, may hold values from 2 to 12
- final_mapping_matrix: bfloat16 [2, 512, 512], replicated, may hold values from -0.5 to 0.5
- terminal_rescale_factor: float32 [512], replicated, may hold values from 0.1 to 1.9
Outputs:
- latent: bfloat16 [1, 256, 128, 512], P(None, 'az', 'rad')
Inputs may be any that keep to these rules, and one draw needn't show every extreme that they name: `mesh_portion_tally`: devices of radial index 0 (t % 8 == 0) get exactly 16 live rows from every source device; other blocks hold any number of live rows. `mesh_entry_site`: A cell local to the target device, numbered (plane * 16 + azimuth) * 16 + radius.
All inputs are finite; a program needn't handle non-finite values.
Results may differ from a plain program's by a relative error of at most 0.017.
Values may be sent and summed in bfloat16 or wider, within the bound.
No kernel may reach another device: no remote copies, remote signals or barrier semaphores. Data moves between devices by JAX's collectives and lax.ppermute only.
A program may use at most 64 MiB of HBM per device.

v0:
```python
import jax
import jax.numpy as jnp
import numpy as np
from jax import lax
from jax.experimental import pallas as pl
from jax.experimental.pallas import tpu as pltpu
from jax.sharding import PartitionSpec as P

HALO = 4
HEADS = 8
WIDTH = 512
EDGE = 2 * HALO
DEAD = 256
NEG = -1024.0
LOG2E = 1.4426950408889634
COLUMN_J = np.array(
    list(range(8, 24)) + list(range(24, 28)) + list(range(4, 8)) + list(range(0, 4)) + list(range(28, 32))
)
SMEM = pl.BlockSpec(memory_space=pltpu.SMEM)
VMEM = pl.BlockSpec(memory_space=pltpu.VMEM)
HBM = pl.BlockSpec(memory_space=pltpu.HBM)


def window_tables():
    i = np.arange(32)
    key = np.zeros((32, 32, 128), np.float32)
    query = np.zeros((24, 24, 128), np.float32)
    for d in range(24):
        key[:, :, d] = np.where(np.abs(COLUMN_J - COLUMN_J[d]) > HALO, NEG, 0.0)[None, :]
        key[:, :, 24 + d] = np.where(np.abs(i - (d + HALO)) > HALO, NEG, 0.0)[:, None]
        query[:, d, d] = 1.0
        query[d, :, 24 + d] = 1.0
    key[:, :, 48] = np.where(COLUMN_J < 8, NEG, 0.0)[None, :]
    key[:, :, 49] = np.where(COLUMN_J >= 24, NEG, 0.0)[None, :]
    tables = (
        query.reshape(576, 128),
        key.reshape(1024, 128),
        query[4:20, :16].reshape(256, 128),
        key[4:28, :24].reshape(576, 128),
    )
    return [jnp.asarray(t, jnp.bfloat16) for t in tables]


def dot(a, b):
    return jnp.dot(a, b, preferred_element_type=jnp.float32)


def rounded(x):
    return x.astype(jnp.bfloat16).astype(jnp.float32)


def norm_rows(x, gain):
    return x * lax.rsqrt(jnp.mean(x * x, -1, keepdims=True) + 1e-05) * gain


def shape_of(x):
    return x if isinstance(x, jax.ShapeDtypeStruct) else jax.ShapeDtypeStruct(x, jnp.bfloat16)


COST = {"pack": 1.5, "stage": 3, "cell_sums": 2, "band": 1.5, "inner": 4, "outer": 8}


def call(kernel, name, outs, in_specs, out_specs=None, scratch=(), mib=8):
    return pl.pallas_call(
        kernel,
        out_shape=[shape_of(x) for x in outs],
        in_specs=in_specs,
        out_specs=out_specs or [VMEM] * len(outs),
        scratch_shapes=scratch,
        compiler_params=pltpu.CompilerParams(vmem_limit_bytes=mib << 20),
        name=name,
        cost_estimate=pl.CostEstimate(
            flops=int(COST[name] * 1e9), bytes_accessed=int(COST[name] * 3e6), transcendentals=0
        ),
    )


def interleave(tasks, depth):
    waiting = list(tasks)
    active = []
    while waiting or active:
        if waiting and len(active) < depth:
            active.append(waiting.pop(0))
        for task in list(active):
            if next(task, True):
                active.remove(task)


def one_by_one(*tasks):
    for task in tasks:
        yield from task


def pack_kernel(rows, cells, tally, packed, token, block, cells_here, tally_here, sems, out_sems):
    parts = [pl.ds(32 * i, 32) for i in range(4)]
    loads = [pltpu.make_async_copy(rows.at[at], block.at[at, 0:16, :], sems.at[i]) for i, at in enumerate(parts)]
    ids_load = pltpu.make_async_copy(cells, cells_here, sems.at[4])
    tally_load = pltpu.make_async_copy(tally, tally_here, sems.at[5])
    ids_load.start()
    tally_load.start()
    for load in loads:
        load.start()
    k = lax.broadcasted_iota(jnp.int32, (16, 128), 0)
    t = lax.broadcasted_iota(jnp.int32, (16, 128), 1)
    a = lax.broadcasted_iota(jnp.int32, (128, 128), 0)
    b = lax.broadcasted_iota(jnp.int32, (128, 128), 1)
    pick = jnp.where(lax.rem(a, 8) == b // 16, 1.0, 0.0).astype(jnp.bfloat16)
    r = lax.axis_index("rad")
    mine = t // 16 == r
    ids_load.wait()
    tally_load.wait()
    spread = jnp.where(t // 8 == k, tally_here[...].astype(jnp.float32), 0.0).astype(jnp.bfloat16)
    live = lax.rem(t, 16).astype(jnp.float32) < dot(spread, pick)
    ids = jnp.where(live, cells_here[...].astype(jnp.float32), float(DEAD))
    turned = [jnp.where(mine, pltpu.roll(ids, lax.rem(r - b + 8, 8) * 16, 1), 0.0) for b in range(8)]
    stores = []
    for i, at in enumerate(parts):
        for k in range(4 * i, 4 * i + 4):
            for b in range(8):
                row = jnp.broadcast_to(turned[b][k : k + 1], (8, 128))
                block[8 * k + b, 16:24, :] = row.astype(jnp.bfloat16)
        loads[i].wait()
        stores.append(pltpu.make_async_copy(block.at[at], packed.at[at], out_sems.at[i]))
        stores[-1].start()
    token[...] = jnp.zeros((8, 128), jnp.float32)
    for store in stores:
        store.wait()


def pack(rows, cells, tally):
    return call(
        pack_kernel,
        "pack",
        [(128, 24, 128), jax.ShapeDtypeStruct((8, 128), jnp.float32)],
        [HBM] * 3,
        [HBM, VMEM],
        [
            pltpu.VMEM((128, 24, 128), jnp.bfloat16),
            pltpu.VMEM((16, 128), jnp.int32),
            pltpu.VMEM((1, 128), jnp.int32),
            pltpu.SemaphoreType.DMA((6,)),
            pltpu.SemaphoreType.DMA((4,)),
        ],
        mib=60,
    )(rows, cells, tally)


def stage_kernel(token, pitch_at, sharp, lookup, hidden, *refs):
    count = (len(refs) - 5) // 2
    sources, copies = refs[:count], refs[count : 2 * count]
    pitch, scale, send_a, send_b, sems = refs[2 * count :]
    moves = [pltpu.make_async_copy(a, b, sems.at[i]) for i, (a, b) in enumerate(zip(sources, copies))]
    for move in moves:
        move.start()
    rows = lax.broadcasted_iota(jnp.int32, (64, 1), 0)
    pitch[...] = jnp.sum(
        jnp.where(rows == pitch_at[0], lookup[...].astype(jnp.float32), 0.0), axis=0, keepdims=True
    )
    head = lax.broadcasted_iota(jnp.int32, (1, WIDTH), 1) // 64
    for layer in range(2):
        line = token[0:1, 0:1] * jnp.ones((1, WIDTH), jnp.float32)
        for h in range(HEADS):
            line = jnp.where(head == h, sharp[layer, h] * LOG2E, line)
        scale[layer : layer + 1] = line
    even = lax.rem(lax.axis_index("rad"), 2) == 0
    low = hidden[:, :EDGE].astype(jnp.float32)
    high = hidden[:, EDGE:].astype(jnp.float32)
    send_a[...] = jnp.where(even, high, low).astype(jnp.bfloat16)
    send_b[...] = jnp.where(even, low, high).astype(jnp.bfloat16)
    for move in moves:
        move.wait()


def stage(token, pitch_at, sharp, lookup, hidden, *arrays):
    edge = (16, EDGE, WIDTH)
    row = jax.ShapeDtypeStruct((1, WIDTH), jnp.float32)
    two = jax.ShapeDtypeStruct((2, WIDTH), jnp.float32)
    return call(
        stage_kernel,
        "stage",
        [jax.ShapeDtypeStruct(x.shape, x.dtype) for x in arrays] + [row, two, edge, edge],
        [VMEM, SMEM, SMEM, VMEM, VMEM] + [HBM] * len(arrays),
        scratch=[pltpu.SemaphoreType.DMA((len(arrays),))],
        mib=24,
    )(token, pitch_at, sharp, lookup, hidden, *arrays)


def cell_sum_kernel(arrived, feat, send_a, send_b, block, sems):
    loads = [
        pltpu.make_async_copy(arrived.at[pl.ds(32 * i, 32)], block.at[pl.ds(32 * i, 32)], sems.at[i]) for i in range(4)
    ]
    for load in loads:
        load.start()
    cell = lax.broadcasted_iota(jnp.int32, (256, 128), 0).astype(jnp.float32)
    total = jnp.zeros((256, 128), jnp.float32)
    for step in range(4):
        loads[step].wait()
        here = slice(step * 32, step * 32 + 32)
        ids = jnp.sum(block[here, 16:24, :].astype(jnp.float32).reshape(4, 8, 8, 128), axis=1)
        picks = []
        for part in range(4):
            wide = jnp.broadcast_to(ids[part][None], (32, 8, 128)).reshape(256, 128)
            picks.append(jnp.where(wide == cell, 1.0, 0.0).astype(jnp.bfloat16))
        total = total + dot(jnp.concatenate(picks, axis=1), block[here, 0:16, :].reshape(512, 128))
    total = rounded(total).reshape(16, 16, 128)
    feat[...] = total.astype(jnp.bfloat16)
    even = lax.rem(lax.axis_index("rad"), 2) == 0
    low = total[:, :EDGE]
    high = total[:, EDGE:]
    send_a[...] = jnp.where(even, high, low).astype(jnp.bfloat16)
    send_b[...] = jnp.where(even, low, high).astype(jnp.bfloat16)


def cell_sums(arrived):
    return call(
        cell_sum_kernel,
        "cell_sums",
        [(16, 16, 128), (16, EDGE, 128), (16, EDGE, 128)],
        [HBM],
        scratch=[pltpu.VMEM((128, 24, 128), jnp.bfloat16), pltpu.SemaphoreType.DMA((4,))],
    )(arrived)


def band_kernel(feat, feat_a, feat_b, hid, hid_a, hid_b, pitch, w_map, first, second):
    even = lax.rem(lax.axis_index("rad"), 2) == 0

    def wide(own, got_a, got_b, at):
        here = slice(at, at + 8)
        a = got_a[here].astype(jnp.float32)
        b = got_b[here].astype(jnp.float32)
        from_a = (lax.broadcasted_iota(jnp.int32, a.shape, 1) < HALO) == even
        parts = [own[here].astype(jnp.float32), jnp.where(from_a, a, b), jnp.where(from_a, b, a)]
        return jnp.concatenate(parts, axis=1).reshape(256, a.shape[-1])

    for at, out in ((0, first), (8, second)):
        x = dot(wide(feat, feat_a, feat_b, at).astype(jnp.bfloat16), w_map[...])
        x = wide(hid, hid_a, hid_b, at) + x + pitch[...]
        out[...] = x.reshape(8, 32, WIDTH).astype(jnp.bfloat16)


def band(*arrays):
    return call(band_kernel, "band", [(EDGE, 32, WIDTH)] * 2, [VMEM] * 8)(*arrays)


def project(w, layer, block, rows, block_ones, target, at, scale=None, plain=False):
    x = dot(rows, w[layer, :, block * 256 : block * 256 + 256])
    lanes = slice(block % 2 * 256, block % 2 * 256 + 256)
    yield
    if not plain:
        x = rounded(x)
        squares = dot((x * x).astype(jnp.bfloat16), block_ones[...])
        yield
        x = x * lax.rsqrt(squares + 1e-06)
    if scale is not None:
        x = x * scale[layer : layer + 1, lanes]
    target[at : at + x.shape[0], lanes] = x.astype(jnp.bfloat16)


def project_all(w, layer, wide, narrow, block_ones, scale, queries, q_at, keys, values, at):
    parts = [project(w, layer, block, wide, block_ones, keys, at) for block in (2, 3)]
    parts += [project(w, layer, block, narrow, block_ones, queries, q_at, scale) for block in (0, 1)]
    return parts + [project(w, layer, block, wide, block_ones, values, at, plain=True) for block in (4, 5)]


def query_lanes(table):
    r = lax.axis_index("rad")
    lane = lax.broadcasted_iota(jnp.int32, (1, 128), 1)
    ends = ((lane == 48) & (r == 0)) | ((lane == 49) & (r == lax.axis_size("rad") - 1))
    return table + jnp.where(ends, 1.0, 0.0).astype(jnp.bfloat16)


def attend(queries, query_aug, keys, key_aug, values, att):
    n = query_aug.shape[0]
    lane = lax.broadcasted_iota(jnp.int32, (1, 128), 1)
    low = jnp.where(lane < 64, 1.0, 0.0).astype(jnp.bfloat16)
    high = jnp.where(lane < 64, 0.0, 1.0).astype(jnp.bfloat16)
    half = lax.broadcasted_iota(jnp.int32, (n, 128), 1) < 64
    one = jnp.ones((key_aug.shape[0], 128), jnp.bfloat16)

    def pair_of_heads(pair):
        lanes = slice(pair * 128, pair * 128 + 128)

        def rows(parts):
            return jnp.concatenate([ref[at : at + count, lanes] for ref, at, count in parts], axis=0)

        q = rows(queries)
        q = jnp.concatenate(
            [jnp.concatenate([q * low, query_aug], axis=1), jnp.concatenate([q * high, query_aug], axis=1)], axis=0
        )
        k = jnp.concatenate([rows(keys), key_aug], axis=1)
        score = lax.dot_general(q, k, (((1,), (1,)), ((), ())), preferred_element_type=jnp.float32)
        yield
        got = dot(jnp.exp2(score).astype(jnp.bfloat16), jnp.concatenate([rows(values), one], axis=1))
        yield
        top = jnp.where(half, got[:n, :128], got[n:, :128])
        total = jnp.where(half, got[:n, 128:], got[n:, 128:])
        att[0:n, lanes] = (top / total).astype(jnp.bfloat16)

    return [pair_of_heads(pair) for pair in range(HEADS // 2)]


def columns(x, at, count, width):
    return x[at : at + count, :width].reshape(count * width, WIDTH)


def inner_kernel(
    first, second, scale, gains, w_qkv, w_out, block_ones, q_aug, k_aug,
    queries, keys, values, stream, queries_1, keys_1, values_1, att,
):
    x = jnp.concatenate([first[...], second[...]], axis=0).astype(jnp.float32)
    normed = norm_rows(x.reshape(512, WIDTH), gains[0:1, :])
    narrow = columns(normed.reshape(16, 32, WIDTH), 0, 16, 24).astype(jnp.bfloat16)
    wide = normed.astype(jnp.bfloat16)
    interleave(project_all(w_qkv, 0, wide, narrow, block_ones, scale, queries, 0, keys, values, 0), 2)
    pairs = attend(
        [(queries, 96, 192)], query_lanes(q_aug[192:384]), [(keys, 0, 512)], k_aug[256:768], [(values, 0, 512)], att
    )
    interleave(pairs, 2)
    x = rounded(columns(x, 4, 8, 24) + dot(att[...], w_out[0]))
    stream[...] = x.astype(jnp.bfloat16)
    normed = norm_rows(x, gains[1:2, :])
    narrow = columns(normed.reshape(8, 24, WIDTH), 0, 8, 16).astype(jnp.bfloat16)
    wide = normed.astype(jnp.bfloat16)
    interleave(project_all(w_qkv, 1, wide, narrow, block_ones, scale, queries_1, 0, keys_1, values_1, 0), 2)


def inner(*arrays):
    outs = [(384, WIDTH), (512, WIDTH), (512, WIDTH), (192, WIDTH), (128, WIDTH), (192, WIDTH), (192, WIDTH)]
    scratch = [pltpu.VMEM((192, WIDTH), jnp.bfloat16)]
    return call(inner_kernel, "inner", outs, [VMEM] * 9, scratch=scratch, mib=14)(*arrays)


def outer_kernel(
    low, high, first, second, scale, gains, w_qkv, w_out, last_gain, block_ones, q_aug, k_aug, q_aug_1, k_aug_1,
    q_mid, k_mid, v_mid, stream_mid, q1_mid, k1_mid, v1_mid,
    out, q_end, k_end, v_end, q1_end, k1_end, v1_end, att_0, att_1,
):
    att = (att_0, att_1)
    x = jnp.concatenate([low[...], high[...]], axis=0).astype(jnp.float32)
    normed = norm_rows(x.reshape(512, WIDTH), gains[0:1, :])
    narrow = columns(normed.reshape(16, 32, WIDTH), 4, 8, 24).astype(jnp.bfloat16)
    wide = normed.astype(jnp.bfloat16)
    interleave(project_all(w_qkv, 0, wide, narrow, block_ones, scale, q_end, 0, k_end, v_end, 0), 2)
    pairs = []
    for part in range(2):
        if part == 0:
            q = [(q_end, 0, 96), (q_mid, 0, 96)]
            k, v = [[(end, 0, 256), (mid, 0, 256)] for end, mid in ((k_end, k_mid), (v_end, v_mid))]
        else:
            q = [(q_mid, 288, 96), (q_end, 96, 96)]
            k, v = [[(mid, 256, 256), (end, 256, 256)] for end, mid in ((k_end, k_mid), (v_end, v_mid))]
        q_lanes = query_lanes(q_aug[384 * part : 384 * part + 192])
        pairs.append(attend(q, q_lanes, k, k_aug[512 * part : 512 * part + 512], v, att[part]))
    kept = [None, None]

    def finish(part):
        at = 4 * (1 - part)
        ours = first if part == 0 else second
        before = [columns(x, 4 + 4 * part, 4, 24), columns(ours[...].astype(jnp.float32), 4 * part, 4, 24)]
        y = dot(att[part][...], w_out[0])
        yield
        y = rounded(jnp.concatenate(before if part == 0 else before[::-1], axis=0) + y)
        normed = norm_rows(y, gains[1:2, :])
        narrow = columns(normed.reshape(8, 24, WIDTH), at, 4, 16).astype(jnp.bfloat16)
        kept[part] = columns(y.reshape(8, 24, WIDTH), at, 4, 16)
        yield
        wide = normed.astype(jnp.bfloat16)
        yield from one_by_one(
            *project_all(
                w_qkv, 1, wide, narrow, block_ones, scale, q1_end, 64 * part, k1_end, v1_end, 192 * part
            )
        )

    interleave(pairs[0], 2)
    interleave([one_by_one(*pairs[1]), finish(0)], 2)
    middle = stream_mid[...].astype(jnp.float32).reshape(8, 24, WIDTH)
    pairs = []
    for part in range(2):
        if part == 0:
            q = [(q1_end, 0, 64), (q1_mid, 0, 64)]
            k, v = [[(end, 0, 192), (mid, 0, 192)] for end, mid in ((k1_end, k1_mid), (v1_end, v1_mid))]
        else:
            q = [(q1_mid, 64, 64), (q1_end, 64, 64)]
            k, v = [[(mid, 0, 192), (end, 192, 192)] for end, mid in ((k1_end, k1_mid), (v1_end, v1_mid))]
        q_lanes = query_lanes(q_aug_1[128 * part : 128 * part + 128])
        pairs.append(attend(q, q_lanes, k, k_aug_1[192 * part : 192 * part + 384], v, att[part]))

    def end(part):
        before = [columns(middle, 4 * part, 4, 16), kept[part]]
        y = dot(att[part][0:128], w_out[1])
        yield
        y = rounded(jnp.concatenate(before if part else before[::-1], axis=0) + y)
        latent = norm_rows(y, last_gain[...])
        out[8 * part : 8 * part + 8] = latent.reshape(8, 16, WIDTH).astype(jnp.bfloat16)

    interleave([finish(1), one_by_one(*pairs[0])], 2)
    interleave([one_by_one(*pairs[1]), end(0)], 2)
    interleave([end(1)], 1)


def outer(*arrays):
    scratch = [192, 512, 512, 128, 384, 384, 192, 192]
    return call(
        outer_kernel,
        "outer",
        [(16, 16, WIDTH)],
        [VMEM] * 21,
        scratch=[pltpu.VMEM((rows, WIDTH), jnp.bfloat16) for rows in scratch],
        mib=14,
    )(*arrays)[0]


def swap(x, shift):
    count = lax.axis_size("rad")
    pairs = [(i, ((i + shift) ^ 1) - shift) for i in range(count)]
    return lax.ppermute(x, "rad", [(i, j) for i, j in pairs if 0 <= j < count])


def pass_on(x, step):
    count = lax.axis_size("az")
    return lax.ppermute(x, "az", [(i, (i + step) % count) for i in range(count)])


def per_device(
    hidden_site_vector,
    mesh_portion_descriptors,
    mesh_entry_site,
    mesh_portion_tally,
    incline_grid_position,
    incline_vector_lookup,
    mesh_mapping_matrix,
    prefocus_rescale_factor,
    probe_lock_payload_matrix,
    sharpness_scale,
    final_mapping_matrix,
    terminal_rescale_factor,
):
    packed, token = pack(
        mesh_portion_descriptors.reshape(128, 16, 128), mesh_entry_site.reshape(16, 128), mesh_portion_tally
    )
    arrived = lax.all_to_all(packed, ("az", "rad"), split_axis=0, concat_axis=0, tiled=True)

    hidden = hidden_site_vector[0]
    block_ones = jnp.asarray(np.kron(np.eye(4), np.ones((64, 64))), jnp.bfloat16)
    gains, w_qkv, w_out, w_map, last_gain, block_ones, q_aug, k_aug, q_aug_1, k_aug_1, pitch, scale, to_a, to_b = stage(
        token,
        incline_grid_position,
        sharpness_scale,
        incline_vector_lookup,
        hidden,
        prefocus_rescale_factor,
        probe_lock_payload_matrix,
        final_mapping_matrix,
        mesh_mapping_matrix,
        terminal_rescale_factor[None, :],
        block_ones,
        *window_tables(),
    )
    hid_a, hid_b = swap(to_a, 0), swap(to_b, 1)

    feat, to_a, to_b = cell_sums(arrived)
    feat_a, feat_b = swap(to_a, 0), swap(to_b, 1)
    first, second = band(feat, feat_a, feat_b, hidden, hid_a, hid_b, pitch, w_map)
    low, high = pass_on(second, 1), pass_on(first, -1)
    middle = inner(first, second, scale, gains, w_qkv, w_out, block_ones, q_aug, k_aug)
    out = outer(
        low, high, first, second, scale, gains, w_qkv, w_out, last_gain,
        block_ones, q_aug, k_aug, q_aug_1, k_aug_1, *middle,
    )
    return out[None]


def solution(mesh):
    rows = P(("az", "rad"), None)
    in_specs = (P(None, "az", "rad", None), rows, P(("az", "rad")), rows) + (P(),) * 8
    return jax.shard_map(
        per_device,
        mesh=mesh,
        in_specs=in_specs,
        out_specs=P(None, "az", "rad", None),
        check_vma=False,
    )
```

profile of v0, /device:TPU:8, one launch (start us, length us, event | category | flops | bytes accessed | tf_op | source)
XLA Modules:
  0.0 58.6 jit_solution(4256666443472880124)
XLA Ops:
  0.0 0.0 copy-start.8
  0.1 2.6 %pack.1 = (bf16[128,24,128]{2,1,0:T(8,128)(2,1)}, f32[8,128]{1,0:T(8,128)}) custom-call(bf16[128,16,128]{2,1,0:T(8,128)(2,1)} %bitcast.8, s32[16,128]{1,0:T(8,128)} %bitcast.9, s32[1,128]{1,0:T(1,128)} %tally.1), custom_call_target="tpu_custom_call" | custom-call | flops 1500000000 | bytes 4500000 | tf_op jit(solution)/shard_map/pack/pallas_call | solution.py:131
  2.8 10.5 %all-to-all-start = ((bf16[128,24,128]{2,1,0:T(8,128)(2,1)}), bf16[128,24,128]{2,1,0:T(8,128)(2,1)S(1)}, u32[]{:S(2)}, u32[]{:S(2)}) async-start(bf16[128,24,128]{2,1,0:T(8,128)(2,1)} %get-tuple-element.33), calls=%async_computation | async-start | bytes 1572864 | tf_op jit(solution)/shard_map/all_to_all | solution.py:441
  14.0 1.9 %copy-done = bf16[2,512,1536]{2,1,0:T(8,128)(2,1)S(1)} copy-done((bf16[2,512,1536]{2,1,0:T(8,128)(2,1)S(1)}, bf16[2,512,1536]{2,1,0:T(8,128)(2,1)}, u32[]{:S(2)}) %copy-start) | copy-done | bytes 3145752
  15.9 0.7 %copy-done.25 = f32[8,128]{1,0:T(8,128)S(1)} copy-done((f32[8,128]{1,0:T(8,128)S(1)}, f32[8,128]{1,0:T(8,128)}, u32[]{:S(2)}) %copy-start.25) | copy-done | bytes 4120
  16.6 2.0 %stage.1 = (f32[2,512]{1,0:T(2,128)S(1)}, bf16[2,512,1536]{2,1,0:T(8,128)(2,1)S(1)}, bf16[2,512,512]{2,1,0:T(8,128)(2,1)S(1)}, bf16[128,512]{1,0:T(8,128)(2,1)S(...) custom-call(f32[8,128]{1,0:T(8,128)S(1)} %copy-done.25, ...), custom_call_target="tpu_custom_call" | custom-call | flops 3000000000 | bytes 9000000 | tf_op jit(solution)/shard_map/stage/pallas_call | solution.py:178
  18.6 1.6 %copy-done.13 = bf16[2,512,1536]{2,1,0:T(8,128)(2,1)} copy-done((bf16[2,512,1536]{2,1,0:T(8,128)(2,1)}, bf16[2,512,1536]{2,1,0:T(8,128)(2,1)S(1)}, u32[]{:S(2)}) %copy-start.13) | copy-done | bytes 3145752
  20.2 1.0 %copy-done.15 = bf16[2,512,512]{2,1,0:T(8,128)(2,1)} copy-done((bf16[2,512,512]{2,1,0:T(8,128)(2,1)}, bf16[2,512,512]{2,1,0:T(8,128)(2,1)S(1)}, u32[]{:S(2)}) %copy-start.15) | copy-done | bytes 1048600
  21.2 0.7 %copy-done.17 = bf16[1024,128]{1,0:T(8,128)(2,1)} copy-done((bf16[1024,128]{1,0:T(8,128)(2,1)}, bf16[1024,128]{1,0:T(8,128)(2,1)S(1)}, u32[]{:S(2)}) %copy-start.17) | copy-done | bytes 262168
  21.9 0.7 %copy-done.19 = bf16[576,128]{1,0:T(8,128)(2,1)} copy-done((bf16[576,128]{1,0:T(8,128)(2,1)}, bf16[576,128]{1,0:T(8,128)(2,1)S(1)}, u32[]{:S(2)}) %copy-start.19) | copy-done | bytes 147480
  22.6 0.7 %copy-done.21 = bf16[576,128]{1,0:T(8,128)(2,1)} copy-done((bf16[576,128]{1,0:T(8,128)(2,1)}, bf16[576,128]{1,0:T(8,128)(2,1)S(1)}, u32[]{:S(2)}) %copy-start.21) | copy-done | bytes 147480
  23.2 0.7 %copy-done.23 = bf16[256,256]{1,0:T(8,128)(2,1)} copy-done((bf16[256,256]{1,0:T(8,128)(2,1)}, bf16[256,256]{1,0:T(8,128)(2,1)S(1)}, u32[]{:S(2)}) %copy-start.23) | copy-done | bytes 131096
  23.9 3.0 %collective-permute-start.2 = (bf16[16,8,512]{2,1,0:T(8,128)(2,1)S(1)}, bf16[16,8,512]{2,1,0:T(8,128)(2,1)S(1)}, u32[]{:S(2)}, u32[]{:S(2)}) collective-permute-start(bf16[16,8,512]{2,1,0:T(8,128)(2,1)S(1)} %get-tuple-element.38), channel_id=1, source_target_pairs={{0,1},{1,0},{2,3},{3,2},{4,5},{5,4},{6,7},{7,6},{8,9},{9,8},{10,11... | collective-permute-start | bytes 393224 | tf_op jit(solution)/shard_map/ppermute | solution.py:416
  26.9 3.0 %collective-permute-start.3 = (bf16[16,8,512]{2,1,0:T(8,128)(2,1)S(1)}, bf16[16,8,512]{2,1,0:T(8,128)(2,1)S(1)}, u32[]{:S(2)}, u32[]{:S(2)}) collective-permute-start(bf16[16,8,512]{2,1,0:T(8,128)(2,1)S(1)} %get-tuple-element.39), channel_id=1, source_target_pairs={{1,2},{2,1},{3,4},{4,3},{5,6},{6,5},{9,10},{10,9},{11,12},{12,11},... | collective-permute-start | bytes 393224 | tf_op jit(solution)/shard_map/ppermute | solution.py:416
  29.8 1.8 %cell_sums.1 = (bf16[16,16,128]{2,1,0:T(8,128)(2,1)S(1)}, bf16[16,8,128]{2,1,0:T(8,128)(2,1)S(1)}, bf16[16,8,128]{2,1,0:T(8,128)(2,1)S(1)}) custom-call(bf16[128,24,128]{2,1,0:T(8,128)(2,1)S(1)} %all-to-all-done.arrived), custom_call_target="tpu_custom_call" | custom-call | flops 2000000000 | bytes 6000000 | tf_op jit(solution)/shard_map/cell_sums/pallas_call | solution.py:215
  31.7 3.5 %collective-permute-start = (bf16[16,8,128]{2,1,0:T(8,128)(2,1)S(1)}, bf16[16,8,128]{2,1,0:T(8,128)(2,1)S(1)}, u32[]{:S(2)}, u32[]{:S(2)}) collective-permute-start(bf16[16,8,128]{2,1,0:T(8,128)(2,1)S(1)} %get-tuple-element.35), channel_id=1, source_target_pairs={{0,1},{1,0},{2,3},{3,2},{4,5},{5,4},{6,7},{7,6},{8,9},{9,8},{10,11... | collective-permute-start | bytes 98312 | tf_op jit(solution)/shard_map/ppermute | solution.py:416
  35.2 2.2 %collective-permute-start.1 = (bf16[16,8,128]{2,1,0:T(8,128)(2,1)S(1)}, bf16[16,8,128]{2,1,0:T(8,128)(2,1)S(1)}, u32[]{:S(2)}, u32[]{:S(2)}) collective-permute-start(bf16[16,8,128]{2,1,0:T(8,128)(2,1)S(1)} %get-tuple-element.36), channel_id=1, source_target_pairs={{1,2},{2,1},{3,4},{4,3},{5,6},{6,5},{9,10},{10,9},{11,12},{12,11},... | collective-permute-start | bytes 98312 | tf_op jit(solution)/shard_map/ppermute | solution.py:416
  37.4 6.0 %collective-permute-done.1.feat_b = bf16[16,8,128]{2,1,0:T(8,128)(2,1)S(1)} collective-permute-done((bf16[16,8,128]{2,1,0:T(8,128)(2,1)S(1)}, bf16[16,8,128]{2,1,0:T(8,128)(2,1)S(1)}, u32[]{:S(2)}, u32[]{:S(2)}) %collective-permute-start.1) | collective-permute-done | bytes 32800 | tf_op jit(solution)/shard_map/ppermute | solution.py:416
  43.4 0.3 band.1
  43.7 0.1 collective-permute-start.4
  43.8 3.8 %collective-permute-start.5 = (bf16[8,32,512]{2,1,0:T(8,128)(2,1)S(1)}, bf16[8,32,512]{2,1,0:T(8,128)(2,1)S(1)}, u32[]{:S(2)}, u32[]{:S(2)}) collective-permute-start(bf16[8,32,512]{2,1,0:T(8,128)(2,1)S(1)} %get-tuple-element.43.first), channel_id=1, source_target_pairs={{0,120},{8,0},{16,8},{24,16},{32,24},{40,32},{48,40},{56,48},{64,5... | collective-permute-start | bytes 786440 | tf_op jit(solution)/shard_map/ppermute | solution.py:421
  47.6 3.3 %inner.1 = (bf16[384,512]{1,0:T(8,128)(2,1)S(1)}, bf16[512,512]{1,0:T(8,128)(2,1)S(1)}, bf16[512,512]{1,0:T(8,128)(2,1)S(1)}, bf16[192,512]{1,0:T(8,128)(2,1)S(1...) custom-call(bf16[8,32,512]{2,1,0:T(8,128)(2,1)S(1)} %get-tuple-element.43.first, ...), custom_call_target="tpu_custom_call" | custom-call | flops 4000000000 | bytes 12000000 | tf_op jit(solution)/shard_map/inner/pallas_call | solution.py:330
  51.0 0.7 %collective-permute-done.4.low = bf16[8,32,512]{2,1,0:T(8,128)(2,1)S(1)} collective-permute-done((bf16[8,32,512]{2,1,0:T(8,128)(2,1)S(1)}, bf16[8,32,512]{2,1,0:T(8,128)(2,1)S(1)}, u32[]{:S(2)}, u32[]{:S(2)}) %collective-permute-start.4) | collective-permute-done | bytes 262176 | tf_op jit(solution)/shard_map/ppermute | solution.py:421
  51.7 7.0 %outer.1 = bf16[16,16,512]{2,1,0:T(8,128)(2,1)} custom-call(bf16[8,32,512]{2,1,0:T(8,128)(2,1)S(1)} %collective-permute-done.4.low, bf16[8,32,512]{2,1,0:T(8,128)(2,1)S(1)} %collective-permute-done.5.high, bf16[8,32,512]{2,1,0:T(8,128)(2,1)S(1)} %get-tuple-element.43.first, bf16[8,32,512]{2,1,0:T(8,128)(2,1)S(1)} %get-tuple-element.42.second, ...), custom_call_target="tpu_custom_call" | custom-call | flops 8000000000 | bytes 24000000 | tf_op jit(solution)/shard_map/outer/pallas_call | solution.py:403
  (48 shorter events, 0.1 us)
Async XLA Ops:
  0.0 13.9 %copy-start.1 = (bf16[2,512,512]{2,1,0:T(8,128)(2,1)S(1)}, bf16[2,512,512]{2,1,0:T(8,128)(2,1)}, u32[]{:S(2)}) copy-start(bf16[2,512,512]{2,1,0:T(8,128)(2,1)} %refs_2_.1) | copy-start | bytes 3145732
  0.0 13.9 %copy-start.2 = (bf16[1,16,16,512]{3,2,1,0:T(8,128)(2,1)S(1)}, bf16[1,16,16,512]{3,2,1,0:T(8,128)(2,1)}, u32[]{:S(2)}) copy-start(bf16[1,16,16,512]{3,2,1,0:T(8,128)(2,1)} %param.17) | copy-start | bytes 786436
  0.0 13.9 %copy-start.3 = (bf16[128,512]{1,0:T(8,128)(2,1)S(1)}, bf16[128,512]{1,0:T(8,128)(2,1)}, u32[]{:S(2)}) copy-start(bf16[128,512]{1,0:T(8,128)(2,1)} %refs_3_.1) | copy-start | bytes 393220
  0.0 13.9 %copy-start.4 = (bf16[64,512]{1,0:T(8,128)(2,1)S(1)}, bf16[64,512]{1,0:T(8,128)(2,1)}, u32[]{:S(2)}) copy-start(bf16[64,512]{1,0:T(8,128)(2,1)} %lookup.1) | copy-start | bytes 196612
  0.0 13.9 %copy-start.5 = (f32[2,512]{1,0:T(2,128)S(1)}, f32[2,512]{1,0:T(2,128)}, u32[]{:S(2)}) copy-start(f32[2,512]{1,0:T(2,128)} %refs_0_.1) | copy-start | bytes 12292
  0.0 13.9 %copy-start.6 = (f32[512]{0:T(512)S(1)}, f32[512]{0:T(512)}, u32[]{:S(2)}) copy-start(f32[512]{0:T(512)} %param.28) | copy-start | bytes 6148
  0.0 13.9 %copy-start.7 = (f32[2,8]{1,0:T(2,128)S(1)}, f32[2,8]{1,0:T(2,128)}, u32[]{:S(2)}) copy-start(f32[2,8]{1,0:T(2,128)} %sharp.1) | copy-start | bytes 196
  0.0 13.9 %copy-start.8 = (bf16[1024,128]{1,0:T(8,128)(2,1)S(1)}, bf16[1024,128]{1,0:T(8,128)(2,1)}, u32[]{:S(2)}) copy-start(bf16[1024,128]{1,0:T(8,128)(2,1)} %constant.12.clone.refs_7_) | copy-start | bytes 786436
  0.1 13.9 %copy-start.9 = (bf16[576,128]{1,0:T(8,128)(2,1)S(1)}, bf16[576,128]{1,0:T(8,128)(2,1)}, u32[]{:S(2)}) copy-start(bf16[576,128]{1,0:T(8,128)(2,1)} %constant.14.clone.refs_9_) | copy-start | bytes 442372
  0.1 13.9 %copy-start.10 = (bf16[576,128]{1,0:T(8,128)(2,1)S(1)}, bf16[576,128]{1,0:T(8,128)(2,1)}, u32[]{:S(2)}) copy-start(bf16[576,128]{1,0:T(8,128)(2,1)} %constant.11.clone.refs_6_) | copy-start | bytes 442372
  0.1 13.9 %copy-start.11 = (bf16[256,256]{1,0:T(8,128)(2,1)S(1)}, bf16[256,256]{1,0:T(8,128)(2,1)}, u32[]{:S(2)}) copy-start(bf16[256,256]{1,0:T(8,128)(2,1)} %constant.10.clone.refs_5_) | copy-start | bytes 393220
  0.1 13.9 %copy-start.12 = (bf16[256,128]{1,0:T(8,128)(2,1)S(1)}, bf16[256,128]{1,0:T(8,128)(2,1)}, u32[]{:S(2)}) copy-start(bf16[256,128]{1,0:T(8,128)(2,1)} %constant.13.clone.refs_8_) | copy-start | bytes 196612
  2.8 27.1 %all-to-all-start = ((bf16[128,24,128]{2,1,0:T(8,128)(2,1)}), bf16[128,24,128]{2,1,0:T(8,128)(2,1)S(1)}, u32[]{:S(2)}, u32[]{:S(2)}) async-start(bf16[128,24,128]{2,1,0:T(8,128)(2,1)} %get-tuple-element.33), calls=%async_computation | async-start | bytes 1572864 | tf_op jit(solution)/shard_map/all_to_all | solution.py:441
  23.9 13.5 %collective-permute-start.2 = (bf16[16,8,512]{2,1,0:T(8,128)(2,1)S(1)}, bf16[16,8,512]{2,1,0:T(8,128)(2,1)S(1)}, u32[]{:S(2)}, u32[]{:S(2)}) collective-permute-start(bf16[16,8,512]{2,1,0:T(8,128)(2,1)S(1)} %get-tuple-element.38), channel_id=1, source_target_pairs={{0,1},{1,0},{2,3},{3,2},{4,5},{5,4},{6,7},{7,6},{8,9},{9,8},{10,11... | collective-permute-start | bytes 393224 | tf_op jit(solution)/shard_map/ppermute | solution.py:416
  26.9 10.5 %collective-permute-start.3 = (bf16[16,8,512]{2,1,0:T(8,128)(2,1)S(1)}, bf16[16,8,512]{2,1,0:T(8,128)(2,1)S(1)}, u32[]{:S(2)}, u32[]{:S(2)}) collective-permute-start(bf16[16,8,512]{2,1,0:T(8,128)(2,1)S(1)} %get-tuple-element.39), channel_id=1, source_target_pairs={{1,2},{2,1},{3,4},{4,3},{5,6},{6,5},{9,10},{10,9},{11,12},{12,11},... | collective-permute-start | bytes 393224 | tf_op jit(solution)/shard_map/ppermute | solution.py:416
  31.7 15.9 %copy-start.14 = (bf16[2,512,1536]{2,1,0:T(8,128)(2,1)S(1)}, bf16[2,512,1536]{2,1,0:T(8,128)(2,1)}, u32[]{:S(2)}) copy-start(bf16[2,512,1536]{2,1,0:T(8,128)(2,1)} %copy-done.13) | copy-start | bytes 9437188
  31.7 15.9 %copy-start.16 = (bf16[2,512,512]{2,1,0:T(8,128)(2,1)S(1)}, bf16[2,512,512]{2,1,0:T(8,128)(2,1)}, u32[]{:S(2)}) copy-start(bf16[2,512,512]{2,1,0:T(8,128)(2,1)} %copy-done.15) | copy-start | bytes 3145732
  31.7 15.9 %copy-start.18 = (bf16[1024,128]{1,0:T(8,128)(2,1)S(1)}, bf16[1024,128]{1,0:T(8,128)(2,1)}, u32[]{:S(2)}) copy-start(bf16[1024,128]{1,0:T(8,128)(2,1)} %copy-done.17) | copy-start | bytes 786436
  31.7 15.9 %copy-start.20 = (bf16[576,128]{1,0:T(8,128)(2,1)S(1)}, bf16[576,128]{1,0:T(8,128)(2,1)}, u32[]{:S(2)}) copy-start(bf16[576,128]{1,0:T(8,128)(2,1)} %copy-done.19) | copy-start | bytes 442372
  31.7 15.9 %copy-start.24 = (bf16[256,256]{1,0:T(8,128)(2,1)S(1)}, bf16[256,256]{1,0:T(8,128)(2,1)}, u32[]{:S(2)}) copy-start(bf16[256,256]{1,0:T(8,128)(2,1)} %copy-done.23) | copy-start | bytes 393220
  31.7 5.7 %collective-permute-start = (bf16[16,8,128]{2,1,0:T(8,128)(2,1)S(1)}, bf16[16,8,128]{2,1,0:T(8,128)(2,1)S(1)}, u32[]{:S(2)}, u32[]{:S(2)}) collective-permute-start(bf16[16,8,128]{2,1,0:T(8,128)(2,1)S(1)} %get-tuple-element.35), channel_id=1, source_target_pairs={{0,1},{1,0},{2,3},{3,2},{4,5},{5,4},{6,7},{7,6},{8,9},{9,8},{10,11... | collective-permute-start | bytes 98312 | tf_op jit(solution)/shard_map/ppermute | solution.py:416
  35.2 8.2 %collective-permute-start.1 = (bf16[16,8,128]{2,1,0:T(8,128)(2,1)S(1)}, bf16[16,8,128]{2,1,0:T(8,128)(2,1)S(1)}, u32[]{:S(2)}, u32[]{:S(2)}) collective-permute-start(bf16[16,8,128]{2,1,0:T(8,128)(2,1)S(1)} %get-tuple-element.36), channel_id=1, source_target_pairs={{1,2},{2,1},{3,4},{4,3},{5,6},{6,5},{9,10},{10,9},{11,12},{12,11},... | collective-permute-start | bytes 98312 | tf_op jit(solution)/shard_map/ppermute | solution.py:416
  43.7 8.0 %collective-permute-start.4 = (bf16[8,32,512]{2,1,0:T(8,128)(2,1)S(1)}, bf16[8,32,512]{2,1,0:T(8,128)(2,1)S(1)}, u32[]{:S(2)}, u32[]{:S(2)}) collective-permute-start(bf16[8,32,512]{2,1,0:T(8,128)(2,1)S(1)} %get-tuple-element.42.second), channel_id=1, source_target_pairs={{0,8},{8,16},{16,24},{24,32},{32,40},{40,48},{48,56},{56,64},{64,7... | collective-permute-start | bytes 786440 | tf_op jit(solution)/shard_map/ppermute | solution.py:421
  43.8 7.9 %collective-permute-start.5 = (bf16[8,32,512]{2,1,0:T(8,128)(2,1)S(1)}, bf16[8,32,512]{2,1,0:T(8,128)(2,1)S(1)}, u32[]{:S(2)}, u32[]{:S(2)}) collective-permute-start(bf16[8,32,512]{2,1,0:T(8,128)(2,1)S(1)} %get-tuple-element.43.first), channel_id=1, source_target_pairs={{0,120},{8,0},{16,8},{24,16},{32,24},{40,32},{48,40},{56,48},{64,5... | collective-permute-start | bytes 786440 | tf_op jit(solution)/shard_map/ppermute | solution.py:421
  (9 other events, 11.9 us)
where the time goes:
time: 59.1 us; the launch traced here: 58.6 us
  starting transfers between devices  25.9 us (44%)
  Pallas kernels  17.1 us (29%)
  local copies, waits for them, and re-layouts  7.96 us (13%)
  waiting for transfers between devices  6.66 us (11%)
  between operations  1.01 us (2%)
    ppermute x4, starting transfers between devices, swap(): return lax.ppermute(x, 'rad', [(i, j) for i, j in pairs if 0 <= j < count])  11.6 us
    all_to_all x1, starting transfers between devices, per_device(): lax.all_to_all(packed, ('az', 'rad'), split_axis=0, concat_axis=0, tiled=...  10.5 us
    unnamed x52, local copies, waits for them, and re-layouts  7.96 us
    pallas_call x1, Pallas kernels, outer(): call(outer_kernel, 'outer', [(16, 16, WIDTH)], [VMEM] * 21, scratch=[pltp...  6.96 us
    ppermute x4, waiting for transfers between devices, swap(): return lax.ppermute(x, 'rad', [(i, j) for i, j in pairs if 0 <= j < count])  5.99 us
    ppermute x2, starting transfers between devices, pass_on(): lax.ppermute(x, 'az', [(i, (i + step) % count) for i in range(count)])  3.92 us
    pallas_call x1, Pallas kernels, inner(): call(inner_kernel, 'inner', outs, [VMEM] * 9, scratch=scratch, mib=14)  3.35 us
    pallas_call x1, Pallas kernels, pack(): call(pack_kernel, 'pack', [(128, 24, 128), jax.ShapeDtypeStruct((8, 128),...  2.64 us
  transfers between devices with their start and end apart: 7, of which 2 were waited for; matrix products, arithmetic and copies ran while one was open for 0% of the time, Pallas kernels for 12%

commit v1 on v0

--- a/solution.py
+++ b/solution.py
@@ -57,7 +57,7 @@
     return x if isinstance(x, jax.ShapeDtypeStruct) else jax.ShapeDtypeStruct(x, jnp.bfloat16)
 
 
-COST = {"pack": 1.5, "stage": 3, "cell_sums": 2, "band": 1.5, "inner": 4, "outer": 8}
+COST = {"pack": 1.5, "stage": 1, "cell_sums": 2, "band": 1.5, "inner": 4, "outer": 8}
 
 
 def call(kernel, name, outs, in_specs, out_specs=None, scratch=(), mib=8):
@@ -145,13 +145,7 @@
     )(rows, cells, tally)
 
 
-def stage_kernel(token, pitch_at, sharp, lookup, hidden, *refs):
-    count = (len(refs) - 5) // 2
-    sources, copies = refs[:count], refs[count : 2 * count]
-    pitch, scale, send_a, send_b, sems = refs[2 * count :]
-    moves = [pltpu.make_async_copy(a, b, sems.at[i]) for i, (a, b) in enumerate(zip(sources, copies))]
-    for move in moves:
-        move.start()
+def stage_kernel(token, pitch_at, sharp, lookup, hidden, pitch, scale, send_a, send_b):
     rows = lax.broadcasted_iota(jnp.int32, (64, 1), 0)
     pitch[...] = jnp.sum(
         jnp.where(rows == pitch_at[0], lookup[...].astype(jnp.float32), 0.0), axis=0, keepdims=True
@@ -167,34 +161,19 @@
     high = hidden[:, EDGE:].astype(jnp.float32)
     send_a[...] = jnp.where(even, high, low).astype(jnp.bfloat16)
     send_b[...] = jnp.where(even, low, high).astype(jnp.bfloat16)
-    for move in moves:
-        move.wait()
-
-
-def stage(token, pitch_at, sharp, lookup, hidden, *arrays):
+
+
+def stage(*arrays):
     edge = (16, EDGE, WIDTH)
     row = jax.ShapeDtypeStruct((1, WIDTH), jnp.float32)
     two = jax.ShapeDtypeStruct((2, WIDTH), jnp.float32)
-    return call(
-        stage_kernel,
-        "stage",
-        [jax.ShapeDtypeStruct(x.shape, x.dtype) for x in arrays] + [row, two, edge, edge],
-        [VMEM, SMEM, SMEM, VMEM, VMEM] + [HBM] * len(arrays),
-        scratch=[pltpu.SemaphoreType.DMA((len(arrays),))],
-        mib=24,
-    )(token, pitch_at, sharp, lookup, hidden, *arrays)
-
-
-def cell_sum_kernel(arrived, feat, send_a, send_b, block, sems):
-    loads = [
-        pltpu.make_async_copy(arrived.at[pl.ds(32 * i, 32)], block.at[pl.ds(32 * i, 32)], sems.at[i]) for i in range(4)
-    ]
-    for load in loads:
-        load.start()
+    return call(stage_kernel, "stage", [row, two, edge, edge], [VMEM, SMEM, SMEM, VMEM, VMEM])(*arrays)
+
+
+def cell_sum_kernel(block, feat, send_a, send_b):
     cell = lax.broadcasted_iota(jnp.int32, (256, 128), 0).astype(jnp.float32)
     total = jnp.zeros((256, 128), jnp.float32)
     for step in range(4):
-        loads[step].wait()
         here = slice(step * 32, step * 32 + 32)
         ids = jnp.sum(block[here, 16:24, :].astype(jnp.float32).reshape(4, 8, 8, 128), axis=1)
         picks = []
@@ -216,8 +195,7 @@
         cell_sum_kernel,
         "cell_sums",
         [(16, 16, 128), (16, EDGE, 128), (16, EDGE, 128)],
-        [HBM],
-        scratch=[pltpu.VMEM((128, 24, 128), jnp.bfloat16), pltpu.SemaphoreType.DMA((4,))],
+        [VMEM],
     )(arrived)
 
 
@@ -442,29 +420,20 @@
 
     hidden = hidden_site_vector[0]
     block_ones = jnp.asarray(np.kron(np.eye(4), np.ones((64, 64))), jnp.bfloat16)
-    gains, w_qkv, w_out, w_map, last_gain, block_ones, q_aug, k_aug, q_aug_1, k_aug_1, pitch, scale, to_a, to_b = stage(
-        token,
-        incline_grid_position,
-        sharpness_scale,
-        incline_vector_lookup,
-        hidden,
-        prefocus_rescale_factor,
-        probe_lock_payload_matrix,
-        final_mapping_matrix,
-        mesh_mapping_matrix,
-        terminal_rescale_factor[None, :],
-        block_ones,
-        *window_tables(),
+    pitch, scale, to_a, to_b = stage(
+        token, incline_grid_position, sharpness_scale, incline_vector_lookup, hidden
     )
     hid_a, hid_b = swap(to_a, 0), swap(to_b, 1)
 
     feat, to_a, to_b = cell_sums(arrived)
     feat_a, feat_b = swap(to_a, 0), swap(to_b, 1)
-    first, second = band(feat, feat_a, feat_b, hidden, hid_a, hid_b, pitch, w_map)
+    first, second = band(feat, feat_a, feat_b, hidden, hid_a, hid_b, pitch, mesh_mapping_matrix)
     low, high = pass_on(second, 1), pass_on(first, -1)
-    middle = inner(first, second, scale, gains, w_qkv, w_out, block_ones, q_aug, k_aug)
+    q_aug, k_aug, q_aug_1, k_aug_1 = window_tables()
+    weights = (scale, prefocus_rescale_factor, probe_lock_payload_matrix, final_mapping_matrix)
+    middle = inner(first, second, *weights, block_ones, q_aug, k_aug)
     out = outer(
-        low, high, first, second, scale, gains, w_qkv, w_out, last_gain,
+        low, high, first, second, *weights, terminal_rescale_factor[None, :],
         block_ones, q_aug, k_aug, q_aug_1, k_aug_1, *middle,
     )
     return out[None]

time: 59.1 us -> 54.6 us (0.924)
  local copies, waits for them, and re-layouts: 7.96 us -> 0.76 us
  waiting for transfers between devices: 6.66 us -> 11.6 us
  Pallas kernels: 17.1 us -> 14.3 us
  starting transfers between devices: 25.9 us -> 26.8 us
    all_to_all x1, waiting for transfers between devices: 0.01 us -> 7.38 us  [per_device(): lax.all_to_all(packed, ('az', 'rad'), split_axis=0, concat_axis=0, tiled=...]
    unnamed x52 -> x28, local copies, waits for them, and re-layouts: 7.96 us -> 0.76 us
    ppermute x4, waiting for transfers between devices: 5.99 us -> 3.62 us  [swap(): return lax.ppermute(x, 'rad', [(i, j) for i, j in pairs if 0 <= j < count])]
    pallas_call x1, Pallas kernels: 1.84 us -> 0.43 us  [cell_sums(): call(cell_sum_kernel, 'cell_sums', [(16, 16, 128), (16, EDGE, 128), (16,...]
    pallas_call x1, Pallas kernels: 2 us -> 0.66 us  [stage(): call(stage_kernel, 'stage', [row, two, edge, edge], [VMEM, SMEM, SMEM, VM...]
    ppermute x4, starting transfers between devices: 11.6 us -> 12.5 us  [swap(): return lax.ppermute(x, 'rad', [(i, j) for i, j in pairs if 0 <= j < count])]
  transfers between devices with their start and end apart: 7 -> 7, of which waited for: 2 -> 3; matrix products, arithmetic and copies ran while one was open for 0% -> 0% of each run, Pallas kernels for 12% -> 8%
where the time goes in v1:
time: 54.6 us; the launch traced here: 54.3 us
  starting transfers between devices  26.8 us (49%)
  Pallas kernels  14.3 us (26%)
  waiting for transfers between devices  11.6 us (21%)
  between operations  0.88 us (2%)
  local copies, waits for them, and re-layouts  0.76 us (1%)
    ppermute x4, starting transfers between devices, swap(): return lax.ppermute(x, 'rad', [(i, j) for i, j in pairs if 0 <= j < count])  12.5 us
    all_to_all x1, starting transfers between devices, per_device(): lax.all_to_all(packed, ('az', 'rad'), split_axis=0, concat_axis=0, tiled=...  10.5 us
    all_to_all x1, waiting for transfers between devices, per_device(): lax.all_to_all(packed, ('az', 'rad'), split_axis=0, concat_axis=0, tiled=...  7.38 us
    pallas_call x1, Pallas kernels, outer(): call(outer_kernel, 'outer', [(16, 16, WIDTH)], [VMEM] * 21, scratch=[pltp...  6.98 us
    ppermute x2, starting transfers between devices, pass_on(): lax.ppermute(x, 'az', [(i, (i + step) % count) for i in range(count)])  3.92 us
    ppermute x4, waiting for transfers between devices, swap(): return lax.ppermute(x, 'rad', [(i, j) for i, j in pairs if 0 <= j < count])  3.62 us
    pallas_call x1, Pallas kernels, inner(): call(inner_kernel, 'inner', outs, [VMEM] * 9, scratch=scratch, mib=14)  3.37 us
    pallas_call x1, Pallas kernels, pack(): call(pack_kernel, 'pack', [(128, 24, 128), jax.ShapeDtypeStruct((8, 128),...  2.55 us
  transfers between devices with their start and end apart: 7, of which 3 were waited for; matrix products, arithmetic and copies ran while one was open for 0% of the time, Pallas kernels for 8%

profile of v1, /device:TPU:8, one launch (start us, length us, event | category | flops | bytes accessed | tf_op | source)
XLA Modules:
  0.0 54.3 jit_solution(10460229086146514797)
XLA Ops:
  0.0 2.6 %pack.1 = (bf16[128,24,128]{2,1,0:T(8,128)(2,1)}, f32[8,128]{1,0:T(8,128)}) custom-call(bf16[128,16,128]{2,1,0:T(8,128)(2,1)} %bitcast.8, s32[16,128]{1,0:T(8,128)} %bitcast.9, s32[1,128]{1,0:T(1,128)} %tally.1), custom_call_target="tpu_custom_call" | custom-call | flops 1500000000 | bytes 4500000 | tf_op jit(solution)/shard_map/pack/pallas_call | solution.py:131
  2.6 10.5 %all-to-all-start = ((bf16[128,24,128]{2,1,0:T(8,128)(2,1)}), bf16[128,24,128]{2,1,0:T(8,128)(2,1)S(1)}, u32[]{:S(2)}, u32[]{:S(2)}) async-start(bf16[128,24,128]{2,1,0:T(8,128)(2,1)} %get-tuple-element.23), calls=%async_computation | async-start | bytes 1572864 | tf_op jit(solution)/shard_map/all_to_all | solution.py:419
  13.7 0.0 copy-start.13
  13.7 0.7 %copy-done.13 = f32[8,128]{1,0:T(8,128)S(1)} copy-done((f32[8,128]{1,0:T(8,128)S(1)}, f32[8,128]{1,0:T(8,128)}, u32[]{:S(2)}) %copy-start.13) | copy-done | bytes 4120
  14.4 0.7 %stage.1 = (f32[1,512]{1,0:T(1,128)S(1)}, f32[2,512]{1,0:T(2,128)S(1)}, bf16[16,8,512]{2,1,0:T(8,128)(2,1)S(1)}, bf16[16,8,512]{2,1,0:T(8,128)(2,1)S(1)}) custom-call(f32[8,128]{1,0:T(8,128)S(1)} %copy-done.13, s32[1]{0:T(128)S(6)} %copy.18.pitch_at, f32[2,8]{1,0:T(2,128)S(1)} %copy-done.7, bf16[64,512]{1,0:T(8,128)(2,1)S(1)} %copy-done.4, ...), custom_call_target="tpu_custom_call" | custom-call | flops 1000000000 | bytes 3000000 | tf_op jit(solution)/shard_map/stage/pallas_call | solution.py:170
  15.1 3.0 %collective-permute-start.2 = (bf16[16,8,512]{2,1,0:T(8,128)(2,1)S(1)}, bf16[16,8,512]{2,1,0:T(8,128)(2,1)S(1)}, u32[]{:S(2)}, u32[]{:S(2)}) collective-permute-start(bf16[16,8,512]{2,1,0:T(8,128)(2,1)S(1)} %get-tuple-element.28), channel_id=1, source_target_pairs={{0,1},{1,0},{2,3},{3,2},{4,5},{5,4},{6,7},{7,6},{8,9},{9,8},{10,11... | collective-permute-start | bytes 393224 | tf_op jit(solution)/shard_map/ppermute | solution.py:394
  18.1 3.1 %collective-permute-start.3 = (bf16[16,8,512]{2,1,0:T(8,128)(2,1)S(1)}, bf16[16,8,512]{2,1,0:T(8,128)(2,1)S(1)}, u32[]{:S(2)}, u32[]{:S(2)}) collective-permute-start(bf16[16,8,512]{2,1,0:T(8,128)(2,1)S(1)} %get-tuple-element.29), channel_id=1, source_target_pairs={{1,2},{2,1},{3,4},{4,3},{5,6},{6,5},{9,10},{10,9},{11,12},{12,11},... | collective-permute-start | bytes 393224 | tf_op jit(solution)/shard_map/ppermute | solution.py:394
  21.2 7.4 %all-to-all-done.block = bf16[128,24,128]{2,1,0:T(8,128)(2,1)S(1)} async-done(((bf16[128,24,128]{2,1,0:T(8,128)(2,1)}), bf16[128,24,128]{2,1,0:T(8,128)(2,1)S(1)}, u32[]{:S(2)}, u32[]{:S(2)}) %all-to-all-start) | async-done | bytes 786464 | tf_op jit(solution)/shard_map/all_to_all | solution.py:419
  28.6 0.4 cell_sums.1
  29.0 0.0 copy-start
  29.1 0.0 copy-start.8
  29.1 0.0 copy-start.9
  29.1 0.0 copy-start.11
  29.1 1.8 %collective-permute-start = (bf16[16,8,128]{2,1,0:T(8,128)(2,1)S(1)}, bf16[16,8,128]{2,1,0:T(8,128)(2,1)S(1)}, u32[]{:S(2)}, u32[]{:S(2)}) collective-permute-start(bf16[16,8,128]{2,1,0:T(8,128)(2,1)S(1)} %get-tuple-element.25), channel_id=1, source_target_pairs={{0,1},{1,0},{2,3},{3,2},{4,5},{5,4},{6,7},{7,6},{8,9},{9,8},{10,11... | collective-permute-start | bytes 98312 | tf_op jit(solution)/shard_map/ppermute | solution.py:394
  30.9 4.5 %collective-permute-start.1 = (bf16[16,8,128]{2,1,0:T(8,128)(2,1)S(1)}, bf16[16,8,128]{2,1,0:T(8,128)(2,1)S(1)}, u32[]{:S(2)}, u32[]{:S(2)}) collective-permute-start(bf16[16,8,128]{2,1,0:T(8,128)(2,1)S(1)} %get-tuple-element.26), channel_id=1, source_target_pairs={{1,2},{2,1},{3,4},{4,3},{5,6},{6,5},{9,10},{10,9},{11,12},{12,11},... | collective-permute-start | bytes 98312 | tf_op jit(solution)/shard_map/ppermute | solution.py:394
  35.5 3.6 %collective-permute-done.1.feat_b = bf16[16,8,128]{2,1,0:T(8,128)(2,1)S(1)} collective-permute-done((bf16[16,8,128]{2,1,0:T(8,128)(2,1)S(1)}, bf16[16,8,128]{2,1,0:T(8,128)(2,1)S(1)}, u32[]{:S(2)}, u32[]{:S(2)}) %collective-permute-start.1) | collective-permute-done | bytes 32800 | tf_op jit(solution)/shard_map/ppermute | solution.py:394
  39.1 0.3 band.1
  39.4 0.1 collective-permute-start.4
  39.4 3.8 %collective-permute-start.5 = (bf16[8,32,512]{2,1,0:T(8,128)(2,1)S(1)}, bf16[8,32,512]{2,1,0:T(8,128)(2,1)S(1)}, u32[]{:S(2)}, u32[]{:S(2)}) collective-permute-start(bf16[8,32,512]{2,1,0:T(8,128)(2,1)S(1)} %get-tuple-element.32.first), channel_id=1, source_target_pairs={{0,120},{8,0},{16,8},{24,16},{32,24},{40,32},{48,40},{56,48},{64,5... | collective-permute-start | bytes 786440 | tf_op jit(solution)/shard_map/ppermute | solution.py:399
  43.3 0.0 copy-start.10
  43.3 0.0 copy-start.12
  43.4 3.4 %inner.1 = (bf16[384,512]{1,0:T(8,128)(2,1)S(1)}, bf16[512,512]{1,0:T(8,128)(2,1)S(1)}, bf16[512,512]{1,0:T(8,128)(2,1)S(1)}, bf16[192,512]{1,0:T(8,128)(2,1)S(1...) custom-call(bf16[8,32,512]{2,1,0:T(8,128)(2,1)S(1)} %get-tuple-element.32.first, ...), custom_call_target="tpu_custom_call" | custom-call | flops 4000000000 | bytes 12000000 | tf_op jit(solution)/shard_map/inner/pallas_call | solution.py:308
  46.7 0.6 %collective-permute-done.4.low = bf16[8,32,512]{2,1,0:T(8,128)(2,1)S(1)} collective-permute-done((bf16[8,32,512]{2,1,0:T(8,128)(2,1)S(1)}, bf16[8,32,512]{2,1,0:T(8,128)(2,1)S(1)}, u32[]{:S(2)}, u32[]{:S(2)}) %collective-permute-start.4) | collective-permute-done | bytes 262176 | tf_op jit(solution)/shard_map/ppermute | solution.py:399
  47.4 7.0 %outer.1 = bf16[16,16,512]{2,1,0:T(8,128)(2,1)} custom-call(bf16[8,32,512]{2,1,0:T(8,128)(2,1)S(1)} %collective-permute-done.4.low, bf16[8,32,512]{2,1,0:T(8,128)(2,1)S(1)} %collective-permute-done.5.high, bf16[8,32,512]{2,1,0:T(8,128)(2,1)S(1)} %get-tuple-element.32.first, bf16[8,32,512]{2,1,0:T(8,128)(2,1)S(1)} %get-tuple-element.31.second, ...), custom_call_target="tpu_custom_call" | custom-call | flops 8000000000 | bytes 24000000 | tf_op jit(solution)/shard_map/outer/pallas_call | solution.py:381
  (24 shorter events, 0.1 us)
Async XLA Ops:
  0.0 13.7 %copy-start.2 = (bf16[1,16,16,512]{3,2,1,0:T(8,128)(2,1)S(1)}, bf16[1,16,16,512]{3,2,1,0:T(8,128)(2,1)}, u32[]{:S(2)}) copy-start(bf16[1,16,16,512]{3,2,1,0:T(8,128)(2,1)} %param.17) | copy-start | bytes 786436
  0.0 13.7 %copy-start.4 = (bf16[64,512]{1,0:T(8,128)(2,1)S(1)}, bf16[64,512]{1,0:T(8,128)(2,1)}, u32[]{:S(2)}) copy-start(bf16[64,512]{1,0:T(8,128)(2,1)} %lookup.1) | copy-start | bytes 196612
  0.0 13.7 %copy-start.7 = (f32[2,8]{1,0:T(2,128)S(1)}, f32[2,8]{1,0:T(2,128)}, u32[]{:S(2)}) copy-start(f32[2,8]{1,0:T(2,128)} %sharp.1) | copy-start | bytes 196
  2.6 26.0 %all-to-all-start = ((bf16[128,24,128]{2,1,0:T(8,128)(2,1)}), bf16[128,24,128]{2,1,0:T(8,128)(2,1)S(1)}, u32[]{:S(2)}, u32[]{:S(2)}) async-start(bf16[128,24,128]{2,1,0:T(8,128)(2,1)} %get-tuple-element.23), calls=%async_computation | async-start | bytes 1572864 | tf_op jit(solution)/shard_map/all_to_all | solution.py:419
  13.7 0.7 %copy-start.13 = (f32[8,128]{1,0:T(8,128)S(1)}, f32[8,128]{1,0:T(8,128)}, u32[]{:S(2)}) copy-start(f32[8,128]{1,0:T(8,128)} %get-tuple-element.27.token) | copy-start | bytes 12292
  15.1 20.4 %collective-permute-start.2 = (bf16[16,8,512]{2,1,0:T(8,128)(2,1)S(1)}, bf16[16,8,512]{2,1,0:T(8,128)(2,1)S(1)}, u32[]{:S(2)}, u32[]{:S(2)}) collective-permute-start(bf16[16,8,512]{2,1,0:T(8,128)(2,1)S(1)} %get-tuple-element.28), channel_id=1, source_target_pairs={{0,1},{1,0},{2,3},{3,2},{4,5},{5,4},{6,7},{7,6},{8,9},{9,8},{10,11... | collective-permute-start | bytes 393224 | tf_op jit(solution)/shard_map/ppermute | solution.py:394
  18.1 21.0 %copy-start.3 = (bf16[128,512]{1,0:T(8,128)(2,1)S(1)}, bf16[128,512]{1,0:T(8,128)(2,1)}, u32[]{:S(2)}) copy-start(bf16[128,512]{1,0:T(8,128)(2,1)} %w_map.1) | copy-start | bytes 393220
  18.1 17.3 %collective-permute-start.3 = (bf16[16,8,512]{2,1,0:T(8,128)(2,1)S(1)}, bf16[16,8,512]{2,1,0:T(8,128)(2,1)S(1)}, u32[]{:S(2)}, u32[]{:S(2)}) collective-permute-start(bf16[16,8,512]{2,1,0:T(8,128)(2,1)S(1)} %get-tuple-element.29), channel_id=1, source_target_pairs={{1,2},{2,1},{3,4},{4,3},{5,6},{6,5},{9,10},{10,9},{11,12},{12,11},... | collective-permute-start | bytes 393224 | tf_op jit(solution)/shard_map/ppermute | solution.py:394
  29.0 14.3 %copy-start = (bf16[2,512,1536]{2,1,0:T(8,128)(2,1)S(1)}, bf16[2,512,1536]{2,1,0:T(8,128)(2,1)}, u32[]{:S(2)}) copy-start(bf16[2,512,1536]{2,1,0:T(8,128)(2,1)} %w_qkv.3) | copy-start | bytes 9437188
  29.0 14.3 %copy-start.1 = (bf16[2,512,512]{2,1,0:T(8,128)(2,1)S(1)}, bf16[2,512,512]{2,1,0:T(8,128)(2,1)}, u32[]{:S(2)}) copy-start(bf16[2,512,512]{2,1,0:T(8,128)(2,1)} %w_out.3) | copy-start | bytes 3145732
  29.0 14.3 %copy-start.5 = (f32[2,512]{1,0:T(2,128)S(1)}, f32[2,512]{1,0:T(2,128)}, u32[]{:S(2)}) copy-start(f32[2,512]{1,0:T(2,128)} %gains.3) | copy-start | bytes 12292
  29.1 14.2 %copy-start.8 = (bf16[1024,128]{1,0:T(8,128)(2,1)S(1)}, bf16[1024,128]{1,0:T(8,128)(2,1)}, u32[]{:S(2)}) copy-start(bf16[1024,128]{1,0:T(8,128)(2,1)} %constant.12.clone.k_aug) | copy-start | bytes 786436
  29.1 14.2 %copy-start.9 = (bf16[576,128]{1,0:T(8,128)(2,1)S(1)}, bf16[576,128]{1,0:T(8,128)(2,1)}, u32[]{:S(2)}) copy-start(bf16[576,128]{1,0:T(8,128)(2,1)} %constant.11.clone.q_aug) | copy-start | bytes 442372
  29.1 14.2 %copy-start.11 = (bf16[256,256]{1,0:T(8,128)(2,1)S(1)}, bf16[256,256]{1,0:T(8,128)(2,1)}, u32[]{:S(2)}) copy-start(bf16[256,256]{1,0:T(8,128)(2,1)} %constant.10.clone.block_ones) | copy-start | bytes 393220
  29.1 6.4 %collective-permute-start = (bf16[16,8,128]{2,1,0:T(8,128)(2,1)S(1)}, bf16[16,8,128]{2,1,0:T(8,128)(2,1)S(1)}, u32[]{:S(2)}, u32[]{:S(2)}) collective-permute-start(bf16[16,8,128]{2,1,0:T(8,128)(2,1)S(1)} %get-tuple-element.25), channel_id=1, source_target_pairs={{0,1},{1,0},{2,3},{3,2},{4,5},{5,4},{6,7},{7,6},{8,9},{9,8},{10,11... | collective-permute-start | bytes 98312 | tf_op jit(solution)/shard_map/ppermute | solution.py:394
  30.9 8.2 %collective-permute-start.1 = (bf16[16,8,128]{2,1,0:T(8,128)(2,1)S(1)}, bf16[16,8,128]{2,1,0:T(8,128)(2,1)S(1)}, u32[]{:S(2)}, u32[]{:S(2)}) collective-permute-start(bf16[16,8,128]{2,1,0:T(8,128)(2,1)S(1)} %get-tuple-element.26), channel_id=1, source_target_pairs={{1,2},{2,1},{3,4},{4,3},{5,6},{6,5},{9,10},{10,9},{11,12},{12,11},... | collective-permute-start | bytes 98312 | tf_op jit(solution)/shard_map/ppermute | solution.py:394
  39.4 8.0 %collective-permute-start.4 = (bf16[8,32,512]{2,1,0:T(8,128)(2,1)S(1)}, bf16[8,32,512]{2,1,0:T(8,128)(2,1)S(1)}, u32[]{:S(2)}, u32[]{:S(2)}) collective-permute-start(bf16[8,32,512]{2,1,0:T(8,128)(2,1)S(1)} %get-tuple-element.31.second), channel_id=1, source_target_pairs={{0,8},{8,16},{16,24},{24,32},{32,40},{40,48},{48,56},{56,64},{64,7... | collective-permute-start | bytes 786440 | tf_op jit(solution)/shard_map/ppermute | solution.py:399
  39.4 7.9 %collective-permute-start.5 = (bf16[8,32,512]{2,1,0:T(8,128)(2,1)S(1)}, bf16[8,32,512]{2,1,0:T(8,128)(2,1)S(1)}, u32[]{:S(2)}, u32[]{:S(2)}) collective-permute-start(bf16[8,32,512]{2,1,0:T(8,128)(2,1)S(1)} %get-tuple-element.32.first), channel_id=1, source_target_pairs={{0,120},{8,0},{16,8},{24,16},{32,24},{40,32},{48,40},{56,48},{64,5... | collective-permute-start | bytes 786440 | tf_op jit(solution)/shard_map/ppermute | solution.py:399
  43.3 4.0 %copy-start.6 = (f32[512]{0:T(512)S(1)}, f32[512]{0:T(512)}, u32[]{:S(2)}) copy-start(f32[512]{0:T(512)} %param.28) | copy-start | bytes 6148
  43.3 4.0 %copy-start.10 = (bf16[576,128]{1,0:T(8,128)(2,1)S(1)}, bf16[576,128]{1,0:T(8,128)(2,1)}, u32[]{:S(2)}) copy-start(bf16[576,128]{1,0:T(8,128)(2,1)} %constant.14.clone.k_aug_1) | copy-start | bytes 442372
  43.3 4.0 %copy-start.12 = (bf16[256,128]{1,0:T(8,128)(2,1)S(1)}, bf16[256,128]{1,0:T(8,128)(2,1)}, u32[]{:S(2)}) copy-start(bf16[256,128]{1,0:T(8,128)(2,1)} %constant.13.clone.q_aug_1) | copy-start | bytes 196612

commit v2 on v1

--- a/solution.py
+++ b/solution.py
@@ -91,55 +91,55 @@
         yield from task
 
 
-def pack_kernel(rows, cells, tally, packed, token, block, cells_here, tally_here, sems, out_sems):
-    parts = [pl.ds(32 * i, 32) for i in range(4)]
-    loads = [pltpu.make_async_copy(rows.at[at], block.at[at, 0:16, :], sems.at[i]) for i, at in enumerate(parts)]
-    ids_load = pltpu.make_async_copy(cells, cells_here, sems.at[4])
-    tally_load = pltpu.make_async_copy(tally, tally_here, sems.at[5])
+def pack_kernel(rows, cells, tally, packed, token, block, cells_here, tally_here, sems, out_sem):
+    ids_load = pltpu.make_async_copy(cells, cells_here, sems.at[8])
+    tally_load = pltpu.make_async_copy(tally, tally_here, sems.at[9])
     ids_load.start()
     tally_load.start()
+    loads = [
+        pltpu.make_async_copy(rows.at[:, k], block.at[:, :, pl.ds(128 * k, 128)], sems.at[k]) for k in range(8)
+    ]
     for load in loads:
         load.start()
-    k = lax.broadcasted_iota(jnp.int32, (16, 128), 0)
-    t = lax.broadcasted_iota(jnp.int32, (16, 128), 1)
-    a = lax.broadcasted_iota(jnp.int32, (128, 128), 0)
-    b = lax.broadcasted_iota(jnp.int32, (128, 128), 1)
-    pick = jnp.where(lax.rem(a, 8) == b // 16, 1.0, 0.0).astype(jnp.bfloat16)
+    t = lax.broadcasted_iota(jnp.int32, (128, 128), 0)
+    lane = lax.broadcasted_iota(jnp.int32, (128, 128), 1)
+    mine = t % 8 == lane // 16
+    slot = lane % 16
+    pick = jnp.where(mine, 1.0, 0.0).astype(jnp.bfloat16)
     r = lax.axis_index("rad")
-    mine = t // 16 == r
+    order = (lane // 16 == t % 16 // 2) & (lane % 16 == 2 * r + t % 2)
+    order = jnp.where(order, 1.0, 0.0).astype(jnp.bfloat16)
     ids_load.wait()
     tally_load.wait()
-    spread = jnp.where(t // 8 == k, tally_here[...].astype(jnp.float32), 0.0).astype(jnp.bfloat16)
-    live = lax.rem(t, 16).astype(jnp.float32) < dot(spread, pick)
+    here = lax.broadcasted_iota(jnp.int32, (16, 128), 1) // 8 == lax.broadcasted_iota(jnp.int32, (16, 128), 0)
+    spread = jnp.where(here, tally_here[...].astype(jnp.float32), 0.0).astype(jnp.bfloat16)
+    live = slot[:16].astype(jnp.float32) < dot(spread, pick)
     ids = jnp.where(live, cells_here[...].astype(jnp.float32), float(DEAD))
-    turned = [jnp.where(mine, pltpu.roll(ids, lax.rem(r - b + 8, 8) * 16, 1), 0.0) for b in range(8)]
-    stores = []
-    for i, at in enumerate(parts):
-        for k in range(4 * i, 4 * i + 4):
-            for b in range(8):
-                row = jnp.broadcast_to(turned[b][k : k + 1], (8, 128))
-                block[8 * k + b, 16:24, :] = row.astype(jnp.bfloat16)
-        loads[i].wait()
-        stores.append(pltpu.make_async_copy(block.at[at], packed.at[at], out_sems.at[i]))
-        stores[-1].start()
+    ids = jnp.broadcast_to(ids[:, None, :], (16, 8, 128)).reshape(128, 128)
+    ids = dot(jnp.where(mine, ids, 0.0).astype(jnp.bfloat16), order)
+    for at in range(128):
+        block[at, :, 1024:1152] = jnp.broadcast_to(ids[at : at + 1], (2, 128)).astype(jnp.bfloat16)
+    for load in loads:
+        load.wait()
+    store = pltpu.make_async_copy(block, packed, out_sem)
+    store.start()
     token[...] = jnp.zeros((8, 128), jnp.float32)
-    for store in stores:
-        store.wait()
+    store.wait()
 
 
 def pack(rows, cells, tally):
     return call(
         pack_kernel,
         "pack",
-        [(128, 24, 128), jax.ShapeDtypeStruct((8, 128), jnp.float32)],
+        [(128, 2, 1152), jax.ShapeDtypeStruct((8, 128), jnp.float32)],
         [HBM] * 3,
         [HBM, VMEM],
         [
-            pltpu.VMEM((128, 24, 128), jnp.bfloat16),
+            pltpu.VMEM((128, 2, 1152), jnp.bfloat16),
             pltpu.VMEM((16, 128), jnp.int32),
             pltpu.VMEM((1, 128), jnp.int32),
-            pltpu.SemaphoreType.DMA((6,)),
-            pltpu.SemaphoreType.DMA((4,)),
+            pltpu.SemaphoreType.DMA((10,)),
+            pltpu.SemaphoreType.DMA,
         ],
         mib=60,
     )(rows, cells, tally)
@@ -173,14 +173,15 @@
 def cell_sum_kernel(block, feat, send_a, send_b):
     cell = lax.broadcasted_iota(jnp.int32, (256, 128), 0).astype(jnp.float32)
     total = jnp.zeros((256, 128), jnp.float32)
+    ids = jnp.sum(block[:, :, 1024:1152].astype(jnp.float32).reshape(16, 8, 2, 128), axis=1)
     for step in range(4):
-        here = slice(step * 32, step * 32 + 32)
-        ids = jnp.sum(block[here, 16:24, :].astype(jnp.float32).reshape(4, 8, 8, 128), axis=1)
         picks = []
-        for part in range(4):
-            wide = jnp.broadcast_to(ids[part][None], (32, 8, 128)).reshape(256, 128)
+        rows = []
+        for part in range(4 * step, 4 * step + 4):
+            wide = jnp.broadcast_to(ids[part, 0:1], (256, 128))
             picks.append(jnp.where(wide == cell, 1.0, 0.0).astype(jnp.bfloat16))
-        total = total + dot(jnp.concatenate(picks, axis=1), block[here, 0:16, :].reshape(512, 128))
+            rows += [block[8 * part : 8 * part + 8, :, 128 * k : 128 * k + 128].reshape(16, 128) for k in range(8)]
+        total = total + dot(jnp.concatenate(picks, axis=1), jnp.concatenate(rows, axis=0))
     total = rounded(total).reshape(16, 16, 128)
     feat[...] = total.astype(jnp.bfloat16)
     even = lax.rem(lax.axis_index("rad"), 2) == 0
@@ -414,7 +415,7 @@
     terminal_rescale_factor,
 ):
     packed, token = pack(
-        mesh_portion_descriptors.reshape(128, 16, 128), mesh_entry_site.reshape(16, 128), mesh_portion_tally
+        mesh_portion_descriptors.reshape(128, 8, 2, 128), mesh_entry_site.reshape(16, 128), mesh_portion_tally
     )
     arrived = lax.all_to_all(packed, ("az", "rad"), split_axis=0, concat_axis=0, tiled=True)
 

time: 54.6 us -> 52.9 us (0.969)
  waiting for transfers between devices: 11.6 us -> 9.56 us
    all_to_all x1, waiting for transfers between devices: 7.38 us -> 5.56 us  [per_device(): lax.all_to_all(packed, ('az', 'rad'), split_axis=0, concat_axis=0, tiled=...]
  transfers between devices with their start and end apart: 7 -> 7, of which waited for: 3 -> 3; matrix products, arithmetic and copies ran while one was open for 0% -> 0% of each run, Pallas kernels for 8% -> 9%
where the time goes in v2:
time: 52.9 us; the launch traced here: 52.6 us
  starting transfers between devices  26.8 us (51%)
  Pallas kernels  14.6 us (28%)
  waiting for transfers between devices  9.56 us (18%)
  between operations  0.87 us (2%)
  local copies, waits for them, and re-layouts  0.76 us (1%)
    ppermute x4, starting transfers between devices, swap(): return lax.ppermute(x, 'rad', [(i, j) for i, j in pairs if 0 <= j < count])  12.5 us
    all_to_all x1, starting transfers between devices, per_device(): lax.all_to_all(packed, ('az', 'rad'), split_axis=0, concat_axis=0, tiled=...  10.5 us
    pallas_call x1, Pallas kernels, outer(): call(outer_kernel, 'outer', [(16, 16, WIDTH)], [VMEM] * 21, scratch=[pltp...  6.98 us
    all_to_all x1, waiting for transfers between devices, per_device(): lax.all_to_all(packed, ('az', 'rad'), split_axis=0, concat_axis=0, tiled=...  5.56 us
    ppermute x2, starting transfers between devices, pass_on(): lax.ppermute(x, 'az', [(i, (i + step) % count) for i in range(count)])  3.92 us
    ppermute x4, waiting for transfers between devices, swap(): return lax.ppermute(x, 'rad', [(i, j) for i, j in pairs if 0 <= j < count])  3.4 us
    pallas_call x1, Pallas kernels, inner(): call(inner_kernel, 'inner', outs, [VMEM] * 9, scratch=scratch, mib=14)  3.37 us
    pallas_call x1, Pallas kernels, pack(): call(pack_kernel, 'pack', [(128, 2, 1152), jax.ShapeDtypeStruct((8, 128),...  2.68 us
  transfers between devices with their start and end apart: 7, of which 3 were waited for; matrix products, arithmetic and copies ran while one was open for 0% of the time, Pallas kernels for 9%

profile of v2, /device:TPU:8, one launch (start us, length us, event | category | flops | bytes accessed | tf_op | source)
XLA Modules:
  0.0 52.6 jit_solution(5589995976290843835)
XLA Ops:
  0.0 2.7 %pack.1 = (bf16[128,2,1152]{2,1,0:T(2,128)(2,1)}, f32[8,128]{1,0:T(8,128)}) custom-call(bf16[128,8,2,128]{3,2,1,0:T(2,128)(2,1)} %bitcast.8, s32[16,128]{1,0:T(8,128)} %bitcast.9, s32[1,128]{1,0:T(1,128)} %tally.1), custom_call_target="tpu_custom_call" | custom-call | flops 1500000000 | bytes 4500000 | tf_op jit(solution)/shard_map/pack/pallas_call | solution.py:131
  2.7 10.5 %all-to-all-start = ((bf16[128,2,1152]{2,1,0:T(2,128)(2,1)}), bf16[128,2,1152]{2,1,0:T(2,128)(2,1)S(1)}, u32[]{:S(2)}, u32[]{:S(2)}) async-start(bf16[128,2,1152]{2,1,0:T(2,128)(2,1)} %get-tuple-element.23), calls=%async_computation | async-start | bytes 1179648 | tf_op jit(solution)/shard_map/all_to_all | solution.py:420
  13.8 0.0 copy-start.13
  13.8 0.7 %copy-done.13 = f32[8,128]{1,0:T(8,128)S(1)} copy-done((f32[8,128]{1,0:T(8,128)S(1)}, f32[8,128]{1,0:T(8,128)}, u32[]{:S(2)}) %copy-start.13) | copy-done | bytes 4120
  14.5 0.7 %stage.1 = (f32[1,512]{1,0:T(1,128)S(1)}, f32[2,512]{1,0:T(2,128)S(1)}, bf16[16,8,512]{2,1,0:T(8,128)(2,1)S(1)}, bf16[16,8,512]{2,1,0:T(8,128)(2,1)S(1)}) custom-call(f32[8,128]{1,0:T(8,128)S(1)} %copy-done.13, s32[1]{0:T(128)S(6)} %copy.18.pitch_at, f32[2,8]{1,0:T(2,128)S(1)} %copy-done.7, bf16[64,512]{1,0:T(8,128)(2,1)S(1)} %copy-done.4, ...), custom_call_target="tpu_custom_call" | custom-call | flops 1000000000 | bytes 3000000 | tf_op jit(solution)/shard_map/stage/pallas_call | solution.py:170
  15.2 3.0 %collective-permute-start.2 = (bf16[16,8,512]{2,1,0:T(8,128)(2,1)S(1)}, bf16[16,8,512]{2,1,0:T(8,128)(2,1)S(1)}, u32[]{:S(2)}, u32[]{:S(2)}) collective-permute-start(bf16[16,8,512]{2,1,0:T(8,128)(2,1)S(1)} %get-tuple-element.28), channel_id=1, source_target_pairs={{0,1},{1,0},{2,3},{3,2},{4,5},{5,4},{6,7},{7,6},{8,9},{9,8},{10,11... | collective-permute-start | bytes 393224 | tf_op jit(solution)/shard_map/ppermute | solution.py:395
  18.2 3.1 %collective-permute-start.3 = (bf16[16,8,512]{2,1,0:T(8,128)(2,1)S(1)}, bf16[16,8,512]{2,1,0:T(8,128)(2,1)S(1)}, u32[]{:S(2)}, u32[]{:S(2)}) collective-permute-start(bf16[16,8,512]{2,1,0:T(8,128)(2,1)S(1)} %get-tuple-element.29), channel_id=1, source_target_pairs={{1,2},{2,1},{3,4},{4,3},{5,6},{6,5},{9,10},{10,9},{11,12},{12,11},... | collective-permute-start | bytes 393224 | tf_op jit(solution)/shard_map/ppermute | solution.py:395
  21.3 5.6 %all-to-all-done.block = bf16[128,2,1152]{2,1,0:T(2,128)(2,1)S(1)} async-done(((bf16[128,2,1152]{2,1,0:T(2,128)(2,1)}), bf16[128,2,1152]{2,1,0:T(2,128)(2,1)S(1)}, u32[]{:S(2)}, u32[]{:S(2)}) %all-to-all-start) | async-done | bytes 589856 | tf_op jit(solution)/shard_map/all_to_all | solution.py:420
  26.9 0.6 %cell_sums.1 = (bf16[16,16,128]{2,1,0:T(8,128)(2,1)S(1)}, bf16[16,8,128]{2,1,0:T(8,128)(2,1)S(1)}, bf16[16,8,128]{2,1,0:T(8,128)(2,1)S(1)}) custom-call(bf16[128,2,1152]{2,1,0:T(2,128)(2,1)S(1)} %all-to-all-done.block), custom_call_target="tpu_custom_call" | custom-call | flops 2000000000 | bytes 6000000 | tf_op jit(solution)/shard_map/cell_sums/pallas_call | solution.py:195
  27.5 0.0 copy-start.1
  27.5 0.0 copy-start.8
  27.5 0.0 copy-start.9
  27.6 0.0 copy-start.11
  27.6 1.6 %collective-permute-start = (bf16[16,8,128]{2,1,0:T(8,128)(2,1)S(1)}, bf16[16,8,128]{2,1,0:T(8,128)(2,1)S(1)}, u32[]{:S(2)}, u32[]{:S(2)}) collective-permute-start(bf16[16,8,128]{2,1,0:T(8,128)(2,1)S(1)} %get-tuple-element.25), channel_id=1, source_target_pairs={{0,1},{1,0},{2,3},{3,2},{4,5},{5,4},{6,7},{7,6},{8,9},{9,8},{10,11... | collective-permute-start | bytes 98312 | tf_op jit(solution)/shard_map/ppermute | solution.py:395
  29.1 4.8 %collective-permute-start.1 = (bf16[16,8,128]{2,1,0:T(8,128)(2,1)S(1)}, bf16[16,8,128]{2,1,0:T(8,128)(2,1)S(1)}, u32[]{:S(2)}, u32[]{:S(2)}) collective-permute-start(bf16[16,8,128]{2,1,0:T(8,128)(2,1)S(1)} %get-tuple-element.26), channel_id=1, source_target_pairs={{1,2},{2,1},{3,4},{4,3},{5,6},{6,5},{9,10},{10,9},{11,12},{12,11},... | collective-permute-start | bytes 98312 | tf_op jit(solution)/shard_map/ppermute | solution.py:395
  33.9 3.4 %collective-permute-done.1.feat_b = bf16[16,8,128]{2,1,0:T(8,128)(2,1)S(1)} collective-permute-done((bf16[16,8,128]{2,1,0:T(8,128)(2,1)S(1)}, bf16[16,8,128]{2,1,0:T(8,128)(2,1)S(1)}, u32[]{:S(2)}, u32[]{:S(2)}) %collective-permute-start.1) | collective-permute-done | bytes 32800 | tf_op jit(solution)/shard_map/ppermute | solution.py:395
  37.3 0.3 band.1
  37.6 0.1 collective-permute-start.4
  37.7 3.8 %collective-permute-start.5 = (bf16[8,32,512]{2,1,0:T(8,128)(2,1)S(1)}, bf16[8,32,512]{2,1,0:T(8,128)(2,1)S(1)}, u32[]{:S(2)}, u32[]{:S(2)}) collective-permute-start(bf16[8,32,512]{2,1,0:T(8,128)(2,1)S(1)} %get-tuple-element.32.first), channel_id=1, source_target_pairs={{0,120},{8,0},{16,8},{24,16},{32,24},{40,32},{48,40},{56,48},{64,5... | collective-permute-start | bytes 786440 | tf_op jit(solution)/shard_map/ppermute | solution.py:400
  41.6 0.0 copy-start.10
  41.6 0.0 copy-start.12
  41.6 3.4 %inner.1 = (bf16[384,512]{1,0:T(8,128)(2,1)S(1)}, bf16[512,512]{1,0:T(8,128)(2,1)S(1)}, bf16[512,512]{1,0:T(8,128)(2,1)S(1)}, bf16[192,512]{1,0:T(8,128)(2,1)S(1...) custom-call(bf16[8,32,512]{2,1,0:T(8,128)(2,1)S(1)} %get-tuple-element.32.first, ...), custom_call_target="tpu_custom_call" | custom-call | flops 4000000000 | bytes 12000000 | tf_op jit(solution)/shard_map/inner/pallas_call | solution.py:309
  45.0 0.6 %collective-permute-done.4.low = bf16[8,32,512]{2,1,0:T(8,128)(2,1)S(1)} collective-permute-done((bf16[8,32,512]{2,1,0:T(8,128)(2,1)S(1)}, bf16[8,32,512]{2,1,0:T(8,128)(2,1)S(1)}, u32[]{:S(2)}, u32[]{:S(2)}) %collective-permute-start.4) | collective-permute-done | bytes 262176 | tf_op jit(solution)/shard_map/ppermute | solution.py:400
  45.6 7.0 %outer.1 = bf16[16,16,512]{2,1,0:T(8,128)(2,1)} custom-call(bf16[8,32,512]{2,1,0:T(8,128)(2,1)S(1)} %collective-permute-done.4.low, bf16[8,32,512]{2,1,0:T(8,128)(2,1)S(1)} %collective-permute-done.5.high, bf16[8,32,512]{2,1,0:T(8,128)(2,1)S(1)} %get-tuple-element.32.first, bf16[8,32,512]{2,1,0:T(8,128)(2,1)S(1)} %get-tuple-element.31.second, ...), custom_call_target="tpu_custom_call" | custom-call | flops 8000000000 | bytes 24000000 | tf_op jit(solution)/shard_map/outer/pallas_call | solution.py:382
  (24 shorter events, 0.1 us)
Async XLA Ops:
  0.0 13.8 %copy-start.2 = (bf16[1,16,16,512]{3,2,1,0:T(8,128)(2,1)S(1)}, bf16[1,16,16,512]{3,2,1,0:T(8,128)(2,1)}, u32[]{:S(2)}) copy-start(bf16[1,16,16,512]{3,2,1,0:T(8,128)(2,1)} %param.17) | copy-start | bytes 786436
  0.0 13.8 %copy-start.4 = (bf16[64,512]{1,0:T(8,128)(2,1)S(1)}, bf16[64,512]{1,0:T(8,128)(2,1)}, u32[]{:S(2)}) copy-start(bf16[64,512]{1,0:T(8,128)(2,1)} %lookup.1) | copy-start | bytes 196612
  0.0 13.8 %copy-start.7 = (f32[2,8]{1,0:T(2,128)S(1)}, f32[2,8]{1,0:T(2,128)}, u32[]{:S(2)}) copy-start(f32[2,8]{1,0:T(2,128)} %sharp.1) | copy-start | bytes 196
  2.7 24.2 %all-to-all-start = ((bf16[128,2,1152]{2,1,0:T(2,128)(2,1)}), bf16[128,2,1152]{2,1,0:T(2,128)(2,1)S(1)}, u32[]{:S(2)}, u32[]{:S(2)}) async-start(bf16[128,2,1152]{2,1,0:T(2,128)(2,1)} %get-tuple-element.23), calls=%async_computation | async-start | bytes 1179648 | tf_op jit(solution)/shard_map/all_to_all | solution.py:420
  13.8 0.7 %copy-start.13 = (f32[8,128]{1,0:T(8,128)S(1)}, f32[8,128]{1,0:T(8,128)}, u32[]{:S(2)}) copy-start(f32[8,128]{1,0:T(8,128)} %get-tuple-element.27.token) | copy-start | bytes 12292
  15.2 18.7 %collective-permute-start.2 = (bf16[16,8,512]{2,1,0:T(8,128)(2,1)S(1)}, bf16[16,8,512]{2,1,0:T(8,128)(2,1)S(1)}, u32[]{:S(2)}, u32[]{:S(2)}) collective-permute-start(bf16[16,8,512]{2,1,0:T(8,128)(2,1)S(1)} %get-tuple-element.28), channel_id=1, source_target_pairs={{0,1},{1,0},{2,3},{3,2},{4,5},{5,4},{6,7},{7,6},{8,9},{9,8},{10,11... | collective-permute-start | bytes 393224 | tf_op jit(solution)/shard_map/ppermute | solution.py:395
  18.2 19.1 %copy-start.3 = (bf16[128,512]{1,0:T(8,128)(2,1)S(1)}, bf16[128,512]{1,0:T(8,128)(2,1)}, u32[]{:S(2)}) copy-start(bf16[128,512]{1,0:T(8,128)(2,1)} %w_map.1) | copy-start | bytes 393220
  18.2 15.7 %collective-permute-start.3 = (bf16[16,8,512]{2,1,0:T(8,128)(2,1)S(1)}, bf16[16,8,512]{2,1,0:T(8,128)(2,1)S(1)}, u32[]{:S(2)}, u32[]{:S(2)}) collective-permute-start(bf16[16,8,512]{2,1,0:T(8,128)(2,1)S(1)} %get-tuple-element.29), channel_id=1, source_target_pairs={{1,2},{2,1},{3,4},{4,3},{5,6},{6,5},{9,10},{10,9},{11,12},{12,11},... | collective-permute-start | bytes 393224 | tf_op jit(solution)/shard_map/ppermute | solution.py:395
  27.5 14.1 %copy-start = (bf16[2,512,1536]{2,1,0:T(8,128)(2,1)S(1)}, bf16[2,512,1536]{2,1,0:T(8,128)(2,1)}, u32[]{:S(2)}) copy-start(bf16[2,512,1536]{2,1,0:T(8,128)(2,1)} %w_qkv.3) | copy-start | bytes 9437188
  27.5 14.1 %copy-start.1 = (bf16[2,512,512]{2,1,0:T(8,128)(2,1)S(1)}, bf16[2,512,512]{2,1,0:T(8,128)(2,1)}, u32[]{:S(2)}) copy-start(bf16[2,512,512]{2,1,0:T(8,128)(2,1)} %w_out.3) | copy-start | bytes 3145732
  27.5 14.0 %copy-start.5 = (f32[2,512]{1,0:T(2,128)S(1)}, f32[2,512]{1,0:T(2,128)}, u32[]{:S(2)}) copy-start(f32[2,512]{1,0:T(2,128)} %gains.3) | copy-start | bytes 12292
  27.5 14.0 %copy-start.8 = (bf16[1024,128]{1,0:T(8,128)(2,1)S(1)}, bf16[1024,128]{1,0:T(8,128)(2,1)}, u32[]{:S(2)}) copy-start(bf16[1024,128]{1,0:T(8,128)(2,1)} %constant.12.clone.k_aug) | copy-start | bytes 786436
  27.5 14.0 %copy-start.9 = (bf16[576,128]{1,0:T(8,128)(2,1)S(1)}, bf16[576,128]{1,0:T(8,128)(2,1)}, u32[]{:S(2)}) copy-start(bf16[576,128]{1,0:T(8,128)(2,1)} %constant.11.clone.q_aug) | copy-start | bytes 442372
  27.6 14.0 %copy-start.11 = (bf16[256,256]{1,0:T(8,128)(2,1)S(1)}, bf16[256,256]{1,0:T(8,128)(2,1)}, u32[]{:S(2)}) copy-start(bf16[256,256]{1,0:T(8,128)(2,1)} %constant.10.clone.block_ones) | copy-start | bytes 393220
  27.6 6.4 %collective-permute-start = (bf16[16,8,128]{2,1,0:T(8,128)(2,1)S(1)}, bf16[16,8,128]{2,1,0:T(8,128)(2,1)S(1)}, u32[]{:S(2)}, u32[]{:S(2)}) collective-permute-start(bf16[16,8,128]{2,1,0:T(8,128)(2,1)S(1)} %get-tuple-element.25), channel_id=1, source_target_pairs={{0,1},{1,0},{2,3},{3,2},{4,5},{5,4},{6,7},{7,6},{8,9},{9,8},{10,11... | collective-permute-start | bytes 98312 | tf_op jit(solution)/shard_map/ppermute | solution.py:395
  29.1 8.2 %collective-permute-start.1 = (bf16[16,8,128]{2,1,0:T(8,128)(2,1)S(1)}, bf16[16,8,128]{2,1,0:T(8,128)(2,1)S(1)}, u32[]{:S(2)}, u32[]{:S(2)}) collective-permute-start(bf16[16,8,128]{2,1,0:T(8,128)(2,1)S(1)} %get-tuple-element.26), channel_id=1, source_target_pairs={{1,2},{2,1},{3,4},{4,3},{5,6},{6,5},{9,10},{10,9},{11,12},{12,11},... | collective-permute-start | bytes 98312 | tf_op jit(solution)/shard_map/ppermute | solution.py:395
  37.6 8.0 %collective-permute-start.4 = (bf16[8,32,512]{2,1,0:T(8,128)(2,1)S(1)}, bf16[8,32,512]{2,1,0:T(8,128)(2,1)S(1)}, u32[]{:S(2)}, u32[]{:S(2)}) collective-permute-start(bf16[8,32,512]{2,1,0:T(8,128)(2,1)S(1)} %get-tuple-element.31.second), channel_id=1, source_target_pairs={{0,8},{8,16},{16,24},{24,32},{32,40},{40,48},{48,56},{56,64},{64,7... | collective-permute-start | bytes 786440 | tf_op jit(solution)/shard_map/ppermute | solution.py:400
  37.7 7.9 %collective-permute-start.5 = (bf16[8,32,512]{2,1,0:T(8,128)(2,1)S(1)}, bf16[8,32,512]{2,1,0:T(8,128)(2,1)S(1)}, u32[]{:S(2)}, u32[]{:S(2)}) collective-permute-start(bf16[8,32,512]{2,1,0:T(8,128)(2,1)S(1)} %get-tuple-element.32.first), channel_id=1, source_target_pairs={{0,120},{8,0},{16,8},{24,16},{32,24},{40,32},{48,40},{56,48},{64,5... | collective-permute-start | bytes 786440 | tf_op jit(solution)/shard_map/ppermute | solution.py:400
  41.6 4.0 %copy-start.6 = (f32[512]{0:T(512)S(1)}, f32[512]{0:T(512)}, u32[]{:S(2)}) copy-start(f32[512]{0:T(512)} %param.28) | copy-start | bytes 6148
  41.6 4.0 %copy-start.10 = (bf16[576,128]{1,0:T(8,128)(2,1)S(1)}, bf16[576,128]{1,0:T(8,128)(2,1)}, u32[]{:S(2)}) copy-start(bf16[576,128]{1,0:T(8,128)(2,1)} %constant.14.clone.k_aug_1) | copy-start | bytes 442372
  41.6 4.0 %copy-start.12 = (bf16[256,128]{1,0:T(8,128)(2,1)S(1)}, bf16[256,128]{1,0:T(8,128)(2,1)}, u32[]{:S(2)}) copy-start(bf16[256,128]{1,0:T(8,128)(2,1)} %constant.13.clone.q_aug_1) | copy-start | bytes 196612

commit v3 on v2

--- a/solution.py
+++ b/solution.py
@@ -57,7 +57,7 @@
     return x if isinstance(x, jax.ShapeDtypeStruct) else jax.ShapeDtypeStruct(x, jnp.bfloat16)
 
 
-COST = {"pack": 1.5, "stage": 1, "cell_sums": 2, "band": 1.5, "inner": 4, "outer": 8}
+COST = {"pack": 1.5, "stage": 1, "cell_sums": 2, "band": 1, "widen": 1, "inner": 4, "outer": 8}
 
 
 def call(kernel, name, outs, in_specs, out_specs=None, scratch=(), mib=8):
@@ -200,25 +200,44 @@
     )(arrived)
 
 
-def band_kernel(feat, feat_a, feat_b, hid, hid_a, hid_b, pitch, w_map, first, second):
+def widened(own, got_a, got_b):
     even = lax.rem(lax.axis_index("rad"), 2) == 0
-
-    def wide(own, got_a, got_b, at):
-        here = slice(at, at + 8)
-        a = got_a[here].astype(jnp.float32)
-        b = got_b[here].astype(jnp.float32)
-        from_a = (lax.broadcasted_iota(jnp.int32, a.shape, 1) < HALO) == even
-        parts = [own[here].astype(jnp.float32), jnp.where(from_a, a, b), jnp.where(from_a, b, a)]
-        return jnp.concatenate(parts, axis=1).reshape(256, a.shape[-1])
-
-    for at, out in ((0, first), (8, second)):
-        x = dot(wide(feat, feat_a, feat_b, at).astype(jnp.bfloat16), w_map[...])
-        x = wide(hid, hid_a, hid_b, at) + x + pitch[...]
-        out[...] = x.reshape(8, 32, WIDTH).astype(jnp.bfloat16)
+    a = got_a[...].astype(jnp.float32)
+    b = got_b[...].astype(jnp.float32)
+    from_a = (lax.broadcasted_iota(jnp.int32, a.shape, 1) < HALO) == even
+    parts = [own[...].astype(jnp.float32), jnp.where(from_a, a, b), jnp.where(from_a, b, a)]
+    return jnp.concatenate(parts, axis=1)
+
+
+def send_halves(x, to_a, to_b):
+    even = lax.rem(lax.axis_index("az"), 2) == 0
+    to_a[...] = jnp.where(even, x[EDGE:], x[:EDGE]).astype(jnp.bfloat16)
+    to_b[...] = jnp.where(even, x[:EDGE], x[EDGE:]).astype(jnp.bfloat16)
+
+
+def widen_kernel(token, own, got_a, got_b, wide, to_a, to_b):
+    x = widened(own, got_a, got_b)
+    wide[...] = x.astype(jnp.bfloat16)
+    send_halves(x, to_a, to_b)
+
+
+def widen(*arrays):
+    return call(widen_kernel, "widen", [(16, 32, WIDTH)] + [(EDGE, 32, WIDTH)] * 2, [VMEM] * 4)(*arrays)
+
+
+def streamed(feat, hid, pitch, w_map):
+    x = dot(feat.reshape(-1, 128).astype(jnp.bfloat16), w_map[...])
+    return rounded(hid.reshape(-1, WIDTH) + x + pitch[...]).reshape(hid.shape)
+
+
+def band_kernel(feat, feat_b, feat_a, hid, pitch, w_map, stream, to_a, to_b):
+    x = widened(feat, feat_a, feat_b)
+    send_halves(x, to_a, to_b)
+    stream[...] = streamed(x, hid[...].astype(jnp.float32), pitch, w_map).astype(jnp.bfloat16)
 
 
 def band(*arrays):
-    return call(band_kernel, "band", [(EDGE, 32, WIDTH)] * 2, [VMEM] * 8)(*arrays)
+    return call(band_kernel, "band", [(16, 32, WIDTH)] + [(EDGE, 32, 128)] * 2, [VMEM] * 6)(*arrays)
 
 
 def project(w, layer, block, rows, block_ones, target, at, scale=None, plain=False):
@@ -283,10 +302,10 @@
 
 
 def inner_kernel(
-    first, second, scale, gains, w_qkv, w_out, block_ones, q_aug, k_aug,
+    band_stream, scale, gains, w_qkv, w_out, block_ones, q_aug, k_aug,
     queries, keys, values, stream, queries_1, keys_1, values_1, att,
 ):
-    x = jnp.concatenate([first[...], second[...]], axis=0).astype(jnp.float32)
+    x = band_stream[...].astype(jnp.float32)
     normed = norm_rows(x.reshape(512, WIDTH), gains[0:1, :])
     narrow = columns(normed.reshape(16, 32, WIDTH), 0, 16, 24).astype(jnp.bfloat16)
     wide = normed.astype(jnp.bfloat16)
@@ -306,16 +325,23 @@
 def inner(*arrays):
     outs = [(384, WIDTH), (512, WIDTH), (512, WIDTH), (192, WIDTH), (128, WIDTH), (192, WIDTH), (192, WIDTH)]
     scratch = [pltpu.VMEM((192, WIDTH), jnp.bfloat16)]
-    return call(inner_kernel, "inner", outs, [VMEM] * 9, scratch=scratch, mib=14)(*arrays)
+    return call(inner_kernel, "inner", outs, [VMEM] * 8, scratch=scratch, mib=14)(*arrays)
 
 
 def outer_kernel(
-    low, high, first, second, scale, gains, w_qkv, w_out, last_gain, block_ones, q_aug, k_aug, q_aug_1, k_aug_1,
+    feat_b, feat_a, hid_b, hid_a, band_stream, pitch, w_map, scale, gains, w_qkv, w_out, last_gain, block_ones, q_aug, k_aug, q_aug_1, k_aug_1,
     q_mid, k_mid, v_mid, stream_mid, q1_mid, k1_mid, v1_mid,
     out, q_end, k_end, v_end, q1_end, k1_end, v1_end, att_0, att_1,
 ):
     att = (att_0, att_1)
-    x = jnp.concatenate([low[...], high[...]], axis=0).astype(jnp.float32)
+    even = lax.rem(lax.axis_index("az"), 2) == 0
+
+    def low_high(from_a, from_b):
+        a = from_a[...].astype(jnp.float32)
+        b = from_b[...].astype(jnp.float32)
+        return jnp.concatenate([jnp.where(even, b, a), jnp.where(even, a, b)], axis=0)
+
+    x = streamed(low_high(feat_a, feat_b), low_high(hid_a, hid_b), pitch, w_map)
     normed = norm_rows(x.reshape(512, WIDTH), gains[0:1, :])
     narrow = columns(normed.reshape(16, 32, WIDTH), 4, 8, 24).astype(jnp.bfloat16)
     wide = normed.astype(jnp.bfloat16)
@@ -334,8 +360,8 @@
 
     def finish(part):
         at = 4 * (1 - part)
-        ours = first if part == 0 else second
-        before = [columns(x, 4 + 4 * part, 4, 24), columns(ours[...].astype(jnp.float32), 4 * part, 4, 24)]
+        ours = band_stream[12 * part : 12 * part + 4].astype(jnp.float32)
+        before = [columns(x, 4 + 4 * part, 4, 24), columns(ours, 0, 4, 24)]
         y = dot(att[part][...], w_out[0])
         yield
         y = rounded(jnp.concatenate(before if part == 0 else before[::-1], axis=0) + y)
@@ -383,21 +409,18 @@
         outer_kernel,
         "outer",
         [(16, 16, WIDTH)],
-        [VMEM] * 21,
+        [VMEM] * 24,
         scratch=[pltpu.VMEM((rows, WIDTH), jnp.bfloat16) for rows in scratch],
         mib=14,
     )(*arrays)[0]
 
 
-def swap(x, shift):
-    count = lax.axis_size("rad")
+def swap(x, axis, shift):
+    count = lax.axis_size(axis)
     pairs = [(i, ((i + shift) ^ 1) - shift) for i in range(count)]
-    return lax.ppermute(x, "rad", [(i, j) for i, j in pairs if 0 <= j < count])
-
-
-def pass_on(x, step):
-    count = lax.axis_size("az")
-    return lax.ppermute(x, "az", [(i, (i + step) % count) for i in range(count)])
+    if axis == "az":
+        pairs = [(i, j % count) for i, j in pairs]
+    return lax.ppermute(x, axis, [(i, j) for i, j in pairs if 0 <= j < count])
 
 
 def per_device(
@@ -424,17 +447,19 @@
     pitch, scale, to_a, to_b = stage(
         token, incline_grid_position, sharpness_scale, incline_vector_lookup, hidden
     )
-    hid_a, hid_b = swap(to_a, 0), swap(to_b, 1)
+    hid_a, hid_b = swap(to_a, "rad", 0), swap(to_b, "rad", 1)
 
     feat, to_a, to_b = cell_sums(arrived)
-    feat_a, feat_b = swap(to_a, 0), swap(to_b, 1)
-    first, second = band(feat, feat_a, feat_b, hidden, hid_a, hid_b, pitch, mesh_mapping_matrix)
-    low, high = pass_on(second, 1), pass_on(first, -1)
+    feat_a, feat_b = swap(to_a, "rad", 0), swap(to_b, "rad", 1)
+    hid, to_a, to_b = widen(feat, hidden, hid_a, hid_b)
+    hid_b, hid_a = swap(to_b, "az", 1), swap(to_a, "az", 0)
+    stream, to_a, to_b = band(feat, feat_b, feat_a, hid, pitch, mesh_mapping_matrix)
+    feat_b, feat_a = swap(to_b, "az", 1), swap(to_a, "az", 0)
     q_aug, k_aug, q_aug_1, k_aug_1 = window_tables()
     weights = (scale, prefocus_rescale_factor, probe_lock_payload_matrix, final_mapping_matrix)
-    middle = inner(first, second, *weights, block_ones, q_aug, k_aug)
+    middle = inner(stream, *weights, block_ones, q_aug, k_aug)
     out = outer(
-        low, high, first, second, *weights, terminal_rescale_factor[None, :],
+        feat_b, feat_a, hid_b, hid_a, stream, pitch, mesh_mapping_matrix, *weights, terminal_rescale_factor[None, :],
         block_ones, q_aug, k_aug, q_aug_1, k_aug_1, *middle,
     )
     return out[None]

time: 52.9 us -> 51.2 us (0.968)
  starting transfers between devices: 26.8 us -> 24 us
  waiting for transfers between devices: 9.56 us -> 10.2 us
    ppermute x6 -> x8, starting transfers between devices: 16.4 us -> 13.5 us  [swap(): return lax.ppermute(x, axis, [(i, j) for i, j in pairs if 0 <= j < count])]
    ppermute x6 -> x8, waiting for transfers between devices: 4 us -> 4.54 us  [swap(): return lax.ppermute(x, axis, [(i, j) for i, j in pairs if 0 <= j < count])]
    pallas_call x3 -> x4, Pallas kernels: 10.6 us -> 11 us  [the longest x1 7.26 us: outer(): call(outer_kernel, 'outer', [(16, 16, WIDTH)], [VMEM] * 24, scratch=[pltp...]
  transfers between devices with their start and end apart: 7 -> 9, of which waited for: 3 -> 4; matrix products, arithmetic and copies ran while one was open for 0% -> 0% of each run, Pallas kernels for 9% -> 10%
where the time goes in v3:
time: 51.2 us; the launch traced here: 50.8 us
  starting transfers between devices  24 us (47%)
  Pallas kernels  14.9 us (29%)
  waiting for transfers between devices  10.2 us (20%)
  between operations  0.89 us (2%)
  local copies, waits for them, and re-layouts  0.76 us (1%)
    ppermute x8, starting transfers between devices, swap(): return lax.ppermute(x, axis, [(i, j) for i, j in pairs if 0 <= j < count])  13.5 us
    all_to_all x1, starting transfers between devices, per_device(): lax.all_to_all(packed, ('az', 'rad'), split_axis=0, concat_axis=0, tiled=...  10.5 us
    pallas_call x1, Pallas kernels, outer(): call(outer_kernel, 'outer', [(16, 16, WIDTH)], [VMEM] * 24, scratch=[pltp...  7.26 us
    all_to_all x1, waiting for transfers between devices, per_device(): lax.all_to_all(packed, ('az', 'rad'), split_axis=0, concat_axis=0, tiled=...  5.7 us
    ppermute x8, waiting for transfers between devices, swap(): return lax.ppermute(x, axis, [(i, j) for i, j in pairs if 0 <= j < count])  4.54 us
    pallas_call x1, Pallas kernels, inner(): call(inner_kernel, 'inner', outs, [VMEM] * 8, scratch=scratch, mib=14)  3.32 us
    pallas_call x1, Pallas kernels, pack(): call(pack_kernel, 'pack', [(128, 2, 1152), jax.ShapeDtypeStruct((8, 128),...  2.65 us
  transfers between devices with their start and end apart: 9, of which 4 were waited for; matrix products, arithmetic and copies ran while one was open for 0% of the time, Pallas kernels for 10%

profile of v3, /device:TPU:8, one launch (start us, length us, event | category | flops | bytes accessed | tf_op | source)
XLA Modules:
  0.0 50.8 jit_solution(4676393053319821599)
XLA Ops:
  0.0 2.6 %pack.1 = (bf16[128,2,1152]{2,1,0:T(2,128)(2,1)}, f32[8,128]{1,0:T(8,128)}) custom-call(bf16[128,8,2,128]{3,2,1,0:T(2,128)(2,1)} %bitcast.8, s32[16,128]{1,0:T(8,128)} %bitcast.9, s32[1,128]{1,0:T(1,128)} %tally.1), custom_call_target="tpu_custom_call" | custom-call | flops 1500000000 | bytes 4500000 | tf_op jit(solution)/shard_map/pack/pallas_call | solution.py:131
  2.7 10.5 %all-to-all-start = ((bf16[128,2,1152]{2,1,0:T(2,128)(2,1)}), bf16[128,2,1152]{2,1,0:T(2,128)(2,1)S(1)}, u32[]{:S(2)}, u32[]{:S(2)}) async-start(bf16[128,2,1152]{2,1,0:T(2,128)(2,1)} %get-tuple-element.27), calls=%async_computation | async-start | bytes 1179648 | tf_op jit(solution)/shard_map/all_to_all | solution.py:443
  13.8 0.7 %copy-done.13 = f32[8,128]{1,0:T(8,128)S(1)} copy-done((f32[8,128]{1,0:T(8,128)S(1)}, f32[8,128]{1,0:T(8,128)}, u32[]{:S(2)}) %copy-start.13) | copy-done | bytes 4120
  14.5 0.7 %stage.1 = (f32[1,512]{1,0:T(1,128)S(1)}, f32[2,512]{1,0:T(2,128)S(1)}, bf16[16,8,512]{2,1,0:T(8,128)(2,1)S(1)}, bf16[16,8,512]{2,1,0:T(8,128)(2,1)S(1)}) custom-call(f32[8,128]{1,0:T(8,128)S(1)} %copy-done.13, s32[1]{0:T(128)S(6)} %copy.18.pitch_at, f32[2,8]{1,0:T(2,128)S(1)} %copy-done.7, bf16[64,512]{1,0:T(8,128)(2,1)S(1)} %copy-done.4, ...), custom_call_target="tpu_custom_call" | custom-call | flops 1000000000 | bytes 3000000 | tf_op jit(solution)/shard_map/stage/pallas_call | solution.py:170
  15.1 3.0 %collective-permute-start.2 = (bf16[16,8,512]{2,1,0:T(8,128)(2,1)S(1)}, bf16[16,8,512]{2,1,0:T(8,128)(2,1)S(1)}, u32[]{:S(2)}, u32[]{:S(2)}) collective-permute-start(bf16[16,8,512]{2,1,0:T(8,128)(2,1)S(1)} %get-tuple-element.32), channel_id=1, source_target_pairs={{0,1},{1,0},{2,3},{3,2},{4,5},{5,4},{6,7},{7,6},{8,9},{9,8},{10,11... | collective-permute-start | bytes 393224 | tf_op jit(solution)/shard_map/ppermute | solution.py:423
  18.2 3.0 %collective-permute-start.3 = (bf16[16,8,512]{2,1,0:T(8,128)(2,1)S(1)}, bf16[16,8,512]{2,1,0:T(8,128)(2,1)S(1)}, u32[]{:S(2)}, u32[]{:S(2)}) collective-permute-start(bf16[16,8,512]{2,1,0:T(8,128)(2,1)S(1)} %get-tuple-element.33), channel_id=1, source_target_pairs={{1,2},{2,1},{3,4},{4,3},{5,6},{6,5},{9,10},{10,9},{11,12},{12,11},... | collective-permute-start | bytes 393224 | tf_op jit(solution)/shard_map/ppermute | solution.py:423
  21.2 5.7 %all-to-all-done.block = bf16[128,2,1152]{2,1,0:T(2,128)(2,1)S(1)} async-done(((bf16[128,2,1152]{2,1,0:T(2,128)(2,1)}), bf16[128,2,1152]{2,1,0:T(2,128)(2,1)S(1)}, u32[]{:S(2)}, u32[]{:S(2)}) %all-to-all-start) | async-done | bytes 589856 | tf_op jit(solution)/shard_map/all_to_all | solution.py:443
  26.9 0.6 %cell_sums.1 = (bf16[16,16,128]{2,1,0:T(8,128)(2,1)S(1)}, bf16[16,8,128]{2,1,0:T(8,128)(2,1)S(1)}, bf16[16,8,128]{2,1,0:T(8,128)(2,1)S(1)}) custom-call(bf16[128,2,1152]{2,1,0:T(2,128)(2,1)S(1)} %all-to-all-done.block), custom_call_target="tpu_custom_call" | custom-call | flops 2000000000 | bytes 6000000 | tf_op jit(solution)/shard_map/cell_sums/pallas_call | solution.py:195
  27.5 4.4 %collective-permute-start = (bf16[16,8,128]{2,1,0:T(8,128)(2,1)S(1)}, bf16[16,8,128]{2,1,0:T(8,128)(2,1)S(1)}, u32[]{:S(2)}, u32[]{:S(2)}) collective-permute-start(bf16[16,8,128]{2,1,0:T(8,128)(2,1)S(1)} %get-tuple-element.29), channel_id=1, source_target_pairs={{1,2},{2,1},{3,4},{4,3},{5,6},{6,5},{9,10},{10,9},{11,12},{12,11},... | collective-permute-start | bytes 98312 | tf_op jit(solution)/shard_map/ppermute | solution.py:423
  31.8 1.2 %collective-permute-start.1 = (bf16[16,8,128]{2,1,0:T(8,128)(2,1)S(1)}, bf16[16,8,128]{2,1,0:T(8,128)(2,1)S(1)}, u32[]{:S(2)}, u32[]{:S(2)}) collective-permute-start(bf16[16,8,128]{2,1,0:T(8,128)(2,1)S(1)} %get-tuple-element.30), channel_id=1, source_target_pairs={{0,1},{1,0},{2,3},{3,2},{4,5},{5,4},{6,7},{7,6},{8,9},{9,8},{10,11... | collective-permute-start | bytes 98312 | tf_op jit(solution)/shard_map/ppermute | solution.py:423
  33.1 0.0 copy-start.8
  33.1 0.0 copy-start.9
  33.1 0.2 widen.1
  33.3 0.1 collective-permute-start.6
  33.4 0.9 %collective-permute-start.7 = (bf16[8,32,512]{2,1,0:T(8,128)(2,1)S(1)}, bf16[8,32,512]{2,1,0:T(8,128)(2,1)S(1)}, u32[]{:S(2)}, u32[]{:S(2)}) collective-permute-start(bf16[8,32,512]{2,1,0:T(8,128)(2,1)S(1)} %get-tuple-element.39), channel_id=1, source_target_pairs={{0,8},{8,0},{16,24},{24,16},{32,40},{40,32},{48,56},{56,48},{64,72... | collective-permute-start | bytes 786440 | tf_op jit(solution)/shard_map/ppermute | solution.py:423
  34.3 1.5 %collective-permute-done.feat_b = bf16[16,8,128]{2,1,0:T(8,128)(2,1)S(1)} collective-permute-done((bf16[16,8,128]{2,1,0:T(8,128)(2,1)S(1)}, bf16[16,8,128]{2,1,0:T(8,128)(2,1)S(1)}, u32[]{:S(2)}, u32[]{:S(2)}) %collective-permute-start) | collective-permute-done | bytes 32800 | tf_op jit(solution)/shard_map/ppermute | solution.py:423
  35.8 1.5 %collective-permute-done.1.feat_a = bf16[16,8,128]{2,1,0:T(8,128)(2,1)S(1)} collective-permute-done((bf16[16,8,128]{2,1,0:T(8,128)(2,1)S(1)}, bf16[16,8,128]{2,1,0:T(8,128)(2,1)S(1)}, u32[]{:S(2)}, u32[]{:S(2)}) %collective-permute-start.1) | collective-permute-done | bytes 32800 | tf_op jit(solution)/shard_map/ppermute | solution.py:423
  37.3 0.3 band.1
  37.6 0.1 collective-permute-start.4
  37.7 0.9 %collective-permute-start.5 = (bf16[8,32,128]{2,1,0:T(8,128)(2,1)S(1)}, bf16[8,32,128]{2,1,0:T(8,128)(2,1)S(1)}, u32[]{:S(2)}, u32[]{:S(2)}) collective-permute-start(bf16[8,32,128]{2,1,0:T(8,128)(2,1)S(1)} %get-tuple-element.37), channel_id=1, source_target_pairs={{0,8},{8,0},{16,24},{24,16},{32,40},{40,32},{48,56},{56,48},{64,72... | collective-permute-start | bytes 196616 | tf_op jit(solution)/shard_map/ppermute | solution.py:423
  38.6 0.0 copy-start.10
  38.7 3.3 %inner.1 = (bf16[384,512]{1,0:T(8,128)(2,1)S(1)}, bf16[512,512]{1,0:T(8,128)(2,1)S(1)}, bf16[512,512]{1,0:T(8,128)(2,1)S(1)}, bf16[192,512]{1,0:T(8,128)(2,1)S(1...) custom-call(bf16[16,32,512]{2,1,0:T(8,128)(2,1)S(1)} %get-tuple-element.40.band_stream, ...), custom_call_target="tpu_custom_call" | custom-call | flops 4000000000 | bytes 12000000 | tf_op jit(solution)/shard_map/inner/pallas_call | solution.py:328
  42.0 1.5 %collective-permute-done.4.feat_b = bf16[8,32,128]{2,1,0:T(8,128)(2,1)S(1)} collective-permute-done((bf16[8,32,128]{2,1,0:T(8,128)(2,1)S(1)}, bf16[8,32,128]{2,1,0:T(8,128)(2,1)S(1)}, u32[]{:S(2)}, u32[]{:S(2)}) %collective-permute-start.4) | collective-permute-done | bytes 65568 | tf_op jit(solution)/shard_map/ppermute | solution.py:423
  43.5 7.3 %outer.1 = bf16[16,16,512]{2,1,0:T(8,128)(2,1)} custom-call(bf16[8,32,128]{2,1,0:T(8,128)(2,1)S(1)} %collective-permute-done.4.feat_b, bf16[8,32,128]{2,1,0:T(8,128)(2,1)S(1)} %collective-permute-done.5.feat_a, bf16[8,32,512]{2,1,0:T(8,128)(2,1)S(1)} %collective-permute-done.6.hid_b, bf16[8,32,512]{2,1,0:T(8,128)(2,1)S(1)} %collective-permute-done.7.hid_a, ...), custom_call_target="tpu_custom_call" | custom-call | flops 8000000000 | bytes 24000000 | tf_op jit(solution)/shard_map/outer/pallas_call | solution.py:408
  (29 shorter events, 0.1 us)
Async XLA Ops:
  0.0 13.8 %copy-start.2 = (bf16[1,16,16,512]{3,2,1,0:T(8,128)(2,1)S(1)}, bf16[1,16,16,512]{3,2,1,0:T(8,128)(2,1)}, u32[]{:S(2)}) copy-start(bf16[1,16,16,512]{3,2,1,0:T(8,128)(2,1)} %param.17) | copy-start | bytes 786436
  0.0 13.8 %copy-start.4 = (bf16[64,512]{1,0:T(8,128)(2,1)S(1)}, bf16[64,512]{1,0:T(8,128)(2,1)}, u32[]{:S(2)}) copy-start(bf16[64,512]{1,0:T(8,128)(2,1)} %lookup.1) | copy-start | bytes 196612
  0.0 13.8 %copy-start.7 = (f32[2,8]{1,0:T(2,128)S(1)}, f32[2,8]{1,0:T(2,128)}, u32[]{:S(2)}) copy-start(f32[2,8]{1,0:T(2,128)} %sharp.1) | copy-start | bytes 196
  2.7 24.2 %all-to-all-start = ((bf16[128,2,1152]{2,1,0:T(2,128)(2,1)}), bf16[128,2,1152]{2,1,0:T(2,128)(2,1)S(1)}, u32[]{:S(2)}, u32[]{:S(2)}) async-start(bf16[128,2,1152]{2,1,0:T(2,128)(2,1)} %get-tuple-element.27), calls=%async_computation | async-start | bytes 1179648 | tf_op jit(solution)/shard_map/all_to_all | solution.py:443
  13.8 0.7 %copy-start.13 = (f32[8,128]{1,0:T(8,128)S(1)}, f32[8,128]{1,0:T(8,128)}, u32[]{:S(2)}) copy-start(f32[8,128]{1,0:T(8,128)} %get-tuple-element.31.token) | copy-start | bytes 12292
  15.1 17.9 %collective-permute-start.2 = (bf16[16,8,512]{2,1,0:T(8,128)(2,1)S(1)}, bf16[16,8,512]{2,1,0:T(8,128)(2,1)S(1)}, u32[]{:S(2)}, u32[]{:S(2)}) collective-permute-start(bf16[16,8,512]{2,1,0:T(8,128)(2,1)S(1)} %get-tuple-element.32), channel_id=1, source_target_pairs={{0,1},{1,0},{2,3},{3,2},{4,5},{5,4},{6,7},{7,6},{8,9},{9,8},{10,11... | collective-permute-start | bytes 393224 | tf_op jit(solution)/shard_map/ppermute | solution.py:423
  18.2 14.8 %collective-permute-start.3 = (bf16[16,8,512]{2,1,0:T(8,128)(2,1)S(1)}, bf16[16,8,512]{2,1,0:T(8,128)(2,1)S(1)}, u32[]{:S(2)}, u32[]{:S(2)}) collective-permute-start(bf16[16,8,512]{2,1,0:T(8,128)(2,1)S(1)} %get-tuple-element.33), channel_id=1, source_target_pairs={{1,2},{2,1},{3,4},{4,3},{5,6},{6,5},{9,10},{10,9},{11,12},{12,11},... | collective-permute-start | bytes 393224 | tf_op jit(solution)/shard_map/ppermute | solution.py:423
  27.5 9.9 %copy-start.3 = (bf16[128,512]{1,0:T(8,128)(2,1)S(1)}, bf16[128,512]{1,0:T(8,128)(2,1)}, u32[]{:S(2)}) copy-start(bf16[128,512]{1,0:T(8,128)(2,1)} %w_map.3) | copy-start | bytes 393220
  27.5 8.3 %collective-permute-start = (bf16[16,8,128]{2,1,0:T(8,128)(2,1)S(1)}, bf16[16,8,128]{2,1,0:T(8,128)(2,1)S(1)}, u32[]{:S(2)}, u32[]{:S(2)}) collective-permute-start(bf16[16,8,128]{2,1,0:T(8,128)(2,1)S(1)} %get-tuple-element.29), channel_id=1, source_target_pairs={{1,2},{2,1},{3,4},{4,3},{5,6},{6,5},{9,10},{10,9},{11,12},{12,11},... | collective-permute-start | bytes 98312 | tf_op jit(solution)/shard_map/ppermute | solution.py:423
  31.8 5.5 %collective-permute-start.1 = (bf16[16,8,128]{2,1,0:T(8,128)(2,1)S(1)}, bf16[16,8,128]{2,1,0:T(8,128)(2,1)S(1)}, u32[]{:S(2)}, u32[]{:S(2)}) collective-permute-start(bf16[16,8,128]{2,1,0:T(8,128)(2,1)S(1)} %get-tuple-element.30), channel_id=1, source_target_pairs={{0,1},{1,0},{2,3},{3,2},{4,5},{5,4},{6,7},{7,6},{8,9},{9,8},{10,11... | collective-permute-start | bytes 98312 | tf_op jit(solution)/shard_map/ppermute | solution.py:423
  33.0 5.5 %copy-start = (bf16[2,512,1536]{2,1,0:T(8,128)(2,1)S(1)}, bf16[2,512,1536]{2,1,0:T(8,128)(2,1)}, u32[]{:S(2)}) copy-start(bf16[2,512,1536]{2,1,0:T(8,128)(2,1)} %w_qkv.3) | copy-start | bytes 9437188
  33.0 5.5 %copy-start.1 = (bf16[2,512,512]{2,1,0:T(8,128)(2,1)S(1)}, bf16[2,512,512]{2,1,0:T(8,128)(2,1)}, u32[]{:S(2)}) copy-start(bf16[2,512,512]{2,1,0:T(8,128)(2,1)} %w_out.3) | copy-start | bytes 3145732
  33.1 5.5 %copy-start.5 = (f32[2,512]{1,0:T(2,128)S(1)}, f32[2,512]{1,0:T(2,128)}, u32[]{:S(2)}) copy-start(f32[2,512]{1,0:T(2,128)} %gains.3) | copy-start | bytes 12292
  33.1 5.5 %copy-start.8 = (bf16[1024,128]{1,0:T(8,128)(2,1)S(1)}, bf16[1024,128]{1,0:T(8,128)(2,1)}, u32[]{:S(2)}) copy-start(bf16[1024,128]{1,0:T(8,128)(2,1)} %constant.12.clone.k_aug) | copy-start | bytes 786436
  33.1 5.5 %copy-start.9 = (bf16[576,128]{1,0:T(8,128)(2,1)S(1)}, bf16[576,128]{1,0:T(8,128)(2,1)}, u32[]{:S(2)}) copy-start(bf16[576,128]{1,0:T(8,128)(2,1)} %constant.11.clone.q_aug) | copy-start | bytes 442372
  33.1 5.5 %copy-start.11 = (bf16[256,256]{1,0:T(8,128)(2,1)S(1)}, bf16[256,256]{1,0:T(8,128)(2,1)}, u32[]{:S(2)}) copy-start(bf16[256,256]{1,0:T(8,128)(2,1)} %constant.10.clone.block_ones) | copy-start | bytes 393220
  33.3 10.2 %collective-permute-start.6 = (bf16[8,32,512]{2,1,0:T(8,128)(2,1)S(1)}, bf16[8,32,512]{2,1,0:T(8,128)(2,1)S(1)}, u32[]{:S(2)}, u32[]{:S(2)}) collective-permute-start(bf16[8,32,512]{2,1,0:T(8,128)(2,1)S(1)} %get-tuple-element.38), channel_id=1, source_target_pairs={{0,120},{8,16},{16,8},{24,32},{32,24},{40,48},{48,40},{56,64},{64,... | collective-permute-start | bytes 786440 | tf_op jit(solution)/shard_map/ppermute | solution.py:423
  33.4 10.1 %collective-permute-start.7 = (bf16[8,32,512]{2,1,0:T(8,128)(2,1)S(1)}, bf16[8,32,512]{2,1,0:T(8,128)(2,1)S(1)}, u32[]{:S(2)}, u32[]{:S(2)}) collective-permute-start(bf16[8,32,512]{2,1,0:T(8,128)(2,1)S(1)} %get-tuple-element.39), channel_id=1, source_target_pairs={{0,8},{8,0},{16,24},{24,16},{32,40},{40,32},{48,56},{56,48},{64,72... | collective-permute-start | bytes 786440 | tf_op jit(solution)/shard_map/ppermute | solution.py:423
  37.6 5.9 %collective-permute-start.4 = (bf16[8,32,128]{2,1,0:T(8,128)(2,1)S(1)}, bf16[8,32,128]{2,1,0:T(8,128)(2,1)S(1)}, u32[]{:S(2)}, u32[]{:S(2)}) collective-permute-start(bf16[8,32,128]{2,1,0:T(8,128)(2,1)S(1)} %get-tuple-element.36), channel_id=1, source_target_pairs={{0,120},{8,16},{16,8},{24,32},{32,24},{40,48},{48,40},{56,64},{64,... | collective-permute-start | bytes 196616 | tf_op jit(solution)/shard_map/ppermute | solution.py:423
  37.7 5.8 %collective-permute-start.5 = (bf16[8,32,128]{2,1,0:T(8,128)(2,1)S(1)}, bf16[8,32,128]{2,1,0:T(8,128)(2,1)S(1)}, u32[]{:S(2)}, u32[]{:S(2)}) collective-permute-start(bf16[8,32,128]{2,1,0:T(8,128)(2,1)S(1)} %get-tuple-element.37), channel_id=1, source_target_pairs={{0,8},{8,0},{16,24},{24,16},{32,40},{40,32},{48,56},{56,48},{64,72... | collective-permute-start | bytes 196616 | tf_op jit(solution)/shard_map/ppermute | solution.py:423
  38.6 4.9 %copy-start.6 = (f32[512]{0:T(512)S(1)}, f32[512]{0:T(512)}, u32[]{:S(2)}) copy-start(f32[512]{0:T(512)} %param.28) | copy-start | bytes 6148
  38.6 4.9 %copy-start.10 = (bf16[576,128]{1,0:T(8,128)(2,1)S(1)}, bf16[576,128]{1,0:T(8,128)(2,1)}, u32[]{:S(2)}) copy-start(bf16[576,128]{1,0:T(8,128)(2,1)} %constant.14.clone.k_aug_1) | copy-start | bytes 442372
  38.6 4.9 %copy-start.12 = (bf16[256,128]{1,0:T(8,128)(2,1)S(1)}, bf16[256,128]{1,0:T(8,128)(2,1)}, u32[]{:S(2)}) copy-start(bf16[256,128]{1,0:T(8,128)(2,1)} %constant.13.clone.q_aug_1) | copy-start | bytes 196612

commit v4 on v3

--- a/solution.py
+++ b/solution.py
@@ -91,7 +91,7 @@
         yield from task
 
 
-def pack_kernel(rows, cells, tally, packed, token, block, cells_here, tally_here, sems, out_sem):
+def pack_kernel(rows, cells, tally, packed, block, cells_here, tally_here, sems, out_sems):
     ids_load = pltpu.make_async_copy(cells, cells_here, sems.at[8])
     tally_load = pltpu.make_async_copy(tally, tally_here, sems.at[9])
     ids_load.start()
@@ -117,42 +117,44 @@
     ids = jnp.where(live, cells_here[...].astype(jnp.float32), float(DEAD))
     ids = jnp.broadcast_to(ids[:, None, :], (16, 8, 128)).reshape(128, 128)
     ids = dot(jnp.where(mine, ids, 0.0).astype(jnp.bfloat16), order)
+    for load in loads:
+        load.wait()
+    stores = [pltpu.make_async_copy(block.at[:, :, 0:1024], packed.at[:, :, 0:1024], out_sems.at[0])]
+    stores[0].start()
     for at in range(128):
         block[at, :, 1024:1152] = jnp.broadcast_to(ids[at : at + 1], (2, 128)).astype(jnp.bfloat16)
-    for load in loads:
-        load.wait()
-    store = pltpu.make_async_copy(block, packed, out_sem)
-    store.start()
-    token[...] = jnp.zeros((8, 128), jnp.float32)
-    store.wait()
+    stores.append(pltpu.make_async_copy(block.at[:, :, 1024:1152], packed.at[:, :, 1024:1152], out_sems.at[1]))
+    stores[1].start()
+    for store in stores:
+        store.wait()
 
 
 def pack(rows, cells, tally):
     return call(
         pack_kernel,
         "pack",
-        [(128, 2, 1152), jax.ShapeDtypeStruct((8, 128), jnp.float32)],
+        [(128, 2, 1152)],
         [HBM] * 3,
-        [HBM, VMEM],
+        [HBM],
         [
             pltpu.VMEM((128, 2, 1152), jnp.bfloat16),
             pltpu.VMEM((16, 128), jnp.int32),
             pltpu.VMEM((1, 128), jnp.int32),
             pltpu.SemaphoreType.DMA((10,)),
-            pltpu.SemaphoreType.DMA,
+            pltpu.SemaphoreType.DMA((2,)),
         ],
         mib=60,
-    )(rows, cells, tally)
-
-
-def stage_kernel(token, pitch_at, sharp, lookup, hidden, pitch, scale, send_a, send_b):
+    )(rows, cells, tally)[0]
+
+
+def stage_kernel(packed, pitch_at, sharp, lookup, hidden, pitch, scale, send_a, send_b):
     rows = lax.broadcasted_iota(jnp.int32, (64, 1), 0)
     pitch[...] = jnp.sum(
         jnp.where(rows == pitch_at[0], lookup[...].astype(jnp.float32), 0.0), axis=0, keepdims=True
     )
     head = lax.broadcasted_iota(jnp.int32, (1, WIDTH), 1) // 64
     for layer in range(2):
-        line = token[0:1, 0:1] * jnp.ones((1, WIDTH), jnp.float32)
+        line = jnp.zeros((1, WIDTH), jnp.float32)
         for h in range(HEADS):
             line = jnp.where(head == h, sharp[layer, h] * LOG2E, line)
         scale[layer : layer + 1] = line
@@ -167,7 +169,7 @@
     edge = (16, EDGE, WIDTH)
     row = jax.ShapeDtypeStruct((1, WIDTH), jnp.float32)
     two = jax.ShapeDtypeStruct((2, WIDTH), jnp.float32)
-    return call(stage_kernel, "stage", [row, two, edge, edge], [VMEM, SMEM, SMEM, VMEM, VMEM])(*arrays)
+    return call(stage_kernel, "stage", [row, two, edge, edge], [HBM, SMEM, SMEM, VMEM, VMEM])(*arrays)
 
 
 def cell_sum_kernel(block, feat, send_a, send_b):
@@ -337,11 +339,10 @@
     even = lax.rem(lax.axis_index("az"), 2) == 0
 
     def low_high(from_a, from_b):
-        a = from_a[...].astype(jnp.float32)
-        b = from_b[...].astype(jnp.float32)
+        a, b = from_a[...], from_b[...]
         return jnp.concatenate([jnp.where(even, b, a), jnp.where(even, a, b)], axis=0)
 
-    x = streamed(low_high(feat_a, feat_b), low_high(hid_a, hid_b), pitch, w_map)
+    x = streamed(low_high(feat_a, feat_b), low_high(hid_a, hid_b).astype(jnp.float32), pitch, w_map)
     normed = norm_rows(x.reshape(512, WIDTH), gains[0:1, :])
     narrow = columns(normed.reshape(16, 32, WIDTH), 4, 8, 24).astype(jnp.bfloat16)
     wide = normed.astype(jnp.bfloat16)
@@ -437,7 +438,7 @@
     final_mapping_matrix,
     terminal_rescale_factor,
 ):
-    packed, token = pack(
+    packed = pack(
         mesh_portion_descriptors.reshape(128, 8, 2, 128), mesh_entry_site.reshape(16, 128), mesh_portion_tally
     )
     arrived = lax.all_to_all(packed, ("az", "rad"), split_axis=0, concat_axis=0, tiled=True)
@@ -445,7 +446,7 @@
     hidden = hidden_site_vector[0]
     block_ones = jnp.asarray(np.kron(np.eye(4), np.ones((64, 64))), jnp.bfloat16)
     pitch, scale, to_a, to_b = stage(
-        token, incline_grid_position, sharpness_scale, incline_vector_lookup, hidden
+        packed, incline_grid_position, sharpness_scale, incline_vector_lookup, hidden
     )
     hid_a, hid_b = swap(to_a, "rad", 0), swap(to_b, "rad", 1)
 

time: 51.2 us -> 50.5 us (0.986)
  Pallas kernels: 14.9 us -> 14.2 us
    pallas_call x2, Pallas kernels: 3.3 us -> 2.73 us  [the longest x1 2.09 us: pack(): call(pack_kernel, 'pack', [(128, 2, 1152)], [HBM] * 3, [HBM], [pltpu.VMEM...]
where the time goes in v4:
time: 50.5 us; the launch traced here: 50.1 us
  starting transfers between devices  23.9 us (47%)
  Pallas kernels  14.2 us (28%)
  waiting for transfers between devices  9.93 us (20%)
  local copies, waits for them, and re-layouts  1.13 us (2%)
  between operations  0.9 us (2%)
    ppermute x8, starting transfers between devices, swap(): return lax.ppermute(x, axis, [(i, j) for i, j in pairs if 0 <= j < count])  13.5 us
    all_to_all x1, starting transfers between devices, per_device(): lax.all_to_all(packed, ('az', 'rad'), split_axis=0, concat_axis=0, tiled=...  10.5 us
    pallas_call x1, Pallas kernels, outer(): call(outer_kernel, 'outer', [(16, 16, WIDTH)], [VMEM] * 24, scratch=[pltp...  7.16 us
    all_to_all x1, waiting for transfers between devices, per_device(): lax.all_to_all(packed, ('az', 'rad'), split_axis=0, concat_axis=0, tiled=...  5.33 us
    ppermute x8, waiting for transfers between devices, swap(): return lax.ppermute(x, axis, [(i, j) for i, j in pairs if 0 <= j < count])  4.61 us
    pallas_call x1, Pallas kernels, inner(): call(inner_kernel, 'inner', outs, [VMEM] * 8, scratch=scratch, mib=14)  3.3 us
    pallas_call x1, Pallas kernels, pack(): call(pack_kernel, 'pack', [(128, 2, 1152)], [HBM] * 3, [HBM], [pltpu.VMEM...  2.09 us
    unnamed x28, local copies, waits for them, and re-layouts  1.13 us
  transfers between devices with their start and end apart: 9, of which 4 were waited for; matrix products, arithmetic and copies ran while one was open for 0% of the time, Pallas kernels for 10%

profile of v4, /device:TPU:8, one launch (start us, length us, event | category | flops | bytes accessed | tf_op | source)
XLA Modules:
  0.0 50.1 jit_solution(8386907496041842894)
XLA Ops:
  0.0 2.1 %pack.1.packed = bf16[128,2,1152]{2,1,0:T(2,128)(2,1)} custom-call(bf16[128,8,2,128]{3,2,1,0:T(2,128)(2,1)} %bitcast.8, s32[16,128]{1,0:T(8,128)} %bitcast.9, s32[1,128]{1,0:T(1,128)} %tally.1), custom_call_target="tpu_custom_call" | custom-call | flops 1500000000 | bytes 4500000 | tf_op jit(solution)/shard_map/pack/pallas_call | solution.py:133
  2.1 10.5 %all-to-all-start = ((bf16[128,2,1152]{2,1,0:T(2,128)(2,1)}), bf16[128,2,1152]{2,1,0:T(2,128)(2,1)S(1)}, u32[]{:S(2)}, u32[]{:S(2)}) async-start(bf16[128,2,1152]{2,1,0:T(2,128)(2,1)} %pack.1.packed), calls=%async_computation | async-start | bytes 1179648 | tf_op jit(solution)/shard_map/all_to_all | solution.py:444
  13.3 1.1 %copy-done = bf16[128,2,1152]{2,1,0:T(2,128)(2,1)S(1)} copy-done((bf16[128,2,1152]{2,1,0:T(2,128)(2,1)S(1)}, bf16[128,2,1152]{2,1,0:T(2,128)(2,1)}, u32[]{:S(2)}) %copy-start) | copy-done | bytes 589848
  14.3 0.6 %stage.1 = (f32[1,512]{1,0:T(1,128)S(1)}, f32[2,512]{1,0:T(2,128)S(1)}, bf16[16,8,512]{2,1,0:T(8,128)(2,1)S(1)}, bf16[16,8,512]{2,1,0:T(8,128)(2,1)S(1)}) custom-call(bf16[128,2,1152]{2,1,0:T(2,128)(2,1)S(1)} %copy-done, s32[1]{0:T(128)S(6)} %copy.18.pitch_at, f32[2,8]{1,0:T(2,128)S(1)} %copy-done.8, bf16[64,512]{1,0:T(8,128)(2,1)S(1)} %copy-done.5, ...), custom_call_target="tpu_custom_call" | custom-call | flops 1000000000 | bytes 3000000 | tf_op jit(solution)/shard_map/stage/pallas_call | solution.py:172
  15.0 3.0 %collective-permute-start.2 = (bf16[16,8,512]{2,1,0:T(8,128)(2,1)S(1)}, bf16[16,8,512]{2,1,0:T(8,128)(2,1)S(1)}, u32[]{:S(2)}, u32[]{:S(2)}) collective-permute-start(bf16[16,8,512]{2,1,0:T(8,128)(2,1)S(1)} %get-tuple-element.28), channel_id=1, source_target_pairs={{0,1},{1,0},{2,3},{3,2},{4,5},{5,4},{6,7},{7,6},{8,9},{9,8},{10,11... | collective-permute-start | bytes 393224 | tf_op jit(solution)/shard_map/ppermute | solution.py:424
  18.0 3.0 %collective-permute-start.3 = (bf16[16,8,512]{2,1,0:T(8,128)(2,1)S(1)}, bf16[16,8,512]{2,1,0:T(8,128)(2,1)S(1)}, u32[]{:S(2)}, u32[]{:S(2)}) collective-permute-start(bf16[16,8,512]{2,1,0:T(8,128)(2,1)S(1)} %get-tuple-element.29), channel_id=1, source_target_pairs={{1,2},{2,1},{3,4},{4,3},{5,6},{6,5},{9,10},{10,9},{11,12},{12,11},... | collective-permute-start | bytes 393224 | tf_op jit(solution)/shard_map/ppermute | solution.py:424
  21.0 5.3 %all-to-all-done.block = bf16[128,2,1152]{2,1,0:T(2,128)(2,1)S(1)} async-done(((bf16[128,2,1152]{2,1,0:T(2,128)(2,1)}), bf16[128,2,1152]{2,1,0:T(2,128)(2,1)S(1)}, u32[]{:S(2)}, u32[]{:S(2)}) %all-to-all-start) | async-done | bytes 589856 | tf_op jit(solution)/shard_map/all_to_all | solution.py:444
  26.3 0.6 %cell_sums.1 = (bf16[16,16,128]{2,1,0:T(8,128)(2,1)S(1)}, bf16[16,8,128]{2,1,0:T(8,128)(2,1)S(1)}, bf16[16,8,128]{2,1,0:T(8,128)(2,1)S(1)}) custom-call(bf16[128,2,1152]{2,1,0:T(2,128)(2,1)S(1)} %all-to-all-done.block), custom_call_target="tpu_custom_call" | custom-call | flops 2000000000 | bytes 6000000 | tf_op jit(solution)/shard_map/cell_sums/pallas_call | solution.py:197
  26.9 4.3 %collective-permute-start = (bf16[16,8,128]{2,1,0:T(8,128)(2,1)S(1)}, bf16[16,8,128]{2,1,0:T(8,128)(2,1)S(1)}, u32[]{:S(2)}, u32[]{:S(2)}) collective-permute-start(bf16[16,8,128]{2,1,0:T(8,128)(2,1)S(1)} %get-tuple-element.26), channel_id=1, source_target_pairs={{1,2},{2,1},{3,4},{4,3},{5,6},{6,5},{9,10},{10,9},{11,12},{12,11},... | collective-permute-start | bytes 98312 | tf_op jit(solution)/shard_map/ppermute | solution.py:424
  31.3 1.2 %collective-permute-start.1 = (bf16[16,8,128]{2,1,0:T(8,128)(2,1)S(1)}, bf16[16,8,128]{2,1,0:T(8,128)(2,1)S(1)}, u32[]{:S(2)}, u32[]{:S(2)}) collective-permute-start(bf16[16,8,128]{2,1,0:T(8,128)(2,1)S(1)} %get-tuple-element.27), channel_id=1, source_target_pairs={{0,1},{1,0},{2,3},{3,2},{4,5},{5,4},{6,7},{7,6},{8,9},{9,8},{10,11... | collective-permute-start | bytes 98312 | tf_op jit(solution)/shard_map/ppermute | solution.py:424
  32.5 0.0 copy-start.9
  32.5 0.0 copy-start.10
  32.5 0.0 copy-start.12
  32.6 0.2 widen.1
  32.7 0.1 collective-permute-start.6
  32.8 0.9 %collective-permute-start.7 = (bf16[8,32,512]{2,1,0:T(8,128)(2,1)S(1)}, bf16[8,32,512]{2,1,0:T(8,128)(2,1)S(1)}, u32[]{:S(2)}, u32[]{:S(2)}) collective-permute-start(bf16[8,32,512]{2,1,0:T(8,128)(2,1)S(1)} %get-tuple-element.35), channel_id=1, source_target_pairs={{0,8},{8,0},{16,24},{24,16},{32,40},{40,32},{48,56},{56,48},{64,72... | collective-permute-start | bytes 786440 | tf_op jit(solution)/shard_map/ppermute | solution.py:424
  33.7 1.5 %collective-permute-done.feat_b = bf16[16,8,128]{2,1,0:T(8,128)(2,1)S(1)} collective-permute-done((bf16[16,8,128]{2,1,0:T(8,128)(2,1)S(1)}, bf16[16,8,128]{2,1,0:T(8,128)(2,1)S(1)}, u32[]{:S(2)}, u32[]{:S(2)}) %collective-permute-start) | collective-permute-done | bytes 32800 | tf_op jit(solution)/shard_map/ppermute | solution.py:424
  35.3 1.5 %collective-permute-done.1.feat_a = bf16[16,8,128]{2,1,0:T(8,128)(2,1)S(1)} collective-permute-done((bf16[16,8,128]{2,1,0:T(8,128)(2,1)S(1)}, bf16[16,8,128]{2,1,0:T(8,128)(2,1)S(1)}, u32[]{:S(2)}, u32[]{:S(2)}) %collective-permute-start.1) | collective-permute-done | bytes 32800 | tf_op jit(solution)/shard_map/ppermute | solution.py:424
  36.8 0.3 band.1
  37.1 0.1 collective-permute-start.4
  37.1 0.8 %collective-permute-start.5 = (bf16[8,32,128]{2,1,0:T(8,128)(2,1)S(1)}, bf16[8,32,128]{2,1,0:T(8,128)(2,1)S(1)}, u32[]{:S(2)}, u32[]{:S(2)}) collective-permute-start(bf16[8,32,128]{2,1,0:T(8,128)(2,1)S(1)} %get-tuple-element.33), channel_id=1, source_target_pairs={{0,8},{8,0},{16,24},{24,16},{32,40},{40,32},{48,56},{56,48},{64,72... | collective-permute-start | bytes 196616 | tf_op jit(solution)/shard_map/ppermute | solution.py:424
  38.1 3.3 %inner.1 = (bf16[384,512]{1,0:T(8,128)(2,1)S(1)}, bf16[512,512]{1,0:T(8,128)(2,1)S(1)}, bf16[512,512]{1,0:T(8,128)(2,1)S(1)}, bf16[192,512]{1,0:T(8,128)(2,1)S(1...) custom-call(bf16[16,32,512]{2,1,0:T(8,128)(2,1)S(1)} %get-tuple-element.36.band_stream, ...), custom_call_target="tpu_custom_call" | custom-call | flops 4000000000 | bytes 12000000 | tf_op jit(solution)/shard_map/inner/pallas_call | solution.py:330
  41.4 1.6 %collective-permute-done.4.feat_b = bf16[8,32,128]{2,1,0:T(8,128)(2,1)S(1)} collective-permute-done((bf16[8,32,128]{2,1,0:T(8,128)(2,1)S(1)}, bf16[8,32,128]{2,1,0:T(8,128)(2,1)S(1)}, u32[]{:S(2)}, u32[]{:S(2)}) %collective-permute-start.4) | collective-permute-done | bytes 65568 | tf_op jit(solution)/shard_map/ppermute | solution.py:424
  43.0 7.2 %outer.1 = bf16[16,16,512]{2,1,0:T(8,128)(2,1)} custom-call(bf16[8,32,128]{2,1,0:T(8,128)(2,1)S(1)} %collective-permute-done.4.feat_b, bf16[8,32,128]{2,1,0:T(8,128)(2,1)S(1)} %collective-permute-done.5.feat_a, bf16[8,32,512]{2,1,0:T(8,128)(2,1)S(1)} %collective-permute-done.6.hid_b, bf16[8,32,512]{2,1,0:T(8,128)(2,1)S(1)} %collective-permute-done.7.hid_a, ...), custom_call_target="tpu_custom_call" | custom-call | flops 8000000000 | bytes 24000000 | tf_op jit(solution)/shard_map/outer/pallas_call | solution.py:409
  (29 shorter events, 0.1 us)
Async XLA Ops:
  0.0 13.2 %copy-start.3 = (bf16[1,16,16,512]{3,2,1,0:T(8,128)(2,1)S(1)}, bf16[1,16,16,512]{3,2,1,0:T(8,128)(2,1)}, u32[]{:S(2)}) copy-start(bf16[1,16,16,512]{3,2,1,0:T(8,128)(2,1)} %param.17) | copy-start | bytes 786436
  0.0 13.2 %copy-start.5 = (bf16[64,512]{1,0:T(8,128)(2,1)S(1)}, bf16[64,512]{1,0:T(8,128)(2,1)}, u32[]{:S(2)}) copy-start(bf16[64,512]{1,0:T(8,128)(2,1)} %lookup.1) | copy-start | bytes 196612
  0.0 13.2 %copy-start.8 = (f32[2,8]{1,0:T(2,128)S(1)}, f32[2,8]{1,0:T(2,128)}, u32[]{:S(2)}) copy-start(f32[2,8]{1,0:T(2,128)} %sharp.1) | copy-start | bytes 196
  2.1 24.2 %all-to-all-start = ((bf16[128,2,1152]{2,1,0:T(2,128)(2,1)}), bf16[128,2,1152]{2,1,0:T(2,128)(2,1)S(1)}, u32[]{:S(2)}, u32[]{:S(2)}) async-start(bf16[128,2,1152]{2,1,0:T(2,128)(2,1)} %pack.1.packed), calls=%async_computation | async-start | bytes 1179648 | tf_op jit(solution)/shard_map/all_to_all | solution.py:444
  13.2 1.1 %copy-start = (bf16[128,2,1152]{2,1,0:T(2,128)(2,1)S(1)}, bf16[128,2,1152]{2,1,0:T(2,128)(2,1)}, u32[]{:S(2)}) copy-start(bf16[128,2,1152]{2,1,0:T(2,128)(2,1)} %pack.1.packed) | copy-start | bytes 1769476
  15.0 17.5 %collective-permute-start.2 = (bf16[16,8,512]{2,1,0:T(8,128)(2,1)S(1)}, bf16[16,8,512]{2,1,0:T(8,128)(2,1)S(1)}, u32[]{:S(2)}, u32[]{:S(2)}) collective-permute-start(bf16[16,8,512]{2,1,0:T(8,128)(2,1)S(1)} %get-tuple-element.28), channel_id=1, source_target_pairs={{0,1},{1,0},{2,3},{3,2},{4,5},{5,4},{6,7},{7,6},{8,9},{9,8},{10,11... | collective-permute-start | bytes 393224 | tf_op jit(solution)/shard_map/ppermute | solution.py:424
  18.0 14.5 %collective-permute-start.3 = (bf16[16,8,512]{2,1,0:T(8,128)(2,1)S(1)}, bf16[16,8,512]{2,1,0:T(8,128)(2,1)S(1)}, u32[]{:S(2)}, u32[]{:S(2)}) collective-permute-start(bf16[16,8,512]{2,1,0:T(8,128)(2,1)S(1)} %get-tuple-element.29), channel_id=1, source_target_pairs={{1,2},{2,1},{3,4},{4,3},{5,6},{6,5},{9,10},{10,9},{11,12},{12,11},... | collective-permute-start | bytes 393224 | tf_op jit(solution)/shard_map/ppermute | solution.py:424
  26.9 9.9 %copy-start.4 = (bf16[128,512]{1,0:T(8,128)(2,1)S(1)}, bf16[128,512]{1,0:T(8,128)(2,1)}, u32[]{:S(2)}) copy-start(bf16[128,512]{1,0:T(8,128)(2,1)} %w_map.3) | copy-start | bytes 393220
  26.9 8.3 %collective-permute-start = (bf16[16,8,128]{2,1,0:T(8,128)(2,1)S(1)}, bf16[16,8,128]{2,1,0:T(8,128)(2,1)S(1)}, u32[]{:S(2)}, u32[]{:S(2)}) collective-permute-start(bf16[16,8,128]{2,1,0:T(8,128)(2,1)S(1)} %get-tuple-element.26), channel_id=1, source_target_pairs={{1,2},{2,1},{3,4},{4,3},{5,6},{6,5},{9,10},{10,9},{11,12},{12,11},... | collective-permute-start | bytes 98312 | tf_op jit(solution)/shard_map/ppermute | solution.py:424
  31.3 5.5 %collective-permute-start.1 = (bf16[16,8,128]{2,1,0:T(8,128)(2,1)S(1)}, bf16[16,8,128]{2,1,0:T(8,128)(2,1)S(1)}, u32[]{:S(2)}, u32[]{:S(2)}) collective-permute-start(bf16[16,8,128]{2,1,0:T(8,128)(2,1)S(1)} %get-tuple-element.27), channel_id=1, source_target_pairs={{0,1},{1,0},{2,3},{3,2},{4,5},{5,4},{6,7},{7,6},{8,9},{9,8},{10,11... | collective-permute-start | bytes 98312 | tf_op jit(solution)/shard_map/ppermute | solution.py:424
  32.5 5.5 %copy-start.1 = (bf16[2,512,1536]{2,1,0:T(8,128)(2,1)S(1)}, bf16[2,512,1536]{2,1,0:T(8,128)(2,1)}, u32[]{:S(2)}) copy-start(bf16[2,512,1536]{2,1,0:T(8,128)(2,1)} %w_qkv.3) | copy-start | bytes 9437188
  32.5 5.5 %copy-start.2 = (bf16[2,512,512]{2,1,0:T(8,128)(2,1)S(1)}, bf16[2,512,512]{2,1,0:T(8,128)(2,1)}, u32[]{:S(2)}) copy-start(bf16[2,512,512]{2,1,0:T(8,128)(2,1)} %w_out.3) | copy-start | bytes 3145732
  32.5 5.5 %copy-start.6 = (f32[2,512]{1,0:T(2,128)S(1)}, f32[2,512]{1,0:T(2,128)}, u32[]{:S(2)}) copy-start(f32[2,512]{1,0:T(2,128)} %gains.3) | copy-start | bytes 12292
  32.5 5.5 %copy-start.9 = (bf16[1024,128]{1,0:T(8,128)(2,1)S(1)}, bf16[1024,128]{1,0:T(8,128)(2,1)}, u32[]{:S(2)}) copy-start(bf16[1024,128]{1,0:T(8,128)(2,1)} %constant.12.clone.k_aug) | copy-start | bytes 786436
  32.5 5.5 %copy-start.10 = (bf16[576,128]{1,0:T(8,128)(2,1)S(1)}, bf16[576,128]{1,0:T(8,128)(2,1)}, u32[]{:S(2)}) copy-start(bf16[576,128]{1,0:T(8,128)(2,1)} %constant.11.clone.q_aug) | copy-start | bytes 442372
  32.5 5.5 %copy-start.12 = (bf16[256,256]{1,0:T(8,128)(2,1)S(1)}, bf16[256,256]{1,0:T(8,128)(2,1)}, u32[]{:S(2)}) copy-start(bf16[256,256]{1,0:T(8,128)(2,1)} %constant.10.clone.block_ones) | copy-start | bytes 393220
  32.7 10.2 %collective-permute-start.6 = (bf16[8,32,512]{2,1,0:T(8,128)(2,1)S(1)}, bf16[8,32,512]{2,1,0:T(8,128)(2,1)S(1)}, u32[]{:S(2)}, u32[]{:S(2)}) collective-permute-start(bf16[8,32,512]{2,1,0:T(8,128)(2,1)S(1)} %get-tuple-element.34), channel_id=1, source_target_pairs={{0,120},{8,16},{16,8},{24,32},{32,24},{40,48},{48,40},{56,64},{64,... | collective-permute-start | bytes 786440 | tf_op jit(solution)/shard_map/ppermute | solution.py:424
  32.8 10.1 %collective-permute-start.7 = (bf16[8,32,512]{2,1,0:T(8,128)(2,1)S(1)}, bf16[8,32,512]{2,1,0:T(8,128)(2,1)S(1)}, u32[]{:S(2)}, u32[]{:S(2)}) collective-permute-start(bf16[8,32,512]{2,1,0:T(8,128)(2,1)S(1)} %get-tuple-element.35), channel_id=1, source_target_pairs={{0,8},{8,0},{16,24},{24,16},{32,40},{40,32},{48,56},{56,48},{64,72... | collective-permute-start | bytes 786440 | tf_op jit(solution)/shard_map/ppermute | solution.py:424
  37.1 5.9 %collective-permute-start.4 = (bf16[8,32,128]{2,1,0:T(8,128)(2,1)S(1)}, bf16[8,32,128]{2,1,0:T(8,128)(2,1)S(1)}, u32[]{:S(2)}, u32[]{:S(2)}) collective-permute-start(bf16[8,32,128]{2,1,0:T(8,128)(2,1)S(1)} %get-tuple-element.32), channel_id=1, source_target_pairs={{0,120},{8,16},{16,8},{24,32},{32,24},{40,48},{48,40},{56,64},{64,... | collective-permute-start | bytes 196616 | tf_op jit(solution)/shard_map/ppermute | solution.py:424
  37.1 5.8 %collective-permute-start.5 = (bf16[8,32,128]{2,1,0:T(8,128)(2,1)S(1)}, bf16[8,32,128]{2,1,0:T(8,128)(2,1)S(1)}, u32[]{:S(2)}, u32[]{:S(2)}) collective-permute-start(bf16[8,32,128]{2,1,0:T(8,128)(2,1)S(1)} %get-tuple-element.33), channel_id=1, source_target_pairs={{0,8},{8,0},{16,24},{24,16},{32,40},{40,32},{48,56},{56,48},{64,72... | collective-permute-start | bytes 196616 | tf_op jit(solution)/shard_map/ppermute | solution.py:424
  38.0 4.9 %copy-start.7 = (f32[512]{0:T(512)S(1)}, f32[512]{0:T(512)}, u32[]{:S(2)}) copy-start(f32[512]{0:T(512)} %param.28) | copy-start | bytes 6148
  38.0 4.9 %copy-start.11 = (bf16[576,128]{1,0:T(8,128)(2,1)S(1)}, bf16[576,128]{1,0:T(8,128)(2,1)}, u32[]{:S(2)}) copy-start(bf16[576,128]{1,0:T(8,128)(2,1)} %constant.14.clone.k_aug_1) | copy-start | bytes 442372
  38.0 4.9 %copy-start.13 = (bf16[256,128]{1,0:T(8,128)(2,1)S(1)}, bf16[256,128]{1,0:T(8,128)(2,1)}, u32[]{:S(2)}) copy-start(bf16[256,128]{1,0:T(8,128)(2,1)} %constant.13.clone.q_aug_1) | copy-start | bytes 196612

commit v5 on v4

--- a/solution.py
+++ b/solution.py
@@ -269,7 +269,7 @@
     return table + jnp.where(ends, 1.0, 0.0).astype(jnp.bfloat16)
 
 
-def attend(queries, query_aug, keys, key_aug, values, att):
+def attend(queries, query_aug, keys, key_aug, values, att, att_at=0):
     n = query_aug.shape[0]
     lane = lax.broadcasted_iota(jnp.int32, (1, 128), 1)
     low = jnp.where(lane < 64, 1.0, 0.0).astype(jnp.bfloat16)
@@ -294,7 +294,7 @@
         yield
         top = jnp.where(half, got[:n, :128], got[n:, :128])
         total = jnp.where(half, got[:n, 128:], got[n:, 128:])
-        att[0:n, lanes] = (top / total).astype(jnp.bfloat16)
+        att[att_at : att_at + n, lanes] = (top / total).astype(jnp.bfloat16)
 
     return [pair_of_heads(pair) for pair in range(HEADS // 2)]
 
@@ -311,7 +311,7 @@
     normed = norm_rows(x.reshape(512, WIDTH), gains[0:1, :])
     narrow = columns(normed.reshape(16, 32, WIDTH), 0, 16, 24).astype(jnp.bfloat16)
     wide = normed.astype(jnp.bfloat16)
-    interleave(project_all(w_qkv, 0, wide, narrow, block_ones, scale, queries, 0, keys, values, 0), 2)
+    interleave(project_all(w_qkv, 0, wide, narrow, block_ones, scale, queries, 0, keys, values, 0), 3)
     pairs = attend(
         [(queries, 96, 192)], query_lanes(q_aug[192:384]), [(keys, 0, 512)], k_aug[256:768], [(values, 0, 512)], att
     )
@@ -321,7 +321,7 @@
     normed = norm_rows(x, gains[1:2, :])
     narrow = columns(normed.reshape(8, 24, WIDTH), 0, 8, 16).astype(jnp.bfloat16)
     wide = normed.astype(jnp.bfloat16)
-    interleave(project_all(w_qkv, 1, wide, narrow, block_ones, scale, queries_1, 0, keys_1, values_1, 0), 2)
+    interleave(project_all(w_qkv, 1, wide, narrow, block_ones, scale, queries_1, 0, keys_1, values_1, 0), 4)
 
 
 def inner(*arrays):
@@ -333,9 +333,8 @@
 def outer_kernel(
     feat_b, feat_a, hid_b, hid_a, band_stream, pitch, w_map, scale, gains, w_qkv, w_out, last_gain, block_ones, q_aug, k_aug, q_aug_1, k_aug_1,
     q_mid, k_mid, v_mid, stream_mid, q1_mid, k1_mid, v1_mid,
-    out, q_end, k_end, v_end, q1_end, k1_end, v1_end, att_0, att_1,
+    out, q_end, k_end, v_end, q1_end, k1_end, v1_end, att,
 ):
-    att = (att_0, att_1)
     even = lax.rem(lax.axis_index("az"), 2) == 0
 
     def low_high(from_a, from_b):
@@ -346,7 +345,7 @@
     normed = norm_rows(x.reshape(512, WIDTH), gains[0:1, :])
     narrow = columns(normed.reshape(16, 32, WIDTH), 4, 8, 24).astype(jnp.bfloat16)
     wide = normed.astype(jnp.bfloat16)
-    interleave(project_all(w_qkv, 0, wide, narrow, block_ones, scale, q_end, 0, k_end, v_end, 0), 2)
+    interleave(project_all(w_qkv, 0, wide, narrow, block_ones, scale, q_end, 0, k_end, v_end, 0), 3)
     pairs = []
     for part in range(2):
         if part == 0:
@@ -356,30 +355,16 @@
             q = [(q_mid, 288, 96), (q_end, 96, 96)]
             k, v = [[(mid, 256, 256), (end, 256, 256)] for end, mid in ((k_end, k_mid), (v_end, v_mid))]
         q_lanes = query_lanes(q_aug[384 * part : 384 * part + 192])
-        pairs.append(attend(q, q_lanes, k, k_aug[512 * part : 512 * part + 512], v, att[part]))
-    kept = [None, None]
-
-    def finish(part):
-        at = 4 * (1 - part)
-        ours = band_stream[12 * part : 12 * part + 4].astype(jnp.float32)
-        before = [columns(x, 4 + 4 * part, 4, 24), columns(ours, 0, 4, 24)]
-        y = dot(att[part][...], w_out[0])
-        yield
-        y = rounded(jnp.concatenate(before if part == 0 else before[::-1], axis=0) + y)
-        normed = norm_rows(y, gains[1:2, :])
-        narrow = columns(normed.reshape(8, 24, WIDTH), at, 4, 16).astype(jnp.bfloat16)
-        kept[part] = columns(y.reshape(8, 24, WIDTH), at, 4, 16)
-        yield
-        wide = normed.astype(jnp.bfloat16)
-        yield from one_by_one(
-            *project_all(
-                w_qkv, 1, wide, narrow, block_ones, scale, q1_end, 64 * part, k1_end, v1_end, 192 * part
-            )
-        )
-
-    interleave(pairs[0], 2)
-    interleave([one_by_one(*pairs[1]), finish(0)], 2)
-    middle = stream_mid[...].astype(jnp.float32).reshape(8, 24, WIDTH)
+        pairs += attend(q, q_lanes, k, k_aug[512 * part : 512 * part + 512], v, att, 192 * part)
+    interleave(pairs, 2)
+    ours = [columns(band_stream[at : at + 4].astype(jnp.float32), 0, 4, 24) for at in (0, 12)]
+    before = [columns(x, 4, 4, 24), *ours, columns(x, 8, 4, 24)]
+    y = rounded(jnp.concatenate(before, axis=0) + dot(att[...], w_out[0]))
+    normed = norm_rows(y, gains[1:2, :])
+    kept = columns(y.reshape(16, 24, WIDTH), 4, 8, 16)
+    narrow = columns(normed.reshape(16, 24, WIDTH), 4, 8, 16).astype(jnp.bfloat16)
+    wide = normed.astype(jnp.bfloat16)
+    interleave(project_all(w_qkv, 1, wide, narrow, block_ones, scale, q1_end, 0, k1_end, v1_end, 0), 4)
     pairs = []
     for part in range(2):
         if part == 0:
@@ -389,23 +374,16 @@
             q = [(q1_mid, 64, 64), (q1_end, 64, 64)]
             k, v = [[(mid, 0, 192), (end, 192, 192)] for end, mid in ((k1_end, k1_mid), (v1_end, v1_mid))]
         q_lanes = query_lanes(q_aug_1[128 * part : 128 * part + 128])
-        pairs.append(attend(q, q_lanes, k, k_aug_1[192 * part : 192 * part + 384], v, att[part]))
-
-    def end(part):
-        before = [columns(middle, 4 * part, 4, 16), kept[part]]
-        y = dot(att[part][0:128], w_out[1])
-        yield
-        y = rounded(jnp.concatenate(before if part else before[::-1], axis=0) + y)
-        latent = norm_rows(y, last_gain[...])
-        out[8 * part : 8 * part + 8] = latent.reshape(8, 16, WIDTH).astype(jnp.bfloat16)
-
-    interleave([finish(1), one_by_one(*pairs[0])], 2)
-    interleave([one_by_one(*pairs[1]), end(0)], 2)
-    interleave([end(1)], 1)
+        pairs += attend(q, q_lanes, k, k_aug_1[192 * part : 192 * part + 384], v, att, 128 * part)
+    interleave(pairs, 2)
+    middle = columns(stream_mid[...].astype(jnp.float32).reshape(8, 24, WIDTH), 0, 8, 16)
+    before = jnp.concatenate([kept[:64], middle, kept[64:]], axis=0)
+    y = rounded(before + dot(att[0:256], w_out[1]))
+    out[...] = norm_rows(y, last_gain[...]).reshape(16, 16, WIDTH).astype(jnp.bfloat16)
 
 
 def outer(*arrays):
-    scratch = [192, 512, 512, 128, 384, 384, 192, 192]
+    scratch = [192, 512, 512, 128, 384, 384, 384]
     return call(
         outer_kernel,
         "outer",

time: 50.5 us -> 49.9 us (0.988)
  Pallas kernels: 14.2 us -> 13.6 us
where the time goes in v5:
time: 49.9 us; the launch traced here: 49.6 us
  starting transfers between devices  23.9 us (48%)
  Pallas kernels  13.6 us (27%)
  waiting for transfers between devices  10 us (20%)
  local copies, waits for them, and re-layouts  1.13 us (2%)
  between operations  0.9 us (2%)
    ppermute x8, starting transfers between devices, swap(): return lax.ppermute(x, axis, [(i, j) for i, j in pairs if 0 <= j < count])  13.5 us
    all_to_all x1, starting transfers between devices, per_device(): lax.all_to_all(packed, ('az', 'rad'), split_axis=0, concat_axis=0, tiled=...  10.5 us
    pallas_call x1, Pallas kernels, outer(): call(outer_kernel, 'outer', [(16, 16, WIDTH)], [VMEM] * 24, scratch=[pltp...  6.66 us
    all_to_all x1, waiting for transfers between devices, per_device(): lax.all_to_all(packed, ('az', 'rad'), split_axis=0, concat_axis=0, tiled=...  5.33 us
    ppermute x8, waiting for transfers between devices, swap(): return lax.ppermute(x, axis, [(i, j) for i, j in pairs if 0 <= j < count])  4.7 us
    pallas_call x1, Pallas kernels, inner(): call(inner_kernel, 'inner', outs, [VMEM] * 8, scratch=scratch, mib=14)  3.2 us
    pallas_call x1, Pallas kernels, pack(): call(pack_kernel, 'pack', [(128, 2, 1152)], [HBM] * 3, [HBM], [pltpu.VMEM...  2.09 us
    unnamed x28, local copies, waits for them, and re-layouts  1.13 us
  transfers between devices with their start and end apart: 9, of which 4 were waited for; matrix products, arithmetic and copies ran while one was open for 0% of the time, Pallas kernels for 10%

profile of v5, /device:TPU:8, one launch (start us, length us, event | category | flops | bytes accessed | tf_op | source)
XLA Modules:
  0.0 49.6 jit_solution(6958825070600801399)
XLA Ops:
  0.0 2.1 %pack.1.packed = bf16[128,2,1152]{2,1,0:T(2,128)(2,1)} custom-call(bf16[128,8,2,128]{3,2,1,0:T(2,128)(2,1)} %bitcast.8, s32[16,128]{1,0:T(8,128)} %bitcast.9, s32[1,128]{1,0:T(1,128)} %tally.1), custom_call_target="tpu_custom_call" | custom-call | flops 1500000000 | bytes 4500000 | tf_op jit(solution)/shard_map/pack/pallas_call | solution.py:133
  2.1 10.5 %all-to-all-start = ((bf16[128,2,1152]{2,1,0:T(2,128)(2,1)}), bf16[128,2,1152]{2,1,0:T(2,128)(2,1)S(1)}, u32[]{:S(2)}, u32[]{:S(2)}) async-start(bf16[128,2,1152]{2,1,0:T(2,128)(2,1)} %pack.1.packed), calls=%async_computation | async-start | bytes 1179648 | tf_op jit(solution)/shard_map/all_to_all | solution.py:422
  13.3 1.1 %copy-done = bf16[128,2,1152]{2,1,0:T(2,128)(2,1)S(1)} copy-done((bf16[128,2,1152]{2,1,0:T(2,128)(2,1)S(1)}, bf16[128,2,1152]{2,1,0:T(2,128)(2,1)}, u32[]{:S(2)}) %copy-start) | copy-done | bytes 589848
  14.3 0.6 %stage.1 = (f32[1,512]{1,0:T(1,128)S(1)}, f32[2,512]{1,0:T(2,128)S(1)}, bf16[16,8,512]{2,1,0:T(8,128)(2,1)S(1)}, bf16[16,8,512]{2,1,0:T(8,128)(2,1)S(1)}) custom-call(bf16[128,2,1152]{2,1,0:T(2,128)(2,1)S(1)} %copy-done, s32[1]{0:T(128)S(6)} %copy.18.pitch_at, f32[2,8]{1,0:T(2,128)S(1)} %copy-done.8, bf16[64,512]{1,0:T(8,128)(2,1)S(1)} %copy-done.5, ...), custom_call_target="tpu_custom_call" | custom-call | flops 1000000000 | bytes 3000000 | tf_op jit(solution)/shard_map/stage/pallas_call | solution.py:172
  15.0 3.0 %collective-permute-start.2 = (bf16[16,8,512]{2,1,0:T(8,128)(2,1)S(1)}, bf16[16,8,512]{2,1,0:T(8,128)(2,1)S(1)}, u32[]{:S(2)}, u32[]{:S(2)}) collective-permute-start(bf16[16,8,512]{2,1,0:T(8,128)(2,1)S(1)} %get-tuple-element.28), channel_id=1, source_target_pairs={{0,1},{1,0},{2,3},{3,2},{4,5},{5,4},{6,7},{7,6},{8,9},{9,8},{10,11... | collective-permute-start | bytes 393224 | tf_op jit(solution)/shard_map/ppermute | solution.py:402
  18.0 3.0 %collective-permute-start.3 = (bf16[16,8,512]{2,1,0:T(8,128)(2,1)S(1)}, bf16[16,8,512]{2,1,0:T(8,128)(2,1)S(1)}, u32[]{:S(2)}, u32[]{:S(2)}) collective-permute-start(bf16[16,8,512]{2,1,0:T(8,128)(2,1)S(1)} %get-tuple-element.29), channel_id=1, source_target_pairs={{1,2},{2,1},{3,4},{4,3},{5,6},{6,5},{9,10},{10,9},{11,12},{12,11},... | collective-permute-start | bytes 393224 | tf_op jit(solution)/shard_map/ppermute | solution.py:402
  21.0 5.3 %all-to-all-done.block = bf16[128,2,1152]{2,1,0:T(2,128)(2,1)S(1)} async-done(((bf16[128,2,1152]{2,1,0:T(2,128)(2,1)}), bf16[128,2,1152]{2,1,0:T(2,128)(2,1)S(1)}, u32[]{:S(2)}, u32[]{:S(2)}) %all-to-all-start) | async-done | bytes 589856 | tf_op jit(solution)/shard_map/all_to_all | solution.py:422
  26.3 0.6 %cell_sums.1 = (bf16[16,16,128]{2,1,0:T(8,128)(2,1)S(1)}, bf16[16,8,128]{2,1,0:T(8,128)(2,1)S(1)}, bf16[16,8,128]{2,1,0:T(8,128)(2,1)S(1)}) custom-call(bf16[128,2,1152]{2,1,0:T(2,128)(2,1)S(1)} %all-to-all-done.block), custom_call_target="tpu_custom_call" | custom-call | flops 2000000000 | bytes 6000000 | tf_op jit(solution)/shard_map/cell_sums/pallas_call | solution.py:197
  26.9 4.3 %collective-permute-start = (bf16[16,8,128]{2,1,0:T(8,128)(2,1)S(1)}, bf16[16,8,128]{2,1,0:T(8,128)(2,1)S(1)}, u32[]{:S(2)}, u32[]{:S(2)}) collective-permute-start(bf16[16,8,128]{2,1,0:T(8,128)(2,1)S(1)} %get-tuple-element.26), channel_id=1, source_target_pairs={{1,2},{2,1},{3,4},{4,3},{5,6},{6,5},{9,10},{10,9},{11,12},{12,11},... | collective-permute-start | bytes 98312 | tf_op jit(solution)/shard_map/ppermute | solution.py:402
  31.3 1.2 %collective-permute-start.1 = (bf16[16,8,128]{2,1,0:T(8,128)(2,1)S(1)}, bf16[16,8,128]{2,1,0:T(8,128)(2,1)S(1)}, u32[]{:S(2)}, u32[]{:S(2)}) collective-permute-start(bf16[16,8,128]{2,1,0:T(8,128)(2,1)S(1)} %get-tuple-element.27), channel_id=1, source_target_pairs={{0,1},{1,0},{2,3},{3,2},{4,5},{5,4},{6,7},{7,6},{8,9},{9,8},{10,11... | collective-permute-start | bytes 98312 | tf_op jit(solution)/shard_map/ppermute | solution.py:402
  32.5 0.0 copy-start.9
  32.5 0.0 copy-start.10
  32.5 0.0 copy-start.12
  32.6 0.2 widen.1
  32.7 0.1 collective-permute-start.6
  32.8 0.9 %collective-permute-start.7 = (bf16[8,32,512]{2,1,0:T(8,128)(2,1)S(1)}, bf16[8,32,512]{2,1,0:T(8,128)(2,1)S(1)}, u32[]{:S(2)}, u32[]{:S(2)}) collective-permute-start(bf16[8,32,512]{2,1,0:T(8,128)(2,1)S(1)} %get-tuple-element.35), channel_id=1, source_target_pairs={{0,8},{8,0},{16,24},{24,16},{32,40},{40,32},{48,56},{56,48},{64,72... | collective-permute-start | bytes 786440 | tf_op jit(solution)/shard_map/ppermute | solution.py:402
  33.7 1.5 %collective-permute-done.feat_b = bf16[16,8,128]{2,1,0:T(8,128)(2,1)S(1)} collective-permute-done((bf16[16,8,128]{2,1,0:T(8,128)(2,1)S(1)}, bf16[16,8,128]{2,1,0:T(8,128)(2,1)S(1)}, u32[]{:S(2)}, u32[]{:S(2)}) %collective-permute-start) | collective-permute-done | bytes 32800 | tf_op jit(solution)/shard_map/ppermute | solution.py:402
  35.3 1.5 %collective-permute-done.1.feat_a = bf16[16,8,128]{2,1,0:T(8,128)(2,1)S(1)} collective-permute-done((bf16[16,8,128]{2,1,0:T(8,128)(2,1)S(1)}, bf16[16,8,128]{2,1,0:T(8,128)(2,1)S(1)}, u32[]{:S(2)}, u32[]{:S(2)}) %collective-permute-start.1) | collective-permute-done | bytes 32800 | tf_op jit(solution)/shard_map/ppermute | solution.py:402
  36.8 0.3 band.1
  37.1 0.1 collective-permute-start.4
  37.1 0.8 %collective-permute-start.5 = (bf16[8,32,128]{2,1,0:T(8,128)(2,1)S(1)}, bf16[8,32,128]{2,1,0:T(8,128)(2,1)S(1)}, u32[]{:S(2)}, u32[]{:S(2)}) collective-permute-start(bf16[8,32,128]{2,1,0:T(8,128)(2,1)S(1)} %get-tuple-element.33), channel_id=1, source_target_pairs={{0,8},{8,0},{16,24},{24,16},{32,40},{40,32},{48,56},{56,48},{64,72... | collective-permute-start | bytes 196616 | tf_op jit(solution)/shard_map/ppermute | solution.py:402
  38.1 3.2 %inner.1 = (bf16[384,512]{1,0:T(8,128)(2,1)S(1)}, bf16[512,512]{1,0:T(8,128)(2,1)S(1)}, bf16[512,512]{1,0:T(8,128)(2,1)S(1)}, bf16[192,512]{1,0:T(8,128)(2,1)S(1...) custom-call(bf16[16,32,512]{2,1,0:T(8,128)(2,1)S(1)} %get-tuple-element.36.band_stream, ...), custom_call_target="tpu_custom_call" | custom-call | flops 4000000000 | bytes 12000000 | tf_op jit(solution)/shard_map/inner/pallas_call | solution.py:330
  41.3 1.7 %collective-permute-done.4.feat_b = bf16[8,32,128]{2,1,0:T(8,128)(2,1)S(1)} collective-permute-done((bf16[8,32,128]{2,1,0:T(8,128)(2,1)S(1)}, bf16[8,32,128]{2,1,0:T(8,128)(2,1)S(1)}, u32[]{:S(2)}, u32[]{:S(2)}) %collective-permute-start.4) | collective-permute-done | bytes 65568 | tf_op jit(solution)/shard_map/ppermute | solution.py:402
  43.0 6.7 %outer.1 = bf16[16,16,512]{2,1,0:T(8,128)(2,1)} custom-call(bf16[8,32,128]{2,1,0:T(8,128)(2,1)S(1)} %collective-permute-done.4.feat_b, bf16[8,32,128]{2,1,0:T(8,128)(2,1)S(1)} %collective-permute-done.5.feat_a, bf16[8,32,512]{2,1,0:T(8,128)(2,1)S(1)} %collective-permute-done.6.hid_b, bf16[8,32,512]{2,1,0:T(8,128)(2,1)S(1)} %collective-permute-done.7.hid_a, ...), custom_call_target="tpu_custom_call" | custom-call | flops 8000000000 | bytes 24000000 | tf_op jit(solution)/shard_map/outer/pallas_call | solution.py:387
  (29 shorter events, 0.1 us)
Async XLA Ops:
  0.0 13.2 %copy-start.3 = (bf16[1,16,16,512]{3,2,1,0:T(8,128)(2,1)S(1)}, bf16[1,16,16,512]{3,2,1,0:T(8,128)(2,1)}, u32[]{:S(2)}) copy-start(bf16[1,16,16,512]{3,2,1,0:T(8,128)(2,1)} %param.17) | copy-start | bytes 786436
  0.0 13.2 %copy-start.5 = (bf16[64,512]{1,0:T(8,128)(2,1)S(1)}, bf16[64,512]{1,0:T(8,128)(2,1)}, u32[]{:S(2)}) copy-start(bf16[64,512]{1,0:T(8,128)(2,1)} %lookup.1) | copy-start | bytes 196612
  0.0 13.2 %copy-start.8 = (f32[2,8]{1,0:T(2,128)S(1)}, f32[2,8]{1,0:T(2,128)}, u32[]{:S(2)}) copy-start(f32[2,8]{1,0:T(2,128)} %sharp.1) | copy-start | bytes 196
  2.1 24.2 %all-to-all-start = ((bf16[128,2,1152]{2,1,0:T(2,128)(2,1)}), bf16[128,2,1152]{2,1,0:T(2,128)(2,1)S(1)}, u32[]{:S(2)}, u32[]{:S(2)}) async-start(bf16[128,2,1152]{2,1,0:T(2,128)(2,1)} %pack.1.packed), calls=%async_computation | async-start | bytes 1179648 | tf_op jit(solution)/shard_map/all_to_all | solution.py:422
  13.2 1.1 %copy-start = (bf16[128,2,1152]{2,1,0:T(2,128)(2,1)S(1)}, bf16[128,2,1152]{2,1,0:T(2,128)(2,1)}, u32[]{:S(2)}) copy-start(bf16[128,2,1152]{2,1,0:T(2,128)(2,1)} %pack.1.packed) | copy-start | bytes 1769476
  15.0 17.5 %collective-permute-start.2 = (bf16[16,8,512]{2,1,0:T(8,128)(2,1)S(1)}, bf16[16,8,512]{2,1,0:T(8,128)(2,1)S(1)}, u32[]{:S(2)}, u32[]{:S(2)}) collective-permute-start(bf16[16,8,512]{2,1,0:T(8,128)(2,1)S(1)} %get-tuple-element.28), channel_id=1, source_target_pairs={{0,1},{1,0},{2,3},{3,2},{4,5},{5,4},{6,7},{7,6},{8,9},{9,8},{10,11... | collective-permute-start | bytes 393224 | tf_op jit(solution)/shard_map/ppermute | solution.py:402
  18.0 14.5 %collective-permute-start.3 = (bf16[16,8,512]{2,1,0:T(8,128)(2,1)S(1)}, bf16[16,8,512]{2,1,0:T(8,128)(2,1)S(1)}, u32[]{:S(2)}, u32[]{:S(2)}) collective-permute-start(bf16[16,8,512]{2,1,0:T(8,128)(2,1)S(1)} %get-tuple-element.29), channel_id=1, source_target_pairs={{1,2},{2,1},{3,4},{4,3},{5,6},{6,5},{9,10},{10,9},{11,12},{12,11},... | collective-permute-start | bytes 393224 | tf_op jit(solution)/shard_map/ppermute | solution.py:402
  26.9 9.9 %copy-start.4 = (bf16[128,512]{1,0:T(8,128)(2,1)S(1)}, bf16[128,512]{1,0:T(8,128)(2,1)}, u32[]{:S(2)}) copy-start(bf16[128,512]{1,0:T(8,128)(2,1)} %w_map.3) | copy-start | bytes 393220
  26.9 8.3 %collective-permute-start = (bf16[16,8,128]{2,1,0:T(8,128)(2,1)S(1)}, bf16[16,8,128]{2,1,0:T(8,128)(2,1)S(1)}, u32[]{:S(2)}, u32[]{:S(2)}) collective-permute-start(bf16[16,8,128]{2,1,0:T(8,128)(2,1)S(1)} %get-tuple-element.26), channel_id=1, source_target_pairs={{1,2},{2,1},{3,4},{4,3},{5,6},{6,5},{9,10},{10,9},{11,12},{12,11},... | collective-permute-start | bytes 98312 | tf_op jit(solution)/shard_map/ppermute | solution.py:402
  31.3 5.5 %collective-permute-start.1 = (bf16[16,8,128]{2,1,0:T(8,128)(2,1)S(1)}, bf16[16,8,128]{2,1,0:T(8,128)(2,1)S(1)}, u32[]{:S(2)}, u32[]{:S(2)}) collective-permute-start(bf16[16,8,128]{2,1,0:T(8,128)(2,1)S(1)} %get-tuple-element.27), channel_id=1, source_target_pairs={{0,1},{1,0},{2,3},{3,2},{4,5},{5,4},{6,7},{7,6},{8,9},{9,8},{10,11... | collective-permute-start | bytes 98312 | tf_op jit(solution)/shard_map/ppermute | solution.py:402
  32.5 5.5 %copy-start.1 = (bf16[2,512,1536]{2,1,0:T(8,128)(2,1)S(1)}, bf16[2,512,1536]{2,1,0:T(8,128)(2,1)}, u32[]{:S(2)}) copy-start(bf16[2,512,1536]{2,1,0:T(8,128)(2,1)} %w_qkv.3) | copy-start | bytes 9437188
  32.5 5.5 %copy-start.2 = (bf16[2,512,512]{2,1,0:T(8,128)(2,1)S(1)}, bf16[2,512,512]{2,1,0:T(8,128)(2,1)}, u32[]{:S(2)}) copy-start(bf16[2,512,512]{2,1,0:T(8,128)(2,1)} %w_out.3) | copy-start | bytes 3145732
  32.5 5.5 %copy-start.6 = (f32[2,512]{1,0:T(2,128)S(1)}, f32[2,512]{1,0:T(2,128)}, u32[]{:S(2)}) copy-start(f32[2,512]{1,0:T(2,128)} %gains.3) | copy-start | bytes 12292
  32.5 5.5 %copy-start.9 = (bf16[1024,128]{1,0:T(8,128)(2,1)S(1)}, bf16[1024,128]{1,0:T(8,128)(2,1)}, u32[]{:S(2)}) copy-start(bf16[1024,128]{1,0:T(8,128)(2,1)} %constant.12.clone.k_aug) | copy-start | bytes 786436
  32.5 5.5 %copy-start.10 = (bf16[576,128]{1,0:T(8,128)(2,1)S(1)}, bf16[576,128]{1,0:T(8,128)(2,1)}, u32[]{:S(2)}) copy-start(bf16[576,128]{1,0:T(8,128)(2,1)} %constant.11.clone.q_aug) | copy-start | bytes 442372
  32.5 5.5 %copy-start.12 = (bf16[256,256]{1,0:T(8,128)(2,1)S(1)}, bf16[256,256]{1,0:T(8,128)(2,1)}, u32[]{:S(2)}) copy-start(bf16[256,256]{1,0:T(8,128)(2,1)} %constant.10.clone.block_ones) | copy-start | bytes 393220
  32.7 10.2 %collective-permute-start.6 = (bf16[8,32,512]{2,1,0:T(8,128)(2,1)S(1)}, bf16[8,32,512]{2,1,0:T(8,128)(2,1)S(1)}, u32[]{:S(2)}, u32[]{:S(2)}) collective-permute-start(bf16[8,32,512]{2,1,0:T(8,128)(2,1)S(1)} %get-tuple-element.34), channel_id=1, source_target_pairs={{0,120},{8,16},{16,8},{24,32},{32,24},{40,48},{48,40},{56,64},{64,... | collective-permute-start | bytes 786440 | tf_op jit(solution)/shard_map/ppermute | solution.py:402
  32.8 10.1 %collective-permute-start.7 = (bf16[8,32,512]{2,1,0:T(8,128)(2,1)S(1)}, bf16[8,32,512]{2,1,0:T(8,128)(2,1)S(1)}, u32[]{:S(2)}, u32[]{:S(2)}) collective-permute-start(bf16[8,32,512]{2,1,0:T(8,128)(2,1)S(1)} %get-tuple-element.35), channel_id=1, source_target_pairs={{0,8},{8,0},{16,24},{24,16},{32,40},{40,32},{48,56},{56,48},{64,72... | collective-permute-start | bytes 786440 | tf_op jit(solution)/shard_map/ppermute | solution.py:402
  37.1 5.9 %collective-permute-start.4 = (bf16[8,32,128]{2,1,0:T(8,128)(2,1)S(1)}, bf16[8,32,128]{2,1,0:T(8,128)(2,1)S(1)}, u32[]{:S(2)}, u32[]{:S(2)}) collective-permute-start(bf16[8,32,128]{2,1,0:T(8,128)(2,1)S(1)} %get-tuple-element.32), channel_id=1, source_target_pairs={{0,120},{8,16},{16,8},{24,32},{32,24},{40,48},{48,40},{56,64},{64,... | collective-permute-start | bytes 196616 | tf_op jit(solution)/shard_map/ppermute | solution.py:402
  37.1 5.8 %collective-permute-start.5 = (bf16[8,32,128]{2,1,0:T(8,128)(2,1)S(1)}, bf16[8,32,128]{2,1,0:T(8,128)(2,1)S(1)}, u32[]{:S(2)}, u32[]{:S(2)}) collective-permute-start(bf16[8,32,128]{2,1,0:T(8,128)(2,1)S(1)} %get-tuple-element.33), channel_id=1, source_target_pairs={{0,8},{8,0},{16,24},{24,16},{32,40},{40,32},{48,56},{56,48},{64,72... | collective-permute-start | bytes 196616 | tf_op jit(solution)/shard_map/ppermute | solution.py:402
  38.0 4.9 %copy-start.7 = (f32[512]{0:T(512)S(1)}, f32[512]{0:T(512)}, u32[]{:S(2)}) copy-start(f32[512]{0:T(512)} %param.28) | copy-start | bytes 6148
  38.0 4.9 %copy-start.11 = (bf16[576,128]{1,0:T(8,128)(2,1)S(1)}, bf16[576,128]{1,0:T(8,128)(2,1)}, u32[]{:S(2)}) copy-start(bf16[576,128]{1,0:T(8,128)(2,1)} %constant.14.clone.k_aug_1) | copy-start | bytes 442372
  38.0 4.9 %copy-start.13 = (bf16[256,128]{1,0:T(8,128)(2,1)S(1)}, bf16[256,128]{1,0:T(8,128)(2,1)}, u32[]{:S(2)}) copy-start(bf16[256,128]{1,0:T(8,128)(2,1)} %constant.13.clone.q_aug_1) | copy-start | bytes 196612

commit v6 on v5

--- a/solution.py
+++ b/solution.py
@@ -91,9 +91,10 @@
         yield from task
 
 
-def pack_kernel(rows, cells, tally, packed, block, cells_here, tally_here, sems, out_sems):
+def pack_kernel(rows, cells, tally, packed, token, block, cells_here, tally_here, sems, out_sems):
     ids_load = pltpu.make_async_copy(cells, cells_here, sems.at[8])
     tally_load = pltpu.make_async_copy(tally, tally_here, sems.at[9])
+    token_store = pltpu.make_async_copy(cells_here.at[0:8], token, sems.at[10])
     ids_load.start()
     tally_load.start()
     loads = [
@@ -111,6 +112,7 @@
     order = jnp.where(order, 1.0, 0.0).astype(jnp.bfloat16)
     ids_load.wait()
     tally_load.wait()
+    token_store.start()
     here = lax.broadcasted_iota(jnp.int32, (16, 128), 1) // 8 == lax.broadcasted_iota(jnp.int32, (16, 128), 0)
     spread = jnp.where(here, tally_here[...].astype(jnp.float32), 0.0).astype(jnp.bfloat16)
     live = slot[:16].astype(jnp.float32) < dot(spread, pick)
@@ -127,27 +129,28 @@
     stores[1].start()
     for store in stores:
         store.wait()
+    token_store.wait()
 
 
 def pack(rows, cells, tally):
     return call(
         pack_kernel,
         "pack",
-        [(128, 2, 1152)],
+        [(128, 2, 1152), jax.ShapeDtypeStruct((8, 128), jnp.int32)],
         [HBM] * 3,
-        [HBM],
+        [HBM] * 2,
         [
             pltpu.VMEM((128, 2, 1152), jnp.bfloat16),
             pltpu.VMEM((16, 128), jnp.int32),
             pltpu.VMEM((1, 128), jnp.int32),
-            pltpu.SemaphoreType.DMA((10,)),
+            pltpu.SemaphoreType.DMA((11,)),
             pltpu.SemaphoreType.DMA((2,)),
         ],
         mib=60,
-    )(rows, cells, tally)[0]
-
-
-def stage_kernel(packed, pitch_at, sharp, lookup, hidden, pitch, scale, send_a, send_b):
+    )(rows, cells, tally)
+
+
+def stage_kernel(token, pitch_at, sharp, lookup, hidden, pitch, scale, send_a, send_b):
     rows = lax.broadcasted_iota(jnp.int32, (64, 1), 0)
     pitch[...] = jnp.sum(
         jnp.where(rows == pitch_at[0], lookup[...].astype(jnp.float32), 0.0), axis=0, keepdims=True
@@ -173,15 +176,16 @@
 
 
 def cell_sum_kernel(block, feat, send_a, send_b):
-    cell = lax.broadcasted_iota(jnp.int32, (256, 128), 0).astype(jnp.float32)
+    cell = lax.broadcasted_iota(jnp.int32, (256, 128), 0).astype(jnp.float32).astype(jnp.bfloat16)
+    one, none = jnp.ones((256, 128), jnp.bfloat16), jnp.zeros((256, 128), jnp.bfloat16)
     total = jnp.zeros((256, 128), jnp.float32)
     ids = jnp.sum(block[:, :, 1024:1152].astype(jnp.float32).reshape(16, 8, 2, 128), axis=1)
     for step in range(4):
         picks = []
         rows = []
         for part in range(4 * step, 4 * step + 4):
-            wide = jnp.broadcast_to(ids[part, 0:1], (256, 128))
-            picks.append(jnp.where(wide == cell, 1.0, 0.0).astype(jnp.bfloat16))
+            wide = jnp.broadcast_to(ids[part, 0:1], (256, 128)).astype(jnp.bfloat16)
+            picks.append(jnp.where(wide == cell, one, none))
             rows += [block[8 * part : 8 * part + 8, :, 128 * k : 128 * k + 128].reshape(16, 128) for k in range(8)]
         total = total + dot(jnp.concatenate(picks, axis=1), jnp.concatenate(rows, axis=0))
     total = rounded(total).reshape(16, 16, 128)
@@ -416,7 +420,7 @@
     final_mapping_matrix,
     terminal_rescale_factor,
 ):
-    packed = pack(
+    packed, token = pack(
         mesh_portion_descriptors.reshape(128, 8, 2, 128), mesh_entry_site.reshape(16, 128), mesh_portion_tally
     )
     arrived = lax.all_to_all(packed, ("az", "rad"), split_axis=0, concat_axis=0, tiled=True)
@@ -424,7 +428,7 @@
     hidden = hidden_site_vector[0]
     block_ones = jnp.asarray(np.kron(np.eye(4), np.ones((64, 64))), jnp.bfloat16)
     pitch, scale, to_a, to_b = stage(
-        packed, incline_grid_position, sharpness_scale, incline_vector_lookup, hidden
+        token, incline_grid_position, sharpness_scale, incline_vector_lookup, hidden
     )
     hid_a, hid_b = swap(to_a, "rad", 0), swap(to_b, "rad", 1)
 

time: 49.9 us -> 50 us (level)
  no operation moved by 1% of the time
where the time goes in v6:
time: 50 us; the launch traced here: 49.7 us
  starting transfers between devices  24 us (48%)
  Pallas kernels  13.7 us (27%)
  waiting for transfers between devices  10.3 us (21%)
  between operations  0.9 us (2%)
  local copies, waits for them, and re-layouts  0.76 us (2%)
    ppermute x8, starting transfers between devices, swap(): return lax.ppermute(x, axis, [(i, j) for i, j in pairs if 0 <= j < count])  13.5 us
    all_to_all x1, starting transfers between devices, per_device(): lax.all_to_all(packed, ('az', 'rad'), split_axis=0, concat_axis=0, tiled=...  10.5 us
    pallas_call x1, Pallas kernels, outer(): call(outer_kernel, 'outer', [(16, 16, WIDTH)], [VMEM] * 24, scratch=[pltp...  6.69 us
    all_to_all x1, waiting for transfers between devices, per_device(): lax.all_to_all(packed, ('az', 'rad'), split_axis=0, concat_axis=0, tiled=...  5.7 us
    ppermute x8, waiting for transfers between devices, swap(): return lax.ppermute(x, axis, [(i, j) for i, j in pairs if 0 <= j < count])  4.63 us
    pallas_call x1, Pallas kernels, inner(): call(inner_kernel, 'inner', outs, [VMEM] * 8, scratch=scratch, mib=14)  3.24 us
    pallas_call x1, Pallas kernels, pack(): call(pack_kernel, 'pack', [(128, 2, 1152), jax.ShapeDtypeStruct((8, 128),...  2.08 us
  transfers between devices with their start and end apart: 9, of which 4 were waited for; matrix products, arithmetic and copies ran while one was open for 0% of the time, Pallas kernels for 10%

profile of v6, /device:TPU:8, one launch (start us, length us, event | category | flops | bytes accessed | tf_op | source)
XLA Modules:
  0.0 49.7 jit_solution(3591541954360969873)
XLA Ops:
  0.0 2.1 %pack.1 = (bf16[128,2,1152]{2,1,0:T(2,128)(2,1)}, s32[8,128]{1,0:T(8,128)}) custom-call(bf16[128,8,2,128]{3,2,1,0:T(2,128)(2,1)} %bitcast.8, s32[16,128]{1,0:T(8,128)} %bitcast.9, s32[1,128]{1,0:T(1,128)} %tally.1), custom_call_target="tpu_custom_call" | custom-call | flops 1500000000 | bytes 4500000 | tf_op jit(solution)/shard_map/pack/pallas_call | solution.py:136
  2.1 10.5 %all-to-all-start = ((bf16[128,2,1152]{2,1,0:T(2,128)(2,1)}), bf16[128,2,1152]{2,1,0:T(2,128)(2,1)S(1)}, u32[]{:S(2)}, u32[]{:S(2)}) async-start(bf16[128,2,1152]{2,1,0:T(2,128)(2,1)} %get-tuple-element.27), calls=%async_computation | async-start | bytes 1179648 | tf_op jit(solution)/shard_map/all_to_all | solution.py:426
  13.2 0.7 %copy-done.13 = s32[8,128]{1,0:T(8,128)S(1)} copy-done((s32[8,128]{1,0:T(8,128)S(1)}, s32[8,128]{1,0:T(8,128)}, u32[]{:S(2)}) %copy-start.13) | copy-done | bytes 4120
  13.9 0.6 %stage.1 = (f32[1,512]{1,0:T(1,128)S(1)}, f32[2,512]{1,0:T(2,128)S(1)}, bf16[16,8,512]{2,1,0:T(8,128)(2,1)S(1)}, bf16[16,8,512]{2,1,0:T(8,128)(2,1)S(1)}) custom-call(s32[8,128]{1,0:T(8,128)S(1)} %copy-done.13, s32[1]{0:T(128)S(6)} %copy.18.pitch_at, f32[2,8]{1,0:T(2,128)S(1)} %copy-done.7, bf16[64,512]{1,0:T(8,128)(2,1)S(1)} %copy-done.4, ...), custom_call_target="tpu_custom_call" | custom-call | flops 1000000000 | bytes 3000000 | tf_op jit(solution)/shard_map/stage/pallas_call | solution.py:175
  14.6 3.0 %collective-permute-start.2 = (bf16[16,8,512]{2,1,0:T(8,128)(2,1)S(1)}, bf16[16,8,512]{2,1,0:T(8,128)(2,1)S(1)}, u32[]{:S(2)}, u32[]{:S(2)}) collective-permute-start(bf16[16,8,512]{2,1,0:T(8,128)(2,1)S(1)} %get-tuple-element.32), channel_id=1, source_target_pairs={{0,1},{1,0},{2,3},{3,2},{4,5},{5,4},{6,7},{7,6},{8,9},{9,8},{10,11... | collective-permute-start | bytes 393224 | tf_op jit(solution)/shard_map/ppermute | solution.py:406
  17.6 3.0 %collective-permute-start.3 = (bf16[16,8,512]{2,1,0:T(8,128)(2,1)S(1)}, bf16[16,8,512]{2,1,0:T(8,128)(2,1)S(1)}, u32[]{:S(2)}, u32[]{:S(2)}) collective-permute-start(bf16[16,8,512]{2,1,0:T(8,128)(2,1)S(1)} %get-tuple-element.33), channel_id=1, source_target_pairs={{1,2},{2,1},{3,4},{4,3},{5,6},{6,5},{9,10},{10,9},{11,12},{12,11},... | collective-permute-start | bytes 393224 | tf_op jit(solution)/shard_map/ppermute | solution.py:406
  20.6 5.7 %all-to-all-done.block = bf16[128,2,1152]{2,1,0:T(2,128)(2,1)S(1)} async-done(((bf16[128,2,1152]{2,1,0:T(2,128)(2,1)}), bf16[128,2,1152]{2,1,0:T(2,128)(2,1)S(1)}, u32[]{:S(2)}, u32[]{:S(2)}) %all-to-all-start) | async-done | bytes 589856 | tf_op jit(solution)/shard_map/all_to_all | solution.py:426
  26.3 0.6 %cell_sums.1 = (bf16[16,16,128]{2,1,0:T(8,128)(2,1)S(1)}, bf16[16,8,128]{2,1,0:T(8,128)(2,1)S(1)}, bf16[16,8,128]{2,1,0:T(8,128)(2,1)S(1)}) custom-call(bf16[128,2,1152]{2,1,0:T(2,128)(2,1)S(1)} %all-to-all-done.block), custom_call_target="tpu_custom_call" | custom-call | flops 2000000000 | bytes 6000000 | tf_op jit(solution)/shard_map/cell_sums/pallas_call | solution.py:201
  26.9 4.3 %collective-permute-start = (bf16[16,8,128]{2,1,0:T(8,128)(2,1)S(1)}, bf16[16,8,128]{2,1,0:T(8,128)(2,1)S(1)}, u32[]{:S(2)}, u32[]{:S(2)}) collective-permute-start(bf16[16,8,128]{2,1,0:T(8,128)(2,1)S(1)} %get-tuple-element.29), channel_id=1, source_target_pairs={{1,2},{2,1},{3,4},{4,3},{5,6},{6,5},{9,10},{10,9},{11,12},{12,11},... | collective-permute-start | bytes 98312 | tf_op jit(solution)/shard_map/ppermute | solution.py:406
  31.3 1.2 %collective-permute-start.1 = (bf16[16,8,128]{2,1,0:T(8,128)(2,1)S(1)}, bf16[16,8,128]{2,1,0:T(8,128)(2,1)S(1)}, u32[]{:S(2)}, u32[]{:S(2)}) collective-permute-start(bf16[16,8,128]{2,1,0:T(8,128)(2,1)S(1)} %get-tuple-element.30), channel_id=1, source_target_pairs={{0,1},{1,0},{2,3},{3,2},{4,5},{5,4},{6,7},{7,6},{8,9},{9,8},{10,11... | collective-permute-start | bytes 98312 | tf_op jit(solution)/shard_map/ppermute | solution.py:406
  32.5 0.0 copy-start.8
  32.5 0.0 copy-start.9
  32.5 0.0 copy-start.11
  32.5 0.2 widen.1
  32.7 0.1 collective-permute-start.6
  32.8 0.9 %collective-permute-start.7 = (bf16[8,32,512]{2,1,0:T(8,128)(2,1)S(1)}, bf16[8,32,512]{2,1,0:T(8,128)(2,1)S(1)}, u32[]{:S(2)}, u32[]{:S(2)}) collective-permute-start(bf16[8,32,512]{2,1,0:T(8,128)(2,1)S(1)} %get-tuple-element.39), channel_id=1, source_target_pairs={{0,8},{8,0},{16,24},{24,16},{32,40},{40,32},{48,56},{56,48},{64,72... | collective-permute-start | bytes 786440 | tf_op jit(solution)/shard_map/ppermute | solution.py:406
  33.7 1.5 %collective-permute-done.feat_b = bf16[16,8,128]{2,1,0:T(8,128)(2,1)S(1)} collective-permute-done((bf16[16,8,128]{2,1,0:T(8,128)(2,1)S(1)}, bf16[16,8,128]{2,1,0:T(8,128)(2,1)S(1)}, u32[]{:S(2)}, u32[]{:S(2)}) %collective-permute-start) | collective-permute-done | bytes 32800 | tf_op jit(solution)/shard_map/ppermute | solution.py:406
  35.2 1.5 %collective-permute-done.1.feat_a = bf16[16,8,128]{2,1,0:T(8,128)(2,1)S(1)} collective-permute-done((bf16[16,8,128]{2,1,0:T(8,128)(2,1)S(1)}, bf16[16,8,128]{2,1,0:T(8,128)(2,1)S(1)}, u32[]{:S(2)}, u32[]{:S(2)}) %collective-permute-start.1) | collective-permute-done | bytes 32800 | tf_op jit(solution)/shard_map/ppermute | solution.py:406
  36.8 0.3 band.1
  37.0 0.1 collective-permute-start.4
  37.1 0.9 %collective-permute-start.5 = (bf16[8,32,128]{2,1,0:T(8,128)(2,1)S(1)}, bf16[8,32,128]{2,1,0:T(8,128)(2,1)S(1)}, u32[]{:S(2)}, u32[]{:S(2)}) collective-permute-start(bf16[8,32,128]{2,1,0:T(8,128)(2,1)S(1)} %get-tuple-element.37), channel_id=1, source_target_pairs={{0,8},{8,0},{16,24},{24,16},{32,40},{40,32},{48,56},{56,48},{64,72... | collective-permute-start | bytes 196616 | tf_op jit(solution)/shard_map/ppermute | solution.py:406
  38.1 3.2 %inner.1 = (bf16[384,512]{1,0:T(8,128)(2,1)S(1)}, bf16[512,512]{1,0:T(8,128)(2,1)S(1)}, bf16[512,512]{1,0:T(8,128)(2,1)S(1)}, bf16[192,512]{1,0:T(8,128)(2,1)S(1...) custom-call(bf16[16,32,512]{2,1,0:T(8,128)(2,1)S(1)} %get-tuple-element.40.band_stream, ...), custom_call_target="tpu_custom_call" | custom-call | flops 4000000000 | bytes 12000000 | tf_op jit(solution)/shard_map/inner/pallas_call | solution.py:334
  41.3 1.6 %collective-permute-done.4.feat_b = bf16[8,32,128]{2,1,0:T(8,128)(2,1)S(1)} collective-permute-done((bf16[8,32,128]{2,1,0:T(8,128)(2,1)S(1)}, bf16[8,32,128]{2,1,0:T(8,128)(2,1)S(1)}, u32[]{:S(2)}, u32[]{:S(2)}) %collective-permute-start.4) | collective-permute-done | bytes 65568 | tf_op jit(solution)/shard_map/ppermute | solution.py:406
  43.0 6.7 %outer.1 = bf16[16,16,512]{2,1,0:T(8,128)(2,1)} custom-call(bf16[8,32,128]{2,1,0:T(8,128)(2,1)S(1)} %collective-permute-done.4.feat_b, bf16[8,32,128]{2,1,0:T(8,128)(2,1)S(1)} %collective-permute-done.5.feat_a, bf16[8,32,512]{2,1,0:T(8,128)(2,1)S(1)} %collective-permute-done.6.hid_b, bf16[8,32,512]{2,1,0:T(8,128)(2,1)S(1)} %collective-permute-done.7.hid_a, ...), custom_call_target="tpu_custom_call" | custom-call | flops 8000000000 | bytes 24000000 | tf_op jit(solution)/shard_map/outer/pallas_call | solution.py:391
  (29 shorter events, 0.1 us)
Async XLA Ops:
  0.0 13.2 %copy-start.2 = (bf16[1,16,16,512]{3,2,1,0:T(8,128)(2,1)S(1)}, bf16[1,16,16,512]{3,2,1,0:T(8,128)(2,1)}, u32[]{:S(2)}) copy-start(bf16[1,16,16,512]{3,2,1,0:T(8,128)(2,1)} %param.17) | copy-start | bytes 786436
  0.0 13.2 %copy-start.4 = (bf16[64,512]{1,0:T(8,128)(2,1)S(1)}, bf16[64,512]{1,0:T(8,128)(2,1)}, u32[]{:S(2)}) copy-start(bf16[64,512]{1,0:T(8,128)(2,1)} %lookup.1) | copy-start | bytes 196612
  0.0 13.2 %copy-start.7 = (f32[2,8]{1,0:T(2,128)S(1)}, f32[2,8]{1,0:T(2,128)}, u32[]{:S(2)}) copy-start(f32[2,8]{1,0:T(2,128)} %sharp.1) | copy-start | bytes 196
  2.1 24.2 %all-to-all-start = ((bf16[128,2,1152]{2,1,0:T(2,128)(2,1)}), bf16[128,2,1152]{2,1,0:T(2,128)(2,1)S(1)}, u32[]{:S(2)}, u32[]{:S(2)}) async-start(bf16[128,2,1152]{2,1,0:T(2,128)(2,1)} %get-tuple-element.27), calls=%async_computation | async-start | bytes 1179648 | tf_op jit(solution)/shard_map/all_to_all | solution.py:426
  13.2 0.7 %copy-start.13 = (s32[8,128]{1,0:T(8,128)S(1)}, s32[8,128]{1,0:T(8,128)}, u32[]{:S(2)}) copy-start(s32[8,128]{1,0:T(8,128)} %get-tuple-element.31.token) | copy-start | bytes 12292
  14.6 17.9 %collective-permute-start.2 = (bf16[16,8,512]{2,1,0:T(8,128)(2,1)S(1)}, bf16[16,8,512]{2,1,0:T(8,128)(2,1)S(1)}, u32[]{:S(2)}, u32[]{:S(2)}) collective-permute-start(bf16[16,8,512]{2,1,0:T(8,128)(2,1)S(1)} %get-tuple-element.32), channel_id=1, source_target_pairs={{0,1},{1,0},{2,3},{3,2},{4,5},{5,4},{6,7},{7,6},{8,9},{9,8},{10,11... | collective-permute-start | bytes 393224 | tf_op jit(solution)/shard_map/ppermute | solution.py:406
  17.6 14.9 %collective-permute-start.3 = (bf16[16,8,512]{2,1,0:T(8,128)(2,1)S(1)}, bf16[16,8,512]{2,1,0:T(8,128)(2,1)S(1)}, u32[]{:S(2)}, u32[]{:S(2)}) collective-permute-start(bf16[16,8,512]{2,1,0:T(8,128)(2,1)S(1)} %get-tuple-element.33), channel_id=1, source_target_pairs={{1,2},{2,1},{3,4},{4,3},{5,6},{6,5},{9,10},{10,9},{11,12},{12,11},... | collective-permute-start | bytes 393224 | tf_op jit(solution)/shard_map/ppermute | solution.py:406
  26.9 9.9 %copy-start.3 = (bf16[128,512]{1,0:T(8,128)(2,1)S(1)}, bf16[128,512]{1,0:T(8,128)(2,1)}, u32[]{:S(2)}) copy-start(bf16[128,512]{1,0:T(8,128)(2,1)} %w_map.3) | copy-start | bytes 393220
  26.9 8.3 %collective-permute-start = (bf16[16,8,128]{2,1,0:T(8,128)(2,1)S(1)}, bf16[16,8,128]{2,1,0:T(8,128)(2,1)S(1)}, u32[]{:S(2)}, u32[]{:S(2)}) collective-permute-start(bf16[16,8,128]{2,1,0:T(8,128)(2,1)S(1)} %get-tuple-element.29), channel_id=1, source_target_pairs={{1,2},{2,1},{3,4},{4,3},{5,6},{6,5},{9,10},{10,9},{11,12},{12,11},... | collective-permute-start | bytes 98312 | tf_op jit(solution)/shard_map/ppermute | solution.py:406
  31.3 5.5 %collective-permute-start.1 = (bf16[16,8,128]{2,1,0:T(8,128)(2,1)S(1)}, bf16[16,8,128]{2,1,0:T(8,128)(2,1)S(1)}, u32[]{:S(2)}, u32[]{:S(2)}) collective-permute-start(bf16[16,8,128]{2,1,0:T(8,128)(2,1)S(1)} %get-tuple-element.30), channel_id=1, source_target_pairs={{0,1},{1,0},{2,3},{3,2},{4,5},{5,4},{6,7},{7,6},{8,9},{9,8},{10,11... | collective-permute-start | bytes 98312 | tf_op jit(solution)/shard_map/ppermute | solution.py:406
  32.5 5.5 %copy-start = (bf16[2,512,1536]{2,1,0:T(8,128)(2,1)S(1)}, bf16[2,512,1536]{2,1,0:T(8,128)(2,1)}, u32[]{:S(2)}) copy-start(bf16[2,512,1536]{2,1,0:T(8,128)(2,1)} %w_qkv.3) | copy-start | bytes 9437188
  32.5 5.5 %copy-start.1 = (bf16[2,512,512]{2,1,0:T(8,128)(2,1)S(1)}, bf16[2,512,512]{2,1,0:T(8,128)(2,1)}, u32[]{:S(2)}) copy-start(bf16[2,512,512]{2,1,0:T(8,128)(2,1)} %w_out.3) | copy-start | bytes 3145732
  32.5 5.5 %copy-start.5 = (f32[2,512]{1,0:T(2,128)S(1)}, f32[2,512]{1,0:T(2,128)}, u32[]{:S(2)}) copy-start(f32[2,512]{1,0:T(2,128)} %gains.3) | copy-start | bytes 12292
  32.5 5.5 %copy-start.8 = (bf16[1024,128]{1,0:T(8,128)(2,1)S(1)}, bf16[1024,128]{1,0:T(8,128)(2,1)}, u32[]{:S(2)}) copy-start(bf16[1024,128]{1,0:T(8,128)(2,1)} %constant.12.clone.k_aug) | copy-start | bytes 786436
  32.5 5.5 %copy-start.9 = (bf16[576,128]{1,0:T(8,128)(2,1)S(1)}, bf16[576,128]{1,0:T(8,128)(2,1)}, u32[]{:S(2)}) copy-start(bf16[576,128]{1,0:T(8,128)(2,1)} %constant.11.clone.q_aug) | copy-start | bytes 442372
  32.5 5.5 %copy-start.11 = (bf16[256,256]{1,0:T(8,128)(2,1)S(1)}, bf16[256,256]{1,0:T(8,128)(2,1)}, u32[]{:S(2)}) copy-start(bf16[256,256]{1,0:T(8,128)(2,1)} %constant.10.clone.block_ones) | copy-start | bytes 393220
  32.7 10.2 %collective-permute-start.6 = (bf16[8,32,512]{2,1,0:T(8,128)(2,1)S(1)}, bf16[8,32,512]{2,1,0:T(8,128)(2,1)S(1)}, u32[]{:S(2)}, u32[]{:S(2)}) collective-permute-start(bf16[8,32,512]{2,1,0:T(8,128)(2,1)S(1)} %get-tuple-element.38), channel_id=1, source_target_pairs={{0,120},{8,16},{16,8},{24,32},{32,24},{40,48},{48,40},{56,64},{64,... | collective-permute-start | bytes 786440 | tf_op jit(solution)/shard_map/ppermute | solution.py:406
  32.8 10.1 %collective-permute-start.7 = (bf16[8,32,512]{2,1,0:T(8,128)(2,1)S(1)}, bf16[8,32,512]{2,1,0:T(8,128)(2,1)S(1)}, u32[]{:S(2)}, u32[]{:S(2)}) collective-permute-start(bf16[8,32,512]{2,1,0:T(8,128)(2,1)S(1)} %get-tuple-element.39), channel_id=1, source_target_pairs={{0,8},{8,0},{16,24},{24,16},{32,40},{40,32},{48,56},{56,48},{64,72... | collective-permute-start | bytes 786440 | tf_op jit(solution)/shard_map/ppermute | solution.py:406
  37.0 5.9 %collective-permute-start.4 = (bf16[8,32,128]{2,1,0:T(8,128)(2,1)S(1)}, bf16[8,32,128]{2,1,0:T(8,128)(2,1)S(1)}, u32[]{:S(2)}, u32[]{:S(2)}) collective-permute-start(bf16[8,32,128]{2,1,0:T(8,128)(2,1)S(1)} %get-tuple-element.36), channel_id=1, source_target_pairs={{0,120},{8,16},{16,8},{24,32},{32,24},{40,48},{48,40},{56,64},{64,... | collective-permute-start | bytes 196616 | tf_op jit(solution)/shard_map/ppermute | solution.py:406
  37.1 5.8 %collective-permute-start.5 = (bf16[8,32,128]{2,1,0:T(8,128)(2,1)S(1)}, bf16[8,32,128]{2,1,0:T(8,128)(2,1)S(1)}, u32[]{:S(2)}, u32[]{:S(2)}) collective-permute-start(bf16[8,32,128]{2,1,0:T(8,128)(2,1)S(1)} %get-tuple-element.37), channel_id=1, source_target_pairs={{0,8},{8,0},{16,24},{24,16},{32,40},{40,32},{48,56},{56,48},{64,72... | collective-permute-start | bytes 196616 | tf_op jit(solution)/shard_map/ppermute | solution.py:406
  38.1 4.9 %copy-start.6 = (f32[512]{0:T(512)S(1)}, f32[512]{0:T(512)}, u32[]{:S(2)}) copy-start(f32[512]{0:T(512)} %param.28) | copy-start | bytes 6148
  38.1 4.9 %copy-start.10 = (bf16[576,128]{1,0:T(8,128)(2,1)S(1)}, bf16[576,128]{1,0:T(8,128)(2,1)}, u32[]{:S(2)}) copy-start(bf16[576,128]{1,0:T(8,128)(2,1)} %constant.14.clone.k_aug_1) | copy-start | bytes 442372
  38.1 4.9 %copy-start.12 = (bf16[256,128]{1,0:T(8,128)(2,1)S(1)}, bf16[256,128]{1,0:T(8,128)(2,1)}, u32[]{:S(2)}) copy-start(bf16[256,128]{1,0:T(8,128)(2,1)} %constant.13.clone.q_aug_1) | copy-start | bytes 196612
